TPU v7x, 32 devices: a whole 2x2x4 slice. The times are simulated.
32 devices in a mesh: section: 2 (over core), seq: 4 (over y, x), fsdp: 4 (over z).
Axes of the slice: x: 2, y: 2, z: 4, core: 2. Of those that a mesh axis runs over, the one named last changes fastest.
Arguments:
- tokens: bfloat16 [2, 4, 256, 1536], P(None, 'fsdp', 'seq'), may hold values from -6 to 6
- cotangent: bfloat16 [2, 4, 256, 1536], P(None, 'fsdp', 'seq'), may hold values from -6 to 6
- norm_gain: float32 [2, 1536], P('section'), may hold values from 0.25 to 1.75
- w_in: bfloat16 [2, 1536, 6448], P('section', 'fsdp'), may hold values from -0.15625 to 0.15625
- conv_weight: float32 [2, 4, 3328], P('section'), may hold values from -3 to 3
- conv_bias: float32 [2, 3328], P('section'), may hold values from -3 to 3
- dt_bias: float32 [2, 48], P('section'), may hold values from -4 to -2
- a_log: float32 [2, 48], P('section'), as said below
- skip_gain: float32 [2, 48], P('section'), may hold values from 0.5 to 1.5
- gate_gain: float32 [2, 3072], P('section'), may hold values from 0.25 to 1.75
- w_out: bfloat16 [2, 3072, 1536], P('section', 'fsdp'), may hold values from -0.109375 to 0.109375
Outputs:
- layer_out: bfloat16 [2, 2, 4, 256, 1536], P('section', None, 'fsdp', 'seq')
- input_grad: bfloat16 [2, 2, 4, 256, 1536], P('section', None, 'fsdp', 'seq')
- grad_norm_gain: float32 [2, 1536], P('section')
- grad_w_in: float32 [2, 1536, 6448], P('section', 'fsdp')
- grad_conv_weight: float32 [2, 4, 3328], P('section')
- grad_conv_bias: float32 [2, 3328], P('section')
- grad_dt_bias: float32 [2, 48], P('section')
- grad_a_log: float32 [2, 48], P('section')
- grad_skip_gain: float32 [2, 48], P('section')
- grad_gate_gain: float32 [2, 3072], P('section')
- grad_w_out: float32 [2, 3072, 1536], P('section', 'fsdp')
Inputs may be any that keep to these rules, and one draw needn't show every extreme that they name: exp(a_log) is the decay coefficient of each head.
All inputs are finite; a program needn't handle non-finite values.
Results may differ from a plain program's by a relative error of at most 0.025.
The roundings to bfloat16 on the way count: a program that leaves them out, or rounds other values in their place, can miss the bound.
Values may be sent and summed in bfloat16 or wider, within the bound.
A program may use at most 256 MiB of HBM per device.

v0:
```python
from functools import partial

import jax
import jax.numpy as jnp
from jax import lax
from jax.sharding import PartitionSpec as P

HEADS = 48
HEADDIM = 64
STATE = 128
CONV = 4
SPAN = 256
INNER = 3072
XBC = 3328


HIGHEST_PRECISION = lax.Precision.HIGHEST
NORM_EPS = 1e-05


def passed_along(block, axis, distance):
    devices = range(lax.axis_size(axis))
    route = [(i - distance, i) for i in devices if i - distance in devices]
    return lax.ppermute(block, axis, route)


def round_value(value):
    return lax.optimization_barrier(value.astype(jnp.bfloat16)).astype(jnp.float32)


def rounded_keep(value):
    return (round_value(value), None)


def rounded_pass(kept, grad):
    return (grad,)


def rounded(value):
    wrapped = jax.custom_vjp(round_value)
    wrapped.defvjp(rounded_keep, rounded_pass)
    return wrapped(value)


def exact_product(form, left, right):
    return jnp.einsum(form, left, right, precision=HIGHEST_PRECISION)


def low_product(form, left, right):

    def plain_product(first, second):
        return jnp.einsum(
            form,
            first.astype(jnp.bfloat16),
            second.astype(jnp.bfloat16),
            preferred_element_type=jnp.float32,
        )

    def product_keep(first, second):
        return (plain_product(first, second), (first, second))

    def product_back(kept, grad):
        _, pull = jax.vjp(partial(exact_product, form), kept[0], kept[1])
        return pull(grad)

    wrapped = jax.custom_vjp(plain_product)
    wrapped.defvjp(product_keep, product_back)
    return wrapped(left, right)


def mix_heads(head_inputs, step_size, decay_rates, state_in, state_out, skip_terms):
    length, head_count, head_width = head_inputs.shape
    blocks = length // SPAN
    row_ids = lax.broadcasted_iota(jnp.int32, (SPAN, SPAN), 0)
    col_ids = lax.broadcasted_iota(jnp.int32, (SPAN, SPAN), 1)
    causal = (row_ids >= col_ids)[:, :, None]

    def advance(carry_state, pieces):
        block_x, block_dt, block_b, block_c = pieces
        log_decay = jnp.cumsum(-decay_rates[None, :] * block_dt, axis=0)
        log_gaps = jnp.where(causal, log_decay[:, None, :] - log_decay[None, :, :], 0.0)
        decay_mask = jnp.where(causal, jnp.exp(log_gaps), 0.0)
        scores = low_product("tn,sn->ts", block_c, block_b)
        weights = rounded(scores[:, :, None] * decay_mask * block_dt[None, :, :])
        within = low_product("tsh,shp->thp", weights, block_x)
        carried = low_product("tn,hnp->thp", block_c, rounded(carry_state))
        carried = carried * jnp.exp(log_decay)[:, :, None]
        tail_decay = jnp.exp(log_decay[-1][None, :] - log_decay) * block_dt
        shaped = rounded(block_b[:, None, :] * tail_decay[:, :, None])
        fresh_state = low_product("shn,shp->hnp", shaped, block_x)
        carry_state = jnp.exp(log_decay[-1])[:, None, None] * carry_state + fresh_state
        return (carry_state, within + carried + skip_terms[None, :, None] * block_x)

    pieces = (
        head_inputs.reshape(blocks, SPAN, head_count, head_width),
        step_size.reshape(blocks, SPAN, head_count),
        state_in.reshape(blocks, SPAN, state_in.shape[1]),
        state_out.reshape(blocks, SPAN, state_out.shape[1]),
    )
    initial = jnp.zeros((head_count, state_in.shape[1], head_width), jnp.float32)
    _, results = lax.scan(jax.checkpoint(advance), initial, pieces)
    return results.reshape(length, head_count, head_width)


def convolve(values, kernel, bias_row):
    length = values.shape[0]
    padded = jnp.pad(values, ((CONV - 1, 0), (0, 0)))
    conv_sum = bias_row[None, :] + kernel[0][None, :] * padded[0:length]
    for offset in range(1, CONV):
        conv_sum = conv_sum + kernel[offset][None, :] * padded[offset : offset + length]
    return rounded(jax.nn.silu(conv_sum))


def head_forward(
    x_raw,
    dt_raw,
    shared_raw,
    conv_x,
    bias_x,
    conv_shared,
    bias_shared,
    dt_shift,
    log_rate,
    skip_terms,
):
    length = x_raw.shape[0]
    act_x = convolve(x_raw, conv_x, bias_x)
    act_shared = convolve(shared_raw, conv_shared, bias_shared)
    head_count = dt_raw.shape[1]
    head_inputs = act_x.reshape(length, head_count, -1)
    step_size = jax.nn.softplus(dt_raw + dt_shift[None, :])
    mixed = mix_heads(
        head_inputs,
        step_size,
        jnp.exp(log_rate),
        act_shared[:, :STATE],
        act_shared[:, STATE:],
        skip_terms,
    )
    return mixed.reshape(length, -1)


def in_norm(rows_in, gain_row):
    row_scale = lax.rsqrt(jnp.mean(rows_in * rows_in, axis=-1, keepdims=True) + NORM_EPS)
    return rows_in * row_scale * gain_row


def out_norm(mixed, gate_part, gain_row):
    gated = mixed * jax.nn.silu(gate_part)
    gscale = lax.rsqrt(jnp.mean(gated * gated, axis=-1, keepdims=True) + NORM_EPS)
    return gated * gscale * gain_row


def store(buffers, fresh, position, usable):

    def place_one(buffer, newer):
        former = lax.dynamic_index_in_dim(buffer, position, 0, False)
        return lax.dynamic_update_index_in_dim(
            buffer, jnp.where(usable, newer, former), position, 0
        )

    return jax.tree.map(place_one, buffers, fresh)


def shards(
    tokens,
    cotangent,
    norm_gain,
    w_in,
    conv_weight,
    conv_bias,
    dt_bias,
    a_log,
    skip_gain,
    gate_gain,
    w_out,
):
    section_index = lax.axis_index("section")
    section_count = lax.axis_size("section")
    seq_index = lax.axis_index("seq")
    seq_count = lax.axis_size("seq")
    micro_count = tokens.shape[0]
    heads_local = HEADS // seq_count
    inner_local = heads_local * HEADDIM
    tick_count = micro_count + section_count - 1
    last_section = section_count - 1
    gain_in = norm_gain[0]
    gain_out = gate_gain[0]
    conv_all = conv_weight[0]
    bias_all = conv_bias[0]
    channel_start = seq_index * inner_local
    head_start = seq_index * heads_local
    head_params = (
        lax.dynamic_slice_in_dim(conv_all[:, :INNER], channel_start, inner_local, 1),
        lax.dynamic_slice_in_dim(bias_all[:INNER], channel_start, inner_local, 0),
        conv_all[:, INNER:],
        bias_all[INNER:],
        lax.dynamic_slice_in_dim(dt_bias[0], head_start, heads_local, 0),
        lax.dynamic_slice_in_dim(a_log[0], head_start, heads_local, 0),
        lax.dynamic_slice_in_dim(skip_gain[0], head_start, heads_local, 0),
    )
    w_in_full, w_out_full = (
        lax.all_gather(w_in[0], "fsdp", axis=0, tiled=True),
        lax.all_gather(w_out[0], "fsdp", axis=0, tiled=True),
    )
    saved_buffers = None
    out_buffer = None
    received = jnp.zeros(tokens.shape[2:], jnp.bfloat16)
    for step_now in range(tick_count):
        position = step_now - section_index
        usable = (position >= 0) & (position < micro_count)
        clamped = jnp.clip(position, 0, micro_count - 1)
        own_rows = tokens[min(step_now, micro_count - 1), 0]
        input_rows = jnp.where(section_index == 0, own_rows, received)
        rows_in = input_rows.astype(jnp.float32)
        forward_normed = in_norm(rows_in, gain_in).astype(jnp.bfloat16)
        projected = jnp.dot(forward_normed, w_in_full, preferred_element_type=jnp.float32)
        forward_gate_part = projected[:, :INNER]
        x_part = projected[:, INNER : 2 * INNER].astype(jnp.bfloat16)
        shared_part = projected[:, 2 * INNER : INNER + XBC].astype(jnp.bfloat16)
        dt_part = projected[:, INNER + XBC :].astype(jnp.bfloat16)
        forward_x_heads = lax.all_to_all(x_part, "seq", split_axis=1, concat_axis=0, tiled=True)
        forward_dt_heads = lax.all_to_all(dt_part, "seq", split_axis=1, concat_axis=0, tiled=True)
        forward_shared_all = lax.all_gather(shared_part, "seq", axis=0, tiled=True)
        mixed = head_forward(
            forward_x_heads.astype(jnp.float32),
            forward_dt_heads.astype(jnp.float32),
            forward_shared_all.astype(jnp.float32),
            *head_params
        )
        forward_mixed_rows = lax.all_to_all(
            mixed.astype(jnp.bfloat16), "seq", split_axis=0, concat_axis=1, tiled=True
        )
        forward_normed_out = out_norm(
            forward_mixed_rows.astype(jnp.float32), forward_gate_part, gain_out
        ).astype(jnp.bfloat16)
        output_rows = rows_in + jnp.dot(
            forward_normed_out, w_out_full, preferred_element_type=jnp.float32
        )
        output_rows, saved = (
            output_rows.astype(jnp.bfloat16),
            (
                input_rows,
                forward_normed,
                forward_gate_part,
                forward_x_heads,
                forward_dt_heads,
                forward_shared_all,
                forward_mixed_rows,
                forward_normed_out,
            ),
        )
        if saved_buffers is None:
            saved_buffers = jax.tree.map(
                lambda newer: jnp.zeros((micro_count,) + newer.shape, newer.dtype), saved
            )
            out_buffer = jnp.zeros((micro_count,) + output_rows.shape, jnp.bfloat16)
        saved_buffers = store(saved_buffers, saved, clamped, usable)
        out_buffer = store(out_buffer, output_rows, clamped, usable)
        if step_now + 1 < tick_count:
            received = passed_along(output_rows, "section", 1)
    totals = None
    grad_buffer = jnp.zeros_like(out_buffer)
    cot_buffer = jnp.zeros_like(out_buffer)
    proj_buffer = None
    received = jnp.zeros(tokens.shape[2:], jnp.bfloat16)
    for step_now in range(tick_count):
        position = micro_count - 1 - step_now + (last_section - section_index)
        usable = (position >= 0) & (position < micro_count)
        clamped = jnp.clip(position, 0, micro_count - 1)
        own_grad = cotangent[max(micro_count - 1 - step_now, 0), 0]
        grad_rows = jnp.where(section_index == last_section, own_grad, received)
        picked = jax.tree.map(
            lambda buffer: lax.dynamic_index_in_dim(buffer, clamped, 0, False), saved_buffers
        )
        (
            backward_input_rows,
            normed,
            gate_part,
            x_heads,
            dt_heads,
            shared_all,
            mixed_rows,
            normed_out,
        ) = picked
        grad_normed_out = lax.dot_general(
            grad_rows, w_out_full, (((1,), (1,)), ((), ())), preferred_element_type=jnp.float32
        )
        _, pull_out = jax.vjp(out_norm, mixed_rows.astype(jnp.float32), gate_part, gain_out)
        grad_mixed, grad_gate, grad_gain_out = pull_out(grad_normed_out)
        grad_heads = lax.all_to_all(
            grad_mixed.astype(jnp.bfloat16), "seq", split_axis=1, concat_axis=0, tiled=True
        )
        _, pull_head = jax.vjp(
            head_forward,
            x_heads.astype(jnp.float32),
            dt_heads.astype(jnp.float32),
            shared_all.astype(jnp.float32),
            *head_params
        )
        head_grads = pull_head(grad_heads.astype(jnp.float32))
        grad_x_rows = lax.all_to_all(
            head_grads[0].astype(jnp.bfloat16), "seq", split_axis=0, concat_axis=1, tiled=True
        )
        grad_dt_rows = lax.all_to_all(
            head_grads[1].astype(jnp.bfloat16), "seq", split_axis=0, concat_axis=1, tiled=True
        )
        grad_shared_rows = lax.psum_scatter(
            head_grads[2], "seq", scatter_dimension=0, tiled=True
        ).astype(jnp.bfloat16)
        proj_grad = jnp.concatenate(
            [grad_gate.astype(jnp.bfloat16), grad_x_rows, grad_shared_rows, grad_dt_rows], axis=1
        )
        grad_normed = lax.dot_general(
            proj_grad, w_in_full, (((1,), (1,)), ((), ())), preferred_element_type=jnp.float32
        )
        _, pull_in = jax.vjp(in_norm, backward_input_rows.astype(jnp.float32), gain_in)
        grad_input, grad_gain_in = pull_in(grad_normed)
        grad_input = grad_input + grad_rows.astype(jnp.float32)
        (
            conv_x_grad,
            bias_x_grad,
            conv_shared_grad,
            bias_shared_grad,
            backward_shift_grad,
            backward_rate_grad,
            backward_skip_grad,
        ) = head_grads[3:]
        backward_conv_grad = jnp.concatenate(
            [
                lax.dynamic_update_slice_in_dim(
                    jnp.zeros((CONV, INNER), jnp.float32), conv_x_grad, channel_start, 1
                ),
                conv_shared_grad,
            ],
            axis=1,
        )
        backward_bias_grad = jnp.concatenate(
            [
                lax.dynamic_update_slice_in_dim(
                    jnp.zeros((INNER,), jnp.float32), bias_x_grad, channel_start, 0
                ),
                bias_shared_grad,
            ],
            axis=0,
        )
        head_zeros = jnp.zeros((HEADS,), jnp.float32)
        shift_full = lax.dynamic_update_slice_in_dim(head_zeros, backward_shift_grad, head_start, 0)
        rate_full = lax.dynamic_update_slice_in_dim(head_zeros, backward_rate_grad, head_start, 0)
        skip_full = lax.dynamic_update_slice_in_dim(head_zeros, backward_skip_grad, head_start, 0)
        grads = (
            grad_gain_in,
            backward_conv_grad,
            backward_bias_grad,
            shift_full,
            rate_full,
            skip_full,
            grad_gain_out,
        )
        grad_input, proj_grad, grads = (grad_input.astype(jnp.bfloat16), proj_grad, grads)
        if totals is None:
            totals = jax.tree.map(jnp.zeros_like, grads)
            proj_buffer = jnp.zeros((micro_count,) + proj_grad.shape, jnp.bfloat16)
        totals = jax.tree.map(
            lambda summed, newer: jnp.where(usable, summed + newer, summed), totals, grads
        )
        grad_buffer = store(grad_buffer, grad_input, clamped, usable)
        cot_buffer = store(cot_buffer, grad_rows, clamped, usable)
        proj_buffer = store(proj_buffer, proj_grad, clamped, usable)
        if step_now + 1 < tick_count:
            received = passed_along(grad_input, "section", -1)
    normed_rows = saved_buffers[1].reshape(-1, saved_buffers[1].shape[-1])
    normed_out_rows = saved_buffers[7].reshape(-1, saved_buffers[7].shape[-1])
    total_win = lax.dot_general(
        normed_rows,
        proj_buffer.reshape(-1, proj_buffer.shape[-1]),
        (((0,), (0,)), ((), ())),
        preferred_element_type=jnp.float32,
    )
    total_wout = lax.dot_general(
        normed_out_rows,
        cot_buffer.reshape(-1, cot_buffer.shape[-1]),
        (((0,), (0,)), ((), ())),
        preferred_element_type=jnp.float32,
    )
    shard_win, shard_wout = (
        lax.psum_scatter(total_win, "fsdp", scatter_dimension=0, tiled=True),
        lax.psum_scatter(total_wout, "fsdp", scatter_dimension=0, tiled=True),
    )
    shard_win, shard_wout = lax.psum((shard_win, shard_wout), "seq")
    small_sums = lax.psum(tuple(totals), ("seq", "fsdp"))
    gain_in_grad, conv_grad, bias_grad, shift_grad, rate_grad, skip_grad, gain_out_grad = small_sums
    layer_out = out_buffer[None, :, None]
    input_grad = grad_buffer[None, :, None]
    return (
        layer_out,
        input_grad,
        gain_in_grad[None],
        shard_win[None],
        conv_grad[None],
        bias_grad[None],
        shift_grad[None],
        rate_grad[None],
        skip_grad[None],
        gain_out_grad[None],
        shard_wout[None],
    )


def solution(mesh):
    return jax.shard_map(
        shards,
        mesh=mesh,
        in_specs=(
            P(None, "fsdp", "seq", None),
            P(None, "fsdp", "seq", None),
            P("section", None),
            P("section", "fsdp", None),
            P("section", None, None),
            P("section", None),
            P("section", None),
            P("section", None),
            P("section", None),
            P("section", None),
            P("section", "fsdp", None),
        ),
        out_specs=(
            P("section", None, "fsdp", "seq", None),
            P("section", None, "fsdp", "seq", None),
            P("section", None),
            P("section", "fsdp", None),
            P("section", None, None),
            P("section", None),
            P("section", None),
            P("section", None),
            P("section", None),
            P("section", None),
            P("section", "fsdp", None),
        ),
        check_vma=False,
    )
```

profile of v0, /device:TPU:0, one launch (start us, length us, event | category | flops | bytes accessed | tf_op | source)
XLA Modules:
  0.0 2500.2 jit_solution(15907207655664515080)
XLA Ops:
  16.9 333.4 %all-gather.5.cloned.1.call-done = bf16[1,1536,6448]{1,2,0:T(8,128)(2,1)} async-done(((bf16[1,384,6448]{1,2,0:T(8,128)(2,1)}), bf16[1,1536,6448]{1,2,0:T(8,128)(2,1)}) %all-gather.5.cloned.1.call-update) | async-done | bytes 19808272 | tf_op jit(solution)/shard_map/all_gather | solution.py:203
  350.3 13.9 fusion.334
  368.9 8.9 all_gather.16
  414.0 103.4 %all-gather.7.cloned.1.call-done = bf16[1,3072,1536]{2,1,0:T(8,128)(2,1)} async-done(((bf16[1,768,1536]{2,1,0:T(8,128)(2,1)}), bf16[1,3072,1536]{2,1,0:T(8,128)(2,1)}) %all-gather.7.cloned.1.call-update) | async-done | bytes 9437200 | tf_op jit(solution)/shard_map/all_gather | solution.py:204
  518.2 6.3 bitcast_dynamic-update-slice_fusion.17
  535.4 14.3 fusion.335
  551.8 8.4 all_gather.18
  618.5 4.2 all-to-all-start.5
  631.5 6.5 bitcast_dynamic-update-slice_fusion.16
  652.4 14.3 fusion.336
  668.9 8.4 all_gather.19
  740.5 4.6 all-to-all-start.8
  755.7 7.7 multiply_reduce_fusion.5
  804.7 7.9 fusion.61
  867.6 10.6 fusion.179
  889.7 4.3 all-to-all-start.12
  938.9 7.9 fusion.63
  998.1 5.3 reduce-scatter.8.cloned.1.call-done
  1004.4 10.6 fusion.183
  1032.5 4.7 all-to-all-done.15
  1058.5 7.8 fusion.65
  1093.8 10.3 convolution_bitcast_fusion.1
  1126.8 5.2 multiply_reduce_fusion.12
  1133.3 4.3 all-to-all-start.16
  1147.2 17.2 convolution_bitcast_fusion
  1170.2 8.4 fusion.187
  1179.3 252.7 %reduce-scatter.14.cloned.1.call-done = f32[768,1536]{1,0:T(8,128)} async-done(((f32[3072,1536]{1,0:T(8,128)}), f32[768,1536]{1,0:T(8,128)}) %reduce-scatter.14.cloned.1.call-update) | async-done | bytes 4718608 | tf_op jit(solution)/shard_map/reduce_scatter | solution.py:388
  1432.0 652.0 %reduce-scatter.12.cloned.1.call-done = f32[384,6448]{0,1:T(8,128)} async-done(((f32[1536,6448]{0,1:T(8,128)}), f32[384,6448]{0,1:T(8,128)}) %reduce-scatter.12.cloned.1.call-update) | async-done | bytes 9904144 | tf_op jit(solution)/shard_map/reduce_scatter | solution.py:387
  2085.1 5.5 fusion.57
  2092.9 107.4 %all-reduce.77.cloned.1.call-done = (f32[1,1536]{1,0:T(1,128)}, f32[1,4,3328]{2,1,0:T(4,128)}, f32[1,3328]{1,0:T(1,128)}, f32[1,48]{1,0:T(1,128)}, f32[1,48]{1,0...) async-done(((f32[1,1536]{1,0:T(1,128)}, f32[1,4,3328]{2,1,0:T(4,128)}, f32[1,3328]{1,0:T(1,128)}, f32[1,48]{1,0:T(1,128)}, f32[1,48]{1,0:T(1,128)}, ...) | async-done | bytes 85584 | tf_op jit(solution)/shard_map/psum | solution.py:391
  2200.3 277.4 %all-reduce.79.cloned.1.call-done = (f32[1,384,6448]{1,2,0:T(8,128)}, f32[1,768,1536]{2,1,0:T(8,128)}) async-done(((f32[1,384,6448]{1,2,0:T(8,128)}, f32[1,768,1536]{2,1,0:T(8,128)}), (f32[1,384,6448]{1,2,0:T(8,128)}, f32[1,768,1536]{2,1,0:T(8,128)})) %all-reduce.79.cloned.1.call-update) | async-done | bytes 14622736 | tf_op jit(solution)/shard_map/psum | solution.py:390
  2479.2 8.4 copy.459
  (953 shorter events, 540.4 us)
Async XLA Ops:
  7.3 343.0 %all-gather.5.cloned.1.call-start = ((), (), s32[]{:S(2)}) async-start(), calls=%async_computation.28 | async-start | bytes 24760320 | tf_op jit(solution)/shard_map/all_gather | solution.py:203
  8.0 509.4 %all-gather.7.cloned.1.call-start = ((), (), s32[]{:S(2)}) async-start(), calls=%async_computation.29 | async-start | bytes 11796480 | tf_op jit(solution)/shard_map/all_gather | solution.py:204
  365.0 18.6 all-to-all-start.1
  383.6 11.4 all-to-all-start
  401.0 10.0 all-to-all-start.2
  524.5 9.5 collective-permute-start
  568.9 11.1 all-to-all-start.4
  580.0 25.9 %all-to-all-start.3 = ((bf16[64,4,768]{2,0,1:T(8,128)(2,1)}), bf16[64,4,768]{2,0,1:T(8,128)(2,1)}, u32[]{:S(2)}, u32[]{:S(2)}) async-start(bf16[64,4,768]{2,0,1:T(8,128)(2,1)} %bitcast.1056), calls=%async_computation.3 | async-start | bytes 786432 | tf_op jit(solution)/shard_map/all_to_all | solution.py:222
  618.5 10.2 all-to-all-start.5
  638.0 11.4 collective-permute-start.1
  689.1 8.7 all-to-all-start.7
  697.8 27.2 %all-to-all-start.6 = ((bf16[64,4,768]{2,0,1:T(8,128)(2,1)}), bf16[64,4,768]{2,0,1:T(8,128)(2,1)}, u32[]{:S(2)}, u32[]{:S(2)}) async-start(bf16[64,4,768]{2,0,1:T(8,128)(2,1)} %bitcast.1055), calls=%async_computation.6 | async-start | bytes 786432 | tf_op jit(solution)/shard_map/all_to_all | solution.py:222
  740.5 10.6 all-to-all-start.8
  765.6 11.5 all-to-all-start.9
  830.2 22.1 all-to-all-start.11
  834.4 32.2 %reduce-scatter.6.cloned.1.call-start = ((), (), s32[]{:S(2)}) async-start(), calls=%async_computation.23 | async-start | bytes 327680 | tf_op jit(solution)/shard_map/reduce_scatter | solution.py:308
  852.3 11.5 all-to-all-start.10
  879.9 3.3 collective-permute-start.2
  889.7 11.6 all-to-all-start.12
  964.3 22.2 all-to-all-start.14
  968.2 35.2 %reduce-scatter.8.cloned.1.call-start = ((), (), s32[]{:S(2)}) async-start(), calls=%async_computation.24 | async-start | bytes 327680 | tf_op jit(solution)/shard_map/reduce_scatter | solution.py:308
  986.6 10.7 all-to-all-start.13
  1016.0 3.3 collective-permute-start.3
  1025.9 11.4 all-to-all-start.15
  1030.0 114.1 %reduce-scatter.10.cloned.1.call-start = ((), (), s32[]{:S(2)}) async-start(), calls=%async_computation.25 | async-start | bytes 327680 | tf_op jit(solution)/shard_map/reduce_scatter | solution.py:308
  1091.6 340.4 %reduce-scatter.14.cloned.1.call-start = ((), (), s32[]{:S(2)}) async-start(), calls=%async_computation.27 | async-start | bytes 23592960 | tf_op jit(solution)/shard_map/reduce_scatter | solution.py:388
  1118.2 15.1 all-to-all-start.17
  1133.3 10.2 all-to-all-start.16
  1137.6 946.5 %reduce-scatter.12.cloned.1.call-start = ((), (), s32[]{:S(2)}) async-start(), calls=%async_computation.26 | async-start | bytes 49520640 | tf_op jit(solution)/shard_map/reduce_scatter | solution.py:387
  1164.8 1035.5 %all-reduce.77.cloned.1.call-start = ((), (), s32[]{:S(2)}) async-start(), calls=%async_computation.30 | async-start | bytes 173056 | tf_op jit(solution)/shard_map/psum | solution.py:391
  1179.3 1298.4 %all-reduce.79.cloned.1.call-start = ((), (), s32[]{:S(2)}) async-start(), calls=%async_computation.31 | async-start | bytes 29245440 | tf_op jit(solution)/shard_map/psum | solution.py:390
  2090.6 397.0 %copy-start.76 = (bf16[1,2,1,64,1536]{4,3,1,2,0:T(8,128)(2,1)}, bf16[1,2,1,64,1536]{4,3,1,2,0:T(8,128)(2,1)S(1)}, u32[]{:S(2)}) copy-start(bf16[1,2,1,64,1536]{4,3,1,2,0:T(8,128)(2,1)S(1)} %fusion.57) | copy-start | bytes 1179652
  (203 other events, 5552.3 us)
Sparse Core Ops, SparseCore 0:
  9.7 340.5 all-gather.4
  351.9 165.4 all-gather.6
  843.8 22.7 reduce-scatter.5
  977.8 25.4 reduce-scatter.7
  1091.7 24.0 reduce-scatter.9
  1118.2 313.7 reduce-scatter.13
  1434.4 649.5 reduce-scatter.11
  2091.6 108.6 all-reduce.76
  2204.0 273.6 all-reduce.78
where the time goes:
time: 2520 us; the launch traced here: 2500 us
  waiting for transfers between devices  1760 us (70%)
  local copies, waits for them, and re-layouts  228 us (9%)
  matrix products  221 us (9%)
  other arithmetic  171 us (7%)
  starting transfers between devices  80.6 us (3%)
  blocking collectives  25.8 us (1%)
    reduce_scatter x1, waiting for transfers between devices, shards(): lax.psum_scatter(total_win, 'fsdp', scatter_dimension=0, tiled=True)  652 us
    all_gather x1, waiting for transfers between devices, shards(): lax.all_gather(w_in[0], 'fsdp', axis=0, tiled=True)  333 us
    psum x1, waiting for transfers between devices, shards(): shard_win, shard_wout = lax.psum((shard_win, shard_wout), 'seq')  277 us
    reduce_scatter x1, waiting for transfers between devices, shards(): lax.psum_scatter(total_wout, 'fsdp', scatter_dimension=0, tiled=True)  253 us
    psum x1, waiting for transfers between devices, shards(): small_sums = lax.psum(tuple(totals), ('seq', 'fsdp'))  107 us
    all_gather x1, waiting for transfers between devices, shards(): lax.all_gather(w_out[0], 'fsdp', axis=0, tiled=True)  103 us
    dot_general x24, matrix products, low_product(): return wrapped(left, right)  67 us
  transfers between devices with their start and end apart: 31, of which 16 were waited for; matrix products, arithmetic and copies ran while one was open for 11% of the time, Pallas kernels for 0%

commit v1 on v0

v1 whole, which is shorter than its diff:
```python
from functools import partial

import jax
import jax.numpy as jnp
from jax import lax
from jax.experimental import pallas as pl
from jax.experimental.pallas import tpu as pltpu
from jax.sharding import PartitionSpec as P

HEADS = 48
HEADDIM = 64
STATE = 128
CONV = 4
SPAN = 256
INNER = 3072
XBC = 3328
SHARED = 2 * STATE
LANES = 128
NORM_EPS = 1e-05
HIGHEST = lax.Precision.HIGHEST
BF16 = jnp.bfloat16
F32 = jnp.float32


def dot(left, right, contract=((1,), (0,)), precision=None):
    return lax.dot_general(
        left, right, (contract, ((), ())), preferred_element_type=F32, precision=precision
    )


def dot_nt(left, right):
    return dot(left, right, ((1,), (1,)))


def dot_tn(left, right):
    return dot(left, right, ((0,), (0,)))


def sigmoid(value):
    return 1.0 / (1.0 + jnp.exp(-value))


def shifted(value, distance):
    if distance == 0:
        return value
    length = value.shape[0]
    rows = lax.broadcasted_iota(jnp.int32, value.shape, 0)
    moved = pltpu.roll(value, distance % length, 0)
    if distance > 0:
        return jnp.where(rows >= distance, moved, 0.0)
    return jnp.where(rows < length + distance, moved, 0.0)


def conv_sum(raw, taps):
    total = taps[CONV : CONV + 1]
    for k in range(CONV):
        total = total + taps[k : k + 1] * shifted(raw, CONV - 1 - k)
    return total


def conv_back(grad, raw, taps):
    grad_raw = 0.0
    rows = []
    for k in range(CONV):
        grad_raw = grad_raw + taps[k : k + 1] * shifted(grad, -(CONV - 1 - k))
        rows.append(jnp.sum(grad * shifted(raw, CONV - 1 - k), axis=0, keepdims=True))
    rows.append(jnp.sum(grad, axis=0, keepdims=True))
    return grad_raw, rows


def stacked(rows, count):
    width = rows[0].shape[1]
    short = count - len(rows)
    return jnp.concatenate(rows + [jnp.zeros((short, width), F32)], axis=0)


def triangles():
    row_ids = lax.broadcasted_iota(jnp.int32, (SPAN, SPAN), 0)
    col_ids = lax.broadcasted_iota(jnp.int32, (SPAN, SPAN), 1)
    return row_ids >= col_ids


def step_sizes(dt_raw, dt_row):
    shift = dt_raw + dt_row
    step = jnp.maximum(shift, 0.0) + jnp.log1p(jnp.exp(-jnp.abs(shift)))
    return step, sigmoid(shift)


def low_half():
    return lax.broadcasted_iota(jnp.int32, (SPAN, LANES), 1) < HEADDIM


def head_lanes(h):
    lanes = lax.broadcasted_iota(jnp.int32, (1, LANES), 1)
    return (lanes < HEADDIM) if h % 2 == 0 else (lanes >= HEADDIM)


def forward_kernel(
    heads, u_ref, gain_ref, w_ref, ch_ref, bc_ref, dtp_ref, wo_ref,
    out_ref, ss_ref, normed_ref, gate_ref, xraw_ref, bcraw_ref, dtraw_ref, mixed_ref,
):
    length = u_ref.shape[1]
    wide = ch_ref.shape[1]
    blocks = length // SPAN
    rows = u_ref[0].astype(F32)
    scale = lax.rsqrt(jnp.mean(rows * rows, axis=-1, keepdims=True) + NORM_EPS)
    normed = (rows * scale * gain_ref[...]).astype(BF16)
    normed_ref[0] = normed
    gate = dot(normed, w_ref[:, :wide])
    gate_ref[0] = gate
    x_raw = dot(normed, w_ref[:, wide : 2 * wide]).astype(BF16)
    xraw_ref[0] = x_raw
    rest = dot(normed, w_ref[:, 2 * wide :]).astype(BF16)
    bcraw_ref[0] = rest[:, :SHARED]
    dtraw_ref[0] = rest[:, SHARED:]
    conv_x = conv_sum(x_raw.astype(F32), ch_ref[...])
    act_x = (conv_x * sigmoid(conv_x)).astype(BF16)
    conv_bc = conv_sum(rest[:, :SHARED].astype(F32), bc_ref[...])
    act_bc = (conv_bc * sigmoid(conv_bc)).astype(BF16)
    step, _ = step_sizes(rest[:, SHARED:].astype(F32), dtp_ref[0:1])
    rate = jnp.exp(dtp_ref[1:2])
    causal = triangles()
    ones = causal.astype(F32)
    lower = low_half()
    carries = [None] * heads
    for b in range(blocks):
        span = slice(b * SPAN, (b + 1) * SPAN)
        step_b = step[span]
        decay = -dot(ones, rate * step_b, precision=HIGHEST)
        decay_t, step_t = decay.T, step_b.T
        b_in, c_out = act_bc[span, :STATE], act_bc[span, STATE:]
        scores = dot_nt(c_out, b_in)
        for first in range(0, heads, 2):
            lanes = slice(first * HEADDIM, first * HEADDIM + LANES)
            x_pair = act_x[span, lanes]
            parts = []
            for h in range(first, min(first + 2, heads)):
                gap = decay[:, h : h + 1] - decay_t[h : h + 1]
                mask = jnp.exp(jnp.where(causal, gap, -1e30))
                weights = (scores * mask * step_t[h : h + 1]).astype(BF16)
                part = dot(weights, x_pair)
                if carries[h] is not None:
                    part += jnp.exp(decay[:, h : h + 1]) * dot(c_out, carries[h].astype(BF16))
                if b + 1 < blocks:
                    last = decay[SPAN - 1 :, h : h + 1]
                    tail = jnp.exp(last - decay[:, h : h + 1]) * step_b[:, h : h + 1]
                    shaped = (b_in.astype(F32) * tail).astype(BF16)
                    fresh = dot_tn(shaped, x_pair)
                    if carries[h] is not None:
                        fresh += jnp.exp(last) * carries[h]
                    carries[h] = fresh
                parts.append(part)
            if len(parts) == 1:
                parts.append(jnp.zeros_like(parts[0]))
            within = jnp.where(lower, parts[0], parts[1])
            mixed = within + ch_ref[5:6, lanes] * x_pair.astype(F32)
            mixed_ref[0, span, lanes] = mixed.astype(BF16)
    gated = mixed_ref[0].astype(F32) * (gate * sigmoid(gate))
    ss_ref[0] = jnp.broadcast_to(jnp.sum(gated * gated, axis=-1, keepdims=True), ss_ref.shape[1:])
    out_ref[0] = dot((gated * ch_ref[6:7]).astype(BF16), wo_ref[...]).astype(BF16)


def backward_kernel(
    heads, h_ref, aux_ref, gate_ref, xraw_ref, bcraw_ref, dtraw_ref, mixed_ref,
    w_ref, ch_ref, bc_ref, dtp_ref, wo_ref,
    dn_ref, pg_ref, no_ref, gch_ref, gbc_ref, gdt_ref,
    dmix_s, dx_s, dbc_s, ddt_s,
):
    length = h_ref.shape[1]
    wide = ch_ref.shape[1]
    blocks = length // SPAN
    scale, rdot = aux_ref[0, :, 0:1], aux_ref[0, :, 1:2]
    gate = gate_ref[0]
    mixed = mixed_ref[0].astype(F32)
    sig = sigmoid(gate)
    silu = gate * sig
    gated = mixed * silu
    gain = ch_ref[6:7]
    grad_no = dot_nt(h_ref[0], wo_ref[...])
    grad_g = scale * (gain * grad_no) - gated * (scale * scale * (1.0 / INNER) * rdot)
    scaled = gated * scale
    no_ref[0] = (scaled * gain).astype(BF16)
    gain_row = jnp.sum(grad_no * scaled, axis=0, keepdims=True)
    dmix_s[...] = (grad_g * silu).astype(BF16)
    pg_ref[0, :, :wide] = (grad_g * mixed * (sig * (1.0 + gate * (1.0 - sig)))).astype(BF16)

    x_raw = xraw_ref[0].astype(F32)
    bc_raw = bcraw_ref[0].astype(F32)
    conv_x = conv_sum(x_raw, ch_ref[...])
    sig_x = sigmoid(conv_x)
    act_x = (conv_x * sig_x).astype(BF16)
    conv_bc = conv_sum(bc_raw, bc_ref[...])
    sig_bc = sigmoid(conv_bc)
    act_bc = (conv_bc * sig_bc).astype(BF16)
    step, slope = step_sizes(dtraw_ref[0].astype(F32), dtp_ref[0:1])
    rate = jnp.exp(dtp_ref[1:2])
    causal = triangles()
    ones = causal.astype(F32)
    lower = low_half()
    lane_ids = lax.broadcasted_iota(jnp.int32, (SPAN, LANES), 1)
    last_row = lax.broadcasted_iota(jnp.int32, (SPAN, 1), 0) == SPAN - 1
    decays = []
    for b in range(blocks):
        decays.append(-dot(ones, rate * step[b * SPAN : (b + 1) * SPAN], precision=HIGHEST))
    entering = [[None] * heads for _ in range(blocks)]
    for b in range(blocks - 1):
        span = slice(b * SPAN, (b + 1) * SPAN)
        b_in = act_bc[span, :STATE].astype(F32)
        for h in range(heads):
            lanes = slice(h // 2 * LANES, h // 2 * LANES + LANES)
            column = decays[b][:, h : h + 1]
            last = column[SPAN - 1 :]
            tail = jnp.exp(last - column) * step[span, h : h + 1]
            fresh = dot_tn((b_in * tail).astype(BF16), act_x[span, lanes])
            if entering[b][h] is not None:
                fresh += jnp.exp(last) * entering[b][h]
            entering[b + 1][h] = fresh
    leaving = [None] * heads
    rate_row = jnp.zeros((1, LANES), F32)
    for b in reversed(range(blocks)):
        span = slice(b * SPAN, (b + 1) * SPAN)
        step_b, decay = step[span], decays[b]
        decay_t, step_t = decay.T, step_b.T
        b_in, c_out = act_bc[span, :STATE], act_bc[span, STATE:]
        scores = dot_nt(c_out, b_in)
        grad_scores = jnp.zeros((SPAN, SPAN), F32)
        grad_b = jnp.zeros((SPAN, STATE), F32)
        grad_c = jnp.zeros((SPAN, STATE), F32)
        row_sums = jnp.zeros((SPAN, LANES), F32)
        grad_step = jnp.zeros((SPAN, LANES), F32)
        col_rows = []
        for first in range(0, heads, 2):
            lanes = slice(first * HEADDIM, first * HEADDIM + LANES)
            x_pair = act_x[span, lanes]
            grad_pair = dmix_s[span, lanes]
            parts = []
            for h in range(first, min(first + 2, heads)):
                own = head_lanes(h)
                grad_own = jnp.where(own, grad_pair, jnp.zeros((), BF16))
                column = decay[:, h : h + 1]
                mask = jnp.exp(jnp.where(causal, column - decay_t[h : h + 1], -1e30))
                spread = mask * step_t[h : h + 1]
                weights = (scores * spread).astype(BF16)
                part = dot_tn(weights, grad_pair)
                grad_w = dot_nt(grad_own, x_pair)
                grad_scores += grad_w * spread
                pulled = grad_w * (scores * mask)
                col_rows.append(jnp.sum(pulled, axis=0, keepdims=True))
                row_sum = jnp.sum(pulled * step_t[h : h + 1], axis=1, keepdims=True)
                if entering[b][h] is not None:
                    carry = entering[b][h].astype(BF16)
                    grown = jnp.exp(column)
                    grad_grown = grad_own.astype(F32) * grown
                    grad_c += dot_nt(grad_grown.astype(BF16), carry)
                    grad_carry = dot_tn(c_out, grad_grown.astype(BF16))
                    row_sum += jnp.sum(grad_grown * dot(c_out, carry), axis=1, keepdims=True)
                else:
                    grad_carry = None
                if leaving[h] is not None:
                    last = column[SPAN - 1 :]
                    fade = jnp.exp(last - column)
                    tail = fade * step_b[:, h : h + 1]
                    b_wide = b_in.astype(F32)
                    grad_state = leaving[h].astype(BF16)
                    grad_shaped = dot_nt(x_pair, grad_state)
                    part += dot((b_wide * tail).astype(BF16), grad_state)
                    grad_b += grad_shaped * tail
                    grad_tail = jnp.sum(grad_shaped * b_wide, axis=1, keepdims=True)
                    grad_step += jnp.where(lane_ids == h, grad_tail * fade, 0.0)
                    moved = grad_tail * tail
                    total = jnp.sum(moved, axis=0, keepdims=True)
                    if entering[b][h] is not None:
                        faded = jnp.exp(last) * leaving[h]
                        kept = jnp.sum(faded * entering[b][h], axis=1, keepdims=True)
                        total += jnp.sum(kept, axis=0, keepdims=True)
                        grad_carry += faded
                    row_sum += jnp.where(last_row, total, 0.0) - moved
                leaving[h] = grad_carry
                row_sums += jnp.where(lane_ids == h, row_sum, 0.0)
                parts.append(part)
            if len(parts) == 1:
                parts.append(jnp.zeros_like(parts[0]))
            grad_x = jnp.where(lower, parts[0], parts[1])
            dx_s[span, lanes] = grad_x + ch_ref[5:6, lanes] * grad_pair.astype(F32)
        col_sums = stacked(col_rows, LANES).T
        low_scores = grad_scores.astype(BF16)
        dbc_s[span, :STATE] = grad_b + dot_tn(low_scores, c_out)
        dbc_s[span, STATE:] = grad_c + dot(low_scores, b_in)
        grad_decay = dot(
            ones, row_sums - step_b * col_sums, ((0,), (0,)), precision=HIGHEST
        )
        ddt_s[span] = col_sums + grad_step - rate * grad_decay
        rate_row -= jnp.sum(grad_decay * step_b, axis=0, keepdims=True)

    skip_row = jnp.sum(dmix_s[...].astype(F32) * act_x.astype(F32), axis=0, keepdims=True)
    grad_conv = dx_s[...] * (sig_x * (1.0 + conv_x * (1.0 - sig_x)))
    grad_raw, ch_rows = conv_back(grad_conv, x_raw, ch_ref[...])
    pg_ref[0, :, wide : 2 * wide] = grad_raw.astype(BF16)
    grad_conv = dbc_s[...] * (sig_bc * (1.0 + conv_bc * (1.0 - sig_bc)))
    grad_raw, bc_rows = conv_back(grad_conv, bc_raw, bc_ref[...])
    pg_ref[0, :, 2 * wide : 2 * wide + SHARED] = grad_raw.astype(BF16)
    grad_dt = ddt_s[...] * slope
    pg_ref[0, :, 2 * wide + SHARED :] = grad_dt.astype(BF16)
    dn_ref[0] = dot_nt(pg_ref[0], w_ref[...]).astype(BF16)
    grads = (
        (gch_ref, ch_rows + [skip_row, gain_row]),
        (gbc_ref, bc_rows),
        (gdt_ref, [jnp.sum(grad_dt, axis=0, keepdims=True), rate_row * rate]),
    )
    for ref, rows in grads:
        value = stacked(rows, 8)

        @pl.when(pl.program_id(0) == 0)
        def _(ref=ref, value=value):
            ref[...] = value

        @pl.when(pl.program_id(0) > 0)
        def _(ref=ref, value=value):
            ref[...] += value


def whole_spec(array):
    return pl.BlockSpec(array.shape, lambda i: (0,) * array.ndim)


def row_spec(length, width):
    return pl.BlockSpec((1, length, width), lambda i: (i, 0, 0))


PARAMS = dict(vmem_limit_bytes=60 * 1024 * 1024)


def run_forward(heads, rows, layer):
    count, length, width = rows.shape
    wide = layer["ch"].shape[1]
    constants = [layer[k] for k in ("gain", "w", "ch", "bc", "dtp", "wo")]
    outs = [
        (width, BF16), (LANES, F32), (width, BF16), (wide, F32),
        (wide, BF16), (SHARED, BF16), (LANES, BF16), (wide, BF16),
    ]
    return pl.pallas_call(
        partial(forward_kernel, heads),
        grid=(count,),
        out_shape=[jax.ShapeDtypeStruct((count, length, n), t) for n, t in outs],
        in_specs=[row_spec(length, width)] + [whole_spec(c) for c in constants],
        out_specs=[row_spec(length, n) for n, _ in outs],
        compiler_params=pltpu.CompilerParams(**PARAMS),
        name="forward",
    )(rows, *constants)


def run_backward(heads, grad_rows, aux, saved, layer):
    count, length, width = grad_rows.shape
    wide = layer["ch"].shape[1]
    columns = layer["w"].shape[1]
    given = [grad_rows, aux, *saved]
    constants = [layer[k] for k in ("w", "ch", "bc", "dtp", "wo")]
    outs = [(width, BF16), (columns, BF16), (wide, BF16)]
    sums = [(8, wide), (8, SHARED), (8, LANES)]
    return pl.pallas_call(
        partial(backward_kernel, heads),
        grid=(count,),
        out_shape=[jax.ShapeDtypeStruct((count, length, n), t) for n, t in outs]
        + [jax.ShapeDtypeStruct(s, F32) for s in sums],
        in_specs=[row_spec(length, g.shape[2]) for g in given] + [whole_spec(c) for c in constants],
        out_specs=[row_spec(length, n) for n, _ in outs]
        + [pl.BlockSpec(s, lambda i: (0, 0)) for s in sums],
        scratch_shapes=[
            pltpu.VMEM((length, wide), BF16),
            pltpu.VMEM((length, wide), F32),
            pltpu.VMEM((length, SHARED), F32),
            pltpu.VMEM((length, LANES), F32),
        ],
        compiler_params=pltpu.CompilerParams(**PARAMS),
        name="backward",
    )(*given, *constants)


class Plan:
    def __init__(self, seq, fsdp):
        self.seq, self.fsdp = seq, fsdp
        halves = 2
        if fsdp % 2 or HEADS % (seq * 2) or (HEADS // fsdp) % seq:
            halves = 1
        self.halves, self.mates = halves, fsdp // halves
        self.heads = HEADS // (seq * halves)
        self.pieces = self.mates if (HEADS // fsdp) % seq == 0 else 1
        channels = self.heads * HEADDIM
        self.channels = channels
        self.wide = -(-channels // LANES) * LANES
        self.peer_groups = [[lo + self.mates * h for h in range(halves)] for lo in range(self.mates)]
        self.mate_groups = [[h * self.mates + j for j in range(self.mates)] for h in range(halves)]

    def split(self, array, axis):
        size = array.shape[axis] // (self.halves * self.pieces * self.seq)
        shape = array.shape[:axis] + (self.halves, self.pieces, self.seq, size) + array.shape[axis + 1 :]
        return array.reshape(shape)

    def take(self, array, axis, place):
        array = lax.dynamic_index_in_dim(self.split(array, axis), place, axis + 2, False)
        shape = array.shape[: axis + 1] + (-1,) + array.shape[axis + 3 :]
        return jnp.moveaxis(array.reshape(shape), axis, 0)

    def put(self, parts, axis):
        size = parts.shape[axis + 2] // self.pieces
        shape = parts.shape[: axis + 2] + (self.pieces, size) + parts.shape[axis + 3 :]
        parts = jnp.moveaxis(parts.reshape(shape), (1, axis + 2, 0), (axis, axis + 1, axis + 2))
        shape = parts.shape[:axis] + (-1,) + parts.shape[axis + 4 :]
        return parts.reshape(shape)


def widened(array, axis, size):
    pads = [(0, 0)] * array.ndim
    pads[axis] = (0, size - array.shape[axis])
    return jnp.pad(array, pads)


def shards(
    tokens, cotangent, norm_gain, w_in, conv_weight, conv_bias, dt_bias, a_log, skip_gain, gate_gain, w_out
):
    section = lax.axis_index("section")
    place = lax.axis_index("seq")
    depth = lax.axis_index("fsdp")
    plan = Plan(lax.axis_size("seq"), lax.axis_size("fsdp"))
    half = depth // plan.mates
    micro, _, span, width = tokens.shape
    layers = lax.axis_size("section")
    wide, channels, heads = plan.wide, plan.channels, plan.heads

    shard = w_in[0]
    gate_part = widened(plan.take(shard[:, :INNER], 1, place), 2, wide)
    x_part = widened(plan.take(shard[:, INNER : 2 * INNER], 1, place), 2, wide)
    shared_part = jnp.broadcast_to(
        shard[:, 2 * INNER : INNER + XBC], (plan.halves, shard.shape[0], SHARED)
    )
    dt_part = widened(plan.take(shard[:, INNER + XBC :], 1, place), 2, LANES)
    tile = jnp.concatenate([gate_part, x_part, shared_part, dt_part], axis=2)
    tile = jnp.repeat(tile, plan.mates, axis=0)
    tile = lax.all_to_all(tile, "fsdp", 0, 0, tiled=True).reshape(width, -1)
    w_tiles = lax.all_gather(tile, "section", axis=0)
    if plan.pieces == plan.mates:
        piece = w_out[0].reshape(plan.seq, -1, width)
        piece = lax.dynamic_index_in_dim(piece, place, 0, False)
        rows_out = lax.all_gather(
            piece, "fsdp", axis=0, tiled=True, axis_index_groups=plan.mate_groups
        )
    else:
        rows_out = lax.all_gather(w_out[0], "fsdp", axis=0, tiled=True)
        rows_out = lax.dynamic_index_in_dim(plan.take(rows_out, 0, place), half, 0, False)
    wo_tiles = lax.all_gather(widened(rows_out, 0, wide), "section", axis=0)

    def own(array, axis, size):
        part = lax.dynamic_index_in_dim(plan.take(array, axis, place), half, 0, False)
        return widened(part, axis, size)

    skip_wide = jnp.repeat(skip_gain[0], HEADDIM)[None]
    by_channel = jnp.concatenate(
        [conv_weight[0, :, :INNER], conv_bias[:, :INNER], skip_wide, gate_gain, jnp.zeros((1, INNER))], 0
    )
    by_channel = own(by_channel, 1, wide)
    by_shared = jnp.concatenate(
        [conv_weight[0, :, INNER:], conv_bias[:, INNER:], jnp.zeros((3, SHARED))], 0
    )
    by_head = jnp.concatenate([dt_bias, a_log, jnp.zeros((6, HEADS))], 0)
    by_head = own(by_head, 1, LANES)
    smalls = jnp.concatenate(
        [by_channel.ravel(), by_shared.ravel(), by_head.ravel(), norm_gain[0]]
    )
    smalls = lax.all_gather(smalls, "section", axis=0)
    cuts = [8 * wide, 8 * (wide + SHARED), 8 * (wide + SHARED + LANES)]
    params = []
    for l in range(layers):
        ch, bc, dtp, gain = jnp.split(smalls[l], cuts)
        params.append(
            dict(
                gain=gain[None], w=w_tiles[l], wo=wo_tiles[l],
                ch=ch.reshape(8, -1), bc=bc.reshape(8, -1), dtp=dtp.reshape(8, -1),
            )
        )

    def gather_rows(own_rows):
        rows = lax.all_gather(own_rows, "seq", axis=0, tiled=True)
        if plan.halves == 1:
            return rows[None]
        return lax.all_gather(rows, "fsdp", axis=0, axis_index_groups=plan.peer_groups)

    def sum_rows(parts):
        if plan.halves == 1:
            rows = parts[0]
        else:
            rows = lax.psum_scatter(
                parts, "fsdp", scatter_dimension=0, axis_index_groups=plan.peer_groups
            )
        return lax.psum_scatter(rows, "seq", scatter_dimension=0, tiled=True)

    own_tokens = lax.dynamic_index_in_dim(tokens, section, 0, False)[0]
    own_cot = lax.dynamic_index_in_dim(cotangent, section, 0, False)[0]
    inputs, outputs, branch, saved, scales = [own_tokens], [], [], [], []
    for l in range(layers):
        rows = gather_rows(inputs[l])
        parts, square, normed, *kept = run_forward(heads, rows, params[l])
        saved.append((normed, kept))
        total = sum_rows(parts).astype(F32)
        square = sum_rows(square)[:, :1]
        scale = lax.rsqrt(square / INNER + NORM_EPS)
        branch.append(total * scale)
        scales.append(scale)
        outputs.append((inputs[l].astype(F32) + branch[l]).astype(BF16))
        inputs.append(outputs[l])
    grads_in, small_grads = [None] * layers, [None] * layers
    w_grads, wo_grads = [None] * layers, [None] * layers
    grad_rows = own_cot
    for l in reversed(range(layers)):
        rdot = jnp.sum(grad_rows.astype(F32) * branch[l], axis=-1, keepdims=True)
        aux = widened(jnp.concatenate([scales[l], rdot], axis=1), 1, LANES)
        all_grads = gather_rows(grad_rows)
        aux = gather_rows(aux)
        normed, kept = saved[l]
        parts, proj_grad, normed_out, g_ch, g_bc, g_dt = run_backward(
            heads, all_grads, aux, kept, params[l]
        )
        w_grads[l] = dot_tn(normed.reshape(-1, width), proj_grad.reshape(-1, proj_grad.shape[-1])).astype(BF16)
        wo_grads[l] = dot_tn(normed_out.reshape(-1, wide), all_grads.reshape(-1, width)).astype(BF16)
        grad_normed = sum_rows(parts).astype(F32)
        rows = inputs[l].astype(F32)
        scale = lax.rsqrt(jnp.mean(rows * rows, axis=-1, keepdims=True) + NORM_EPS)
        scaled = rows * scale
        g_gain = jnp.sum(grad_normed * scaled, axis=0)
        pulled = grad_normed * params[l]["gain"]
        inner = jnp.mean(pulled * scaled, axis=-1, keepdims=True)
        grad = scale * (pulled - scaled * inner) + grad_rows.astype(F32)
        grad_rows = grad.astype(BF16)
        grads_in[l] = grad_rows

        def placed(value, size):
            value = value[..., :size]
            full = jnp.zeros((plan.seq, plan.halves) + value.shape, F32)
            full = lax.dynamic_update_slice(full, value[None, None], (place, half, 0, 0))
            return plan.put(full, 1)

        by_channel = placed(g_ch, channels)
        by_head = placed(g_dt, heads)
        skip = by_channel[5].reshape(HEADS, HEADDIM).sum(-1)
        small_grads[l] = jnp.concatenate(
            [
                g_gain, by_channel[:5].ravel(), g_bc[:5].ravel(), by_head[0], by_head[1], skip, by_channel[6]
            ]
        )

    smalls = lax.psum(jnp.stack(small_grads), ("section", "seq", "fsdp"))
    smalls = lax.dynamic_index_in_dim(smalls, section, 0, False)
    cuts, at = [], 0
    for size in (width, (CONV + 1) * INNER, (CONV + 1) * SHARED, HEADS, HEADS, HEADS):
        at += size
        cuts.append(at)
    g_gain, g_x, g_bc, g_shift, g_rate, g_skip, g_gate = jnp.split(smalls, cuts)
    conv_rows = jnp.concatenate([g_x.reshape(CONV + 1, -1), g_bc.reshape(CONV + 1, -1)], axis=1)

    w_grad = lax.psum_scatter(jnp.stack(w_grads), "section", scatter_dimension=0)
    w_grad = lax.all_to_all(w_grad, "fsdp", 0, 0, tiled=True)
    w_grad = w_grad.reshape(plan.halves, plan.mates, -1, w_grad.shape[-1]).astype(F32).sum(1)
    shared_grad = lax.psum(w_grad[..., 2 * wide : 2 * wide + SHARED].sum(0), "seq")
    head_grads = jnp.concatenate(
        [
            w_grad[..., :channels],
            w_grad[..., wide : wide + channels],
            w_grad[..., 2 * wide + SHARED : 2 * wide + SHARED + heads],
        ],
        axis=-1,
    ).astype(BF16)
    head_grads = lax.all_gather(head_grads, "seq", axis=0)
    grad_w_in = jnp.concatenate(
        [
            plan.put(head_grads[..., :channels], 1),
            plan.put(head_grads[..., channels : 2 * channels], 1),
            shared_grad.astype(BF16),
            plan.put(head_grads[..., 2 * channels :], 1),
        ],
        axis=-1,
    ).astype(F32)
    wo_grad = lax.psum_scatter(jnp.stack(wo_grads)[:, :channels], "section", scatter_dimension=0)
    if plan.pieces == plan.mates:
        wo_grad = lax.psum_scatter(
            wo_grad, "fsdp", scatter_dimension=0, tiled=True, axis_index_groups=plan.mate_groups
        )
        wo_grad = lax.all_gather(wo_grad, "seq", axis=0, tiled=True)
    else:
        full = jnp.zeros((plan.seq, plan.halves) + wo_grad.shape, BF16)
        full = lax.dynamic_update_slice(full, wo_grad[None, None], (place, half, 0, 0))
        full = plan.put(full, 0)
        wo_grad = lax.psum_scatter(full, "fsdp", scatter_dimension=0, tiled=True)
        wo_grad = lax.psum(wo_grad, "seq")

    def home(per_layer):
        return lax.all_to_all(jnp.stack(per_layer), "section", 0, 0, tiled=True)[None, :, None]

    return (
        home(outputs),
        home(grads_in),
        g_gain[None],
        grad_w_in[None],
        conv_rows[None, :CONV],
        conv_rows[CONV:],
        g_shift[None],
        g_rate[None],
        g_skip[None],
        g_gate[None],
        wo_grad.astype(F32)[None],
    )


def solution(mesh):
    return jax.shard_map(
        shards,
        mesh=mesh,
        in_specs=(
            P(None, "fsdp", "seq", None),
            P(None, "fsdp", "seq", None),
            P("section", None),
            P("section", "fsdp", None),
            P("section", None, None),
            P("section", None),
            P("section", None),
            P("section", None),
            P("section", None),
            P("section", None),
            P("section", "fsdp", None),
        ),
        out_specs=(
            P("section", None, "fsdp", "seq", None),
            P("section", None, "fsdp", "seq", None),
            P("section", None),
            P("section", "fsdp", None),
            P("section", None, None),
            P("section", None),
            P("section", None),
            P("section", None),
            P("section", None),
            P("section", None),
            P("section", "fsdp", None),
        ),
        check_vma=False,
    )
```

time: 2520 us -> 1140 us (0.45)
  waiting for transfers between devices: 1760 us -> 771 us
  matrix products: 221 us -> 7.99 us
  blocking collectives: 25.8 us -> 162 us
  local copies, waits for them, and re-layouts: 228 us -> 95 us
  other arithmetic: 171 us -> 44.5 us
  starting transfers between devices: 80.6 us -> 12.6 us
    reduce_scatter x5 -> x15, waiting for transfers between devices: 911 us -> 414 us  [the longest x6 189 us: sum_rows(): lax.psum_scatter(parts, 'fsdp', scatter_dimension=0, axis_index_groups=pl...]
    psum x2 -> x1, waiting for transfers between devices: 385 us -> 108 us  [shards(): smalls = lax.psum(jnp.stack(small_grads), ('section', 'seq', 'fsdp'))]
    all_gather x2 -> x9, waiting for transfers between devices: 437 us -> 230 us  [the longest x4 107 us: gather_rows(): lax.all_gather(rows, 'fsdp', axis=0, axis_index_groups=plan.peer_groups)]
    dot_general x44 -> x4, matrix products: 211 us -> 7.99 us  [dot(): lax.dot_general(left, right, (contract, ((), ())), preferred_element_type...]
    all_gather x3 -> x9, blocking collectives: 25.8 us -> 119 us  [the longest x6 63.7 us: gather_rows(): rows = lax.all_gather(own_rows, 'seq', axis=0, tiled=True)]
    all_to_all x18 -> x2, starting transfers between devices: 71.9 us -> 11.3 us  [the longest x1 6.32 us: shards(): tile = lax.all_to_all(tile, 'fsdp', 0, 0, tiled=True).reshape(width, -1)]
    all_to_all x40 -> x0, local copies, waits for them, and re-layouts: 43 us -> none  [the longest x15 13.7 us: shards(): lax.all_to_all(head_grads[1].astype(jnp.bfloat16), 'seq', split_axis=0, c...]
    another operation x65 -> x9, local copies, waits for them, and re-layouts: 38.9 us -> 0.3 us  [the longest x2 0.16 us: shards(): skip = by_channel[5].reshape(HEADS, HEADDIM).sum(-1)]
  transfers between devices with their start and end apart: 31 -> 27, of which waited for: 16 -> 24; matrix products, arithmetic and copies ran while one was open for 11% -> 7% of each run, Pallas kernels for 0% -> 0%
where the time goes in v1:
time: 1140 us; the launch traced here: 1130 us
  waiting for transfers between devices  771 us (68%)
  blocking collectives  162 us (14%)
  local copies, waits for them, and re-layouts  95 us (8%)
  other arithmetic  44.5 us (4%)
  Pallas kernels  21.5 us (2%)
  between operations  15.4 us (1%)
  starting transfers between devices  12.6 us (1%)
    reduce_scatter x6, waiting for transfers between devices, sum_rows(): lax.psum_scatter(parts, 'fsdp', scatter_dimension=0, axis_index_groups=pl...  189 us
    reduce_scatter x6, waiting for transfers between devices, sum_rows(): return lax.psum_scatter(rows, 'seq', scatter_dimension=0, tiled=True)  163 us
    psum x1, waiting for transfers between devices, shards(): smalls = lax.psum(jnp.stack(small_grads), ('section', 'seq', 'fsdp'))  108 us
    all_gather x4, waiting for transfers between devices, gather_rows(): lax.all_gather(rows, 'fsdp', axis=0, axis_index_groups=plan.peer_groups)  107 us
    all_gather x6, blocking collectives, gather_rows(): rows = lax.all_gather(own_rows, 'seq', axis=0, tiled=True)  63.7 us
    all_gather x1, waiting for transfers between devices, shards(): lax.all_gather(piece, 'fsdp', axis=0, tiled=True, axis_index_groups=plan....  61.8 us
    all_gather x2, blocking collectives, gather_rows(): lax.all_gather(rows, 'fsdp', axis=0, axis_index_groups=plan.peer_groups)  53.4 us
    reduce_scatter x1, waiting for transfers between devices, shards(): lax.psum_scatter(wo_grad, 'fsdp', scatter_dimension=0, tiled=True, axis_i...  39.7 us
  transfers between devices with their start and end apart: 27, of which 24 were waited for; matrix products, arithmetic and copies ran while one was open for 7% of the time, Pallas kernels for 0%

profile of v1, /device:TPU:0, one launch (start us, length us, event | category | flops | bytes accessed | tf_op | source)
XLA Modules:
  0.0 1129.7 jit_solution(16231595370303558336)
XLA Ops:
  31.6 61.8 %all-gather.30.cloned.1.call-done = bf16[1,384,1536]{2,1,0:T(8,128)(2,1)} async-done(((bf16[1,192,1536]{2,1,0:T(8,128)(2,1)}), bf16[1,384,1536]{2,1,0:T(8,128)(2,1)}) %all-gather.30.cloned.1.call-update) | async-done | bytes 1179664 | tf_op jit(solution)/shard_map/all_gather | solution.py:444
  93.5 16.5 %all-to-all-done = bf16[4,384,1152]{2,1,0:T(8,128)(2,1)} async-done(((bf16[4,384,1152]{2,1,0:T(8,128)(2,1)}), bf16[4,384,1152]{2,1,0:T(8,128)(2,1)}, u32[]{:S(2)}, u32[]{:S(2)}) %all-to-all-start) | async-done | bytes 3538976 | tf_op jit(solution)/shard_map/all_to_all | solution.py:439
  110.8 11.9 %all-gather = bf16[1,1,256,1536]{3,2,1,0:T(8,128)(2,1)} all-gather(bf16[1,1,64,1536]{3,2,1,0:T(8,128)(2,1)S(1)} %get-tuple-element.168), channel_id=2, replica_groups=mesh['section'=2,'seq'=4,'fsdp'=4] {'seq'}, dimensions={2}, use_global_device_ids=true | all-gather | bytes 983040 | tf_op jit(solution)/shard_map/all_gather | solution.py:482
  141.0 36.0 %all-gather.28.cloned.1.call-done = bf16[2,1,256,1536]{3,2,1,0:T(8,128)(2,1)} async-done(((bf16[1,1,256,1536]{3,2,1,0:T(8,128)(2,1)}), bf16[2,1,256,1536]{3,2,1,0:T(8,128)(2,1)}) %all-gather.28.cloned.1.call-update) | async-done | bytes 1572880 | tf_op jit(solution)/shard_map/all_gather | solution.py:485
  188.4 13.9 %reduce-scatter.20.cloned.1.call-done = f32[1,256,128]{2,1,0:T(8,128)} async-done(((f32[2,256,128]{2,1,0:T(8,128)}), f32[1,256,128]{2,1,0:T(8,128)}) %reduce-scatter.20.cloned.1.call-update) | async-done | bytes 131088 | tf_op jit(solution)/shard_map/reduce_scatter | solution.py:491
  202.4 45.0 %reduce-scatter.16.cloned.1.call-done = bf16[1,256,1536]{2,1,0:T(8,128)(2,1)} async-done(((bf16[2,256,1536]{2,1,0:T(8,128)(2,1)}), bf16[1,256,1536]{2,1,0:T(8,128)(2,1)}) %reduce-scatter.16.cloned.1.call-update) | async-done | bytes 786448 | tf_op jit(solution)/shard_map/reduce_scatter | solution.py:491
  247.5 25.5 %reduce-scatter.22.cloned.1.call-done = f32[64,128]{1,0:T(8,128)} async-done(((f32[256,128]{1,0:T(8,128)}), f32[64,128]{1,0:T(8,128)}) %reduce-scatter.22.cloned.1.call-update) | async-done | bytes 32784 | tf_op jit(solution)/shard_map/reduce_scatter | solution.py:494
  274.5 27.8 %reduce-scatter.18.cloned.1.call-done = bf16[64,1536]{1,0:T(8,128)(2,1)} async-done(((bf16[256,1536]{1,0:T(8,128)(2,1)}), bf16[64,1536]{1,0:T(8,128)(2,1)}) %reduce-scatter.18.cloned.1.call-update) | async-done | bytes 196624 | tf_op jit(solution)/shard_map/reduce_scatter | solution.py:494
  304.7 11.7 %all_gather.88 = bf16[256,1536]{1,0:T(8,128)(2,1)} all-gather(bf16[64,1536]{1,0:T(8,128)(2,1)S(1)} %get-tuple-element.172), channel_id=1, replica_groups=mesh['section'=2,'seq'=4,'fsdp'=4] {'seq'}, dimensions={0}, use_global_device_ids=true | all-gather | bytes 983040 | tf_op jit(solution)/shard_map/all_gather | solution.py:482
  317.7 43.9 %all-gather.34.cloned.1.call-done = bf16[512,1536]{1,0:T(8,128)(2,1)} async-done(((bf16[256,1536]{1,0:T(8,128)(2,1)}), bf16[512,1536]{1,0:T(8,128)(2,1)}) %all-gather.34.cloned.1.call-update) | async-done | bytes 1572880 | tf_op jit(solution)/shard_map/all_gather | solution.py:485
  373.2 13.8 %reduce-scatter.28.cloned.1.call-done = f32[1,256,128]{2,1,0:T(8,128)} async-done(((f32[2,256,128]{2,1,0:T(8,128)}), f32[1,256,128]{2,1,0:T(8,128)}) %reduce-scatter.28.cloned.1.call-update) | async-done | bytes 131088 | tf_op jit(solution)/shard_map/reduce_scatter | solution.py:491
  387.1 45.1 %reduce-scatter.24.cloned.1.call-done = bf16[1,256,1536]{2,1,0:T(8,128)(2,1)} async-done(((bf16[2,256,1536]{2,1,0:T(8,128)(2,1)}), bf16[1,256,1536]{2,1,0:T(8,128)(2,1)}) %reduce-scatter.24.cloned.1.call-update) | async-done | bytes 786448 | tf_op jit(solution)/shard_map/reduce_scatter | solution.py:491
  432.4 25.4 %reduce-scatter.30.cloned.1.call-done = f32[64,128]{1,0:T(8,128)} async-done(((f32[256,128]{1,0:T(8,128)}), f32[64,128]{1,0:T(8,128)}) %reduce-scatter.30.cloned.1.call-update) | async-done | bytes 32784 | tf_op jit(solution)/shard_map/reduce_scatter | solution.py:494
  459.8 27.0 %reduce-scatter.26.cloned.1.call-done = bf16[64,1536]{1,0:T(8,128)(2,1)} async-done(((bf16[256,1536]{1,0:T(8,128)(2,1)}), bf16[64,1536]{1,0:T(8,128)(2,1)}) %reduce-scatter.26.cloned.1.call-update) | async-done | bytes 196624 | tf_op jit(solution)/shard_map/reduce_scatter | solution.py:494
  490.1 11.7 %all-gather.6 = bf16[1,1,256,1536]{3,2,1,0:T(8,128)(2,1)} all-gather(bf16[1,1,64,1536]{3,2,1,0:T(8,128)(2,1)S(1)} %get-tuple-element.174), channel_id=8, replica_groups=mesh['section'=2,'seq'=4,'fsdp'=4] {'seq'}, dimensions={2}, use_global_device_ids=true | all-gather | bytes 983040 | tf_op jit(solution)/shard_map/all_gather | solution.py:482
  512.4 26.7 %all-gather.8 = f32[512,128]{1,0:T(8,128)} all-gather(f32[256,128]{1,0:T(8,128)S(1)} %all_gather.94), channel_id=10, replica_groups={{0,2},{1,3},{4,6},{5,7},{8,10},{9,11},{12,14},{13,15},{16,18},{17,19},{..., dimensions={0}, use_global_device_ids=true | all-gather | bytes 393216 | tf_op jit(solution)/shard_map/all_gather | solution.py:485
  539.1 13.5 %all-gather.36.cloned.1.call-done = bf16[2,1,256,1536]{3,2,1,0:T(8,128)(2,1)} async-done(((bf16[1,1,256,1536]{3,2,1,0:T(8,128)(2,1)}), bf16[2,1,256,1536]{3,2,1,0:T(8,128)(2,1)}) %all-gather.36.cloned.1.call-update) | async-done | bytes 1572880 | tf_op jit(solution)/shard_map/all_gather | solution.py:485
  552.6 12.9 %backward.2 = (f32[4,2,8,384]{3,2,1,0:T(8,128)S(1)}, bf16[2,256,1536]{2,1,0:T(8,128)(2,1)}, f32[8,256]{1,0:T(8,128)}, f32[8,128]{1,0:T(8,128)}, bf16[2,256,1152]{2,1,0:T(8,128)(2,1)}, /*index=5*/bf16[2,256,384]{2,1,0:T(8,128)(2,1)}) fusion(f32[4,2,8,384]{3,2,1,0:T(8,128)S(1)} %broadcast.71.clone, s32[]{:T(128)S(6)} %select_n.40, s32[]{:T(128)S(6)} %select_n.42, ...), kind=kCustom, calls=%fused_computation.93 | custom fusion | bytes 11714568 | tf_op jit(solution)/shard_map/backward/pallas_call | solution.py:360
  566.2 43.0 %reduce-scatter.32.cloned.1.call-done = bf16[1,256,1536]{2,1,0:T(8,128)(2,1)} async-done(((bf16[2,256,1536]{2,1,0:T(8,128)(2,1)}), bf16[1,256,1536]{2,1,0:T(8,128)(2,1)}) %reduce-scatter.32.cloned.1.call-update) | async-done | bytes 786448 | tf_op jit(solution)/shard_map/reduce_scatter | solution.py:491
  610.6 26.7 %reduce-scatter.34.cloned.1.call-done = bf16[64,1536]{1,0:T(8,128)(2,1)} async-done(((bf16[256,1536]{1,0:T(8,128)(2,1)}), bf16[64,1536]{1,0:T(8,128)(2,1)}) %reduce-scatter.34.cloned.1.call-update) | async-done | bytes 196624 | tf_op jit(solution)/shard_map/reduce_scatter | solution.py:494
  641.9 11.7 %all_gather.97 = bf16[256,1536]{1,0:T(8,128)(2,1)} all-gather(bf16[64,1536]{1,0:T(8,128)(2,1)S(1)} %get-tuple-element.170), channel_id=1, replica_groups=mesh['section'=2,'seq'=4,'fsdp'=4] {'seq'}, dimensions={0}, use_global_device_ids=true | all-gather | bytes 983040 | tf_op jit(solution)/shard_map/all_gather | solution.py:482
  664.2 26.7 %all-gather.10 = f32[512,128]{1,0:T(8,128)} all-gather(f32[256,128]{1,0:T(8,128)S(1)} %all_gather.100), channel_id=12, replica_groups={{0,2},{1,3},{4,6},{5,7},{8,10},{9,11},{12,14},{13,15},{16,18},{17,19},{..., dimensions={0}, use_global_device_ids=true | all-gather | bytes 393216 | tf_op jit(solution)/shard_map/all_gather | solution.py:485
  690.9 13.5 %all-gather.38.cloned.1.call-done = bf16[512,1536]{1,0:T(8,128)(2,1)} async-done(((bf16[256,1536]{1,0:T(8,128)(2,1)}), bf16[512,1536]{1,0:T(8,128)(2,1)}) %all-gather.38.cloned.1.call-update) | async-done | bytes 1572880 | tf_op jit(solution)/shard_map/all_gather | solution.py:485
  704.4 12.8 %backward.3 = (f32[4,2,8,384]{3,2,1,0:T(8,128)S(1)}, bf16[2,256,1536]{2,1,0:T(8,128)(2,1)}, f32[8,256]{1,0:T(8,128)}, f32[8,128]{1,0:T(8,128)}, bf16[2,256,1152]{2,1,0:T(8,128)(2,1)}, /*index=5*/bf16[2,256,384]{2,1,0:T(8,128)(2,1)}) fusion(f32[4,2,8,384]{3,2,1,0:T(8,128)S(1)} %broadcast.71, s32[]{:T(128)S(6)} %select_n.40, s32[]{:T(128)S(6)} %select_n.42, ...), kind=kCustom, calls=%fused_computation.94 | custom fusion | bytes 11714568 | tf_op jit(solution)/shard_map/backward/pallas_call | solution.py:360
  733.2 27.8 %reduce-scatter.36.cloned.1.call-done = bf16[1,256,1536]{2,1,0:T(8,128)(2,1)} async-done(((bf16[2,256,1536]{2,1,0:T(8,128)(2,1)}), bf16[1,256,1536]{2,1,0:T(8,128)(2,1)}) %reduce-scatter.36.cloned.1.call-update) | async-done | bytes 786448 | tf_op jit(solution)/shard_map/reduce_scatter | solution.py:491
  763.7 14.7 %reduce-scatter.40.cloned.1.call-done = bf16[1,1536,1152]{2,1,0:T(8,128)(2,1)} async-done(((bf16[2,1536,1152]{2,1,0:T(8,128)(2,1)}), bf16[1,1536,1152]{2,1,0:T(8,128)(2,1)}) %reduce-scatter.40.cloned.1.call-update) | async-done | bytes 3538960 | tf_op jit(solution)/shard_map/reduce_scatter | solution.py:559
  792.3 30.1 %reduce-scatter.38.cloned.1.call-done = bf16[64,1536]{1,0:T(8,128)(2,1)} async-done(((bf16[256,1536]{1,0:T(8,128)(2,1)}), bf16[64,1536]{1,0:T(8,128)(2,1)}) %reduce-scatter.38.cloned.1.call-update) | async-done | bytes 196624 | tf_op jit(solution)/shard_map/reduce_scatter | solution.py:494
  824.6 39.7 %reduce-scatter.44.cloned.1.call-done = bf16[192,1536]{1,0:T(8,128)(2,1)} async-done(((bf16[384,1536]{1,0:T(8,128)(2,1)}), bf16[192,1536]{1,0:T(8,128)(2,1)}) %reduce-scatter.44.cloned.1.call-update) | async-done | bytes 589840 | tf_op jit(solution)/shard_map/reduce_scatter | solution.py:583
  885.7 108.4 %all-reduce.7.cloned.1.call-done = f32[2,21392]{1,0:T(2,128)} async-done(((f32[2,21392]{1,0:T(2,128)}), f32[2,21392]{1,0:T(2,128)}) %all-reduce.7.cloned.1.call-update) | async-done | bytes 171152 | tf_op jit(solution)/shard_map/psum | solution.py:550
  1004.4 31.1 %all-gather.26.cloned.1.call-done = bf16[768,1536]{1,0:T(8,128)(2,1)} async-done(((bf16[192,1536]{1,0:T(8,128)(2,1)}), bf16[768,1536]{1,0:T(8,128)(2,1)}) %all-gather.26.cloned.1.call-update) | async-done | bytes 2359312 | tf_op jit(solution)/shard_map/all_gather | solution.py:586
  1040.8 33.2 %all-reduce.8 = bf16[384,256]{1,0:T(8,128)(2,1)S(1)} all-reduce(f32[384,256]{1,0:T(8,128)} %slice_reduce_fusion), channel_id=1, replica_groups=mesh['section'=2,'seq'=4,'fsdp'=4] {'seq'}, use_global_device_ids=true, to_apply=%region_26.27 | all-reduce | flops 98304 | bytes 589824 | tf_op jit(solution)/shard_map/psum | solution.py:562
  1074.1 30.7 %all-gather.24.cloned.1.call-done = bf16[4,2,384,774]{2,1,3,0:T(2,128)(2,1)} async-done(((bf16[1,2,384,774]{2,1,3,0:T(2,128)(2,1)}), bf16[4,2,384,774]{2,1,3,0:T(2,128)(2,1)}) %all-gather.24.cloned.1.call-update) | async-done | bytes 4755472 | tf_op jit(solution)/shard_map/all_gather | solution.py:571
  (313 shorter events, 194.2 us)
Async XLA Ops:
  24.3 85.6 %all-to-all-start = ((bf16[4,384,1152]{2,1,0:T(8,128)(2,1)}), bf16[4,384,1152]{2,1,0:T(8,128)(2,1)}, u32[]{:S(2)}, u32[]{:S(2)}) async-start(bf16[4,384,1152]{2,1,0:T(8,128)(2,1)} %bitcast.178), calls=%async_computation | async-start | bytes 7077888 | tf_op jit(solution)/shard_map/all_to_all | solution.py:439
  30.7 62.7 %all-gather.30.cloned.1.call-start = ((), (), s32[]{:S(2)}) async-start(), calls=%async_computation.39 | async-start | bytes 1769472 | tf_op jit(solution)/shard_map/all_gather | solution.py:444
  31.5 99.7 %all-gather.32.cloned.1.call-start = ((), (), s32[]{:S(2)}) async-start(), calls=%async_computation.40 | async-start | bytes 3538944 | tf_op jit(solution)/shard_map/all_gather | solution.py:450
  93.4 41.1 %all-gather.22.cloned.1.call-start = ((), (), s32[]{:S(2)}) async-start(), calls=%async_computation.19 | async-start | bytes 10616832 | tf_op jit(solution)/shard_map/all_gather | solution.py:440
  110.0 67.0 %all-gather.28.cloned.1.call-start = ((), (), s32[]{:S(2)}) async-start(), calls=%async_computation.38 | async-start | bytes 2359296 | tf_op jit(solution)/shard_map/all_gather | solution.py:485
  110.8 191.6 %copy-start.5 = (bf16[1,1,64,1536]{3,2,1,0:T(8,128)(2,1)}, bf16[1,1,64,1536]{3,2,1,0:T(8,128)(2,1)S(1)}, u32[]{:S(2)}) copy-start(bf16[1,1,64,1536]{3,2,1,0:T(8,128)(2,1)S(1)} %get-tuple-element.168) | copy-start | bytes 589828
  122.7 79.7 %reduce-scatter.20.cloned.1.call-start = ((), (), s32[]{:S(2)}) async-start(), calls=%async_computation.22 | async-start | bytes 393216 | tf_op jit(solution)/shard_map/reduce_scatter | solution.py:491
  187.8 59.6 %reduce-scatter.16.cloned.1.call-start = ((), (), s32[]{:S(2)}) async-start(), calls=%async_computation.20 | async-start | bytes 2359296 | tf_op jit(solution)/shard_map/reduce_scatter | solution.py:491
  188.4 84.7 %reduce-scatter.22.cloned.1.call-start = ((), (), s32[]{:S(2)}) async-start(), calls=%async_computation.23 | async-start | bytes 163840 | tf_op jit(solution)/shard_map/reduce_scatter | solution.py:494
  202.4 99.9 %reduce-scatter.18.cloned.1.call-start = ((), (), s32[]{:S(2)}) async-start(), calls=%async_computation.21 | async-start | bytes 983040 | tf_op jit(solution)/shard_map/reduce_scatter | solution.py:494
  247.5 114.1 %all-gather.34.cloned.1.call-start = ((), (), s32[]{:S(2)}) async-start(), calls=%async_computation.41 | async-start | bytes 2359296 | tf_op jit(solution)/shard_map/all_gather | solution.py:485
  274.5 97.9 %copy-start.36 = (f32[64]{0:T(128)}, f32[64]{0:T(128)S(1)}, u32[]{:S(2)}) copy-start(f32[64]{0:T(128)S(1)} %get-tuple-element.196) | copy-start | bytes 772
  316.5 70.5 %reduce-scatter.28.cloned.1.call-start = ((), (), s32[]{:S(2)}) async-start(), calls=%async_computation.26 | async-start | bytes 393216 | tf_op jit(solution)/shard_map/reduce_scatter | solution.py:491
  372.4 59.7 %reduce-scatter.24.cloned.1.call-start = ((), (), s32[]{:S(2)}) async-start(), calls=%async_computation.24 | async-start | bytes 2359296 | tf_op jit(solution)/shard_map/reduce_scatter | solution.py:491
  373.2 179.5 %copy-start.3 = (bf16[1536,1152]{1,0:T(8,128)(2,1)S(1)}, bf16[1536,1152]{1,0:T(8,128)(2,1)}, u32[]{:S(2)}) copy-start(bf16[1536,1152]{1,0:T(8,128)(2,1)} %get-tuple-element.175.w_ref) | copy-start | bytes 10616836
  373.2 179.5 %copy-start.23 = (f32[8,384]{1,0:T(8,128)S(1)}, f32[8,384]{1,0:T(8,128)}, u32[]{:S(2)}) copy-start(f32[8,384]{1,0:T(8,128)} %reshape.347.ch_ref) | copy-start | bytes 36868
  373.2 179.4 %copy-start.27 = (f32[1,1024]{1,0:T(1,128)S(1)}, f32[1,1024]{1,0:T(1,128)}, u32[]{:S(2)}) copy-start(f32[1,1024]{1,0:T(1,128)} %get-tuple-element.193) | copy-start | bytes 12292
  373.2 84.6 %reduce-scatter.30.cloned.1.call-start = ((), (), s32[]{:S(2)}) async-start(), calls=%async_computation.27 | async-start | bytes 163840 | tf_op jit(solution)/shard_map/reduce_scatter | solution.py:494
  387.0 99.8 %reduce-scatter.26.cloned.1.call-start = ((), (), s32[]{:S(2)}) async-start(), calls=%async_computation.25 | async-start | bytes 983040 | tf_op jit(solution)/shard_map/reduce_scatter | solution.py:494
  432.2 120.4 %all-gather.36.cloned.1.call-start = ((), (), s32[]{:S(2)}) async-start(), calls=%async_computation.42 | async-start | bytes 2359296 | tf_op jit(solution)/shard_map/all_gather | solution.py:485
  501.8 107.3 %reduce-scatter.32.cloned.1.call-start = ((), (), s32[]{:S(2)}) async-start(), calls=%async_computation.28 | async-start | bytes 2359296 | tf_op jit(solution)/shard_map/reduce_scatter | solution.py:491
  566.2 71.1 %reduce-scatter.34.cloned.1.call-start = ((), (), s32[]{:S(2)}) async-start(), calls=%async_computation.29 | async-start | bytes 983040 | tf_op jit(solution)/shard_map/reduce_scatter | solution.py:494
  609.2 95.2 %all-gather.38.cloned.1.call-start = ((), (), s32[]{:S(2)}) async-start(), calls=%async_computation.43 | async-start | bytes 2359296 | tf_op jit(solution)/shard_map/all_gather | solution.py:485
  653.6 107.3 %reduce-scatter.36.cloned.1.call-start = ((), (), s32[]{:S(2)}) async-start(), calls=%async_computation.30 | async-start | bytes 2359296 | tf_op jit(solution)/shard_map/reduce_scatter | solution.py:491
  717.9 60.5 %reduce-scatter.40.cloned.1.call-start = ((), (), s32[]{:S(2)}) async-start(), calls=%async_computation.33 | async-start | bytes 10616832 | tf_op jit(solution)/shard_map/reduce_scatter | solution.py:559
  728.4 63.8 %reduce-scatter.42.cloned.1.call-start = ((), (), s32[]{:S(2)}) async-start(), calls=%async_computation.35 | async-start | bytes 3538944 | tf_op jit(solution)/shard_map/reduce_scatter | solution.py:581
  733.1 89.3 %reduce-scatter.38.cloned.1.call-start = ((), (), s32[]{:S(2)}) async-start(), calls=%async_computation.31 | async-start | bytes 983040 | tf_op jit(solution)/shard_map/reduce_scatter | solution.py:494
  778.4 86.0 %all-to-all-start.3 = ((bf16[4,384,1152]{2,1,0:T(8,128)(2,1)}), bf16[4,384,1152]{2,1,0:T(8,128)(2,1)}, u32[]{:S(2)}, u32[]{:S(2)}) async-start(bf16[4,384,1152]{2,1,0:T(8,128)(2,1)} %bitcast.190), calls=%async_computation.16 | async-start | bytes 7077888 | tf_op jit(solution)/shard_map/all_to_all | solution.py:560
  783.4 80.9 %reduce-scatter.44.cloned.1.call-start = ((), (), s32[]{:S(2)}) async-start(), calls=%async_computation.36 | async-start | bytes 1769472 | tf_op jit(solution)/shard_map/reduce_scatter | solution.py:583
  792.2 201.9 %all-reduce.7.cloned.1.call-start = ((), (), s32[]{:S(2)}) async-start(), calls=%async_computation.32 | async-start | bytes 344064 | tf_op jit(solution)/shard_map/psum | solution.py:550
  824.6 210.9 %all-gather.26.cloned.1.call-start = ((), (), s32[]{:S(2)}) async-start(), calls=%async_computation.37 | async-start | bytes 2949120 | tf_op jit(solution)/shard_map/all_gather | solution.py:586
  864.3 240.5 %all-gather.24.cloned.1.call-start = ((), (), s32[]{:S(2)}) async-start(), calls=%async_computation.34 | async-start | bytes 5944320 | tf_op jit(solution)/shard_map/all_gather | solution.py:571
  (40 other events, 802.9 us)
Sparse Core Ops, SparseCore 0:
  33.6 59.7 all-gather.29
  94.9 13.8 all-gather.31
  110.3 19.1 all-gather.21
  130.9 46.1 all-gather.27
  187.9 14.3 reduce-scatter.19
  204.5 42.8 reduce-scatter.15
  250.2 22.8 reduce-scatter.21
  276.2 26.0 reduce-scatter.17
  316.6 44.9 all-gather.33
  372.5 14.4 reduce-scatter.27
  389.2 42.8 reduce-scatter.23
  434.9 22.8 reduce-scatter.29
  460.7 26.0 reduce-scatter.25
  502.0 50.6 all-gather.35
  566.3 42.8 reduce-scatter.31
  612.2 25.0 reduce-scatter.33
  653.7 50.6 all-gather.37
  718.1 42.8 reduce-scatter.35
  763.8 14.5 reduce-scatter.39
  781.2 11.0 reduce-scatter.41
  795.1 27.2 reduce-scatter.37
  824.7 39.6 reduce-scatter.43
  871.4 122.7 all-reduce.6
  996.0 39.4 all-gather.25
  1038.1 66.6 all-gather.23

commit v2 on v1

--- a/solution.py
+++ b/solution.py
@@ -16,6 +16,9 @@
 XBC = 3328
 SHARED = 2 * STATE
 LANES = 128
+GAIN_END = 1536
+DT_AT = 1536
+RATE_AT = DT_AT + LANES
 NORM_EPS = 1e-05
 HIGHEST = lax.Precision.HIGHEST
 BF16 = jnp.bfloat16
@@ -95,16 +98,55 @@
     return (lanes < HEADDIM) if h % 2 == 0 else (lanes >= HEADDIM)
 
 
-def forward_kernel(
-    heads, u_ref, gain_ref, w_ref, ch_ref, bc_ref, dtp_ref, wo_ref,
-    out_ref, ss_ref, normed_ref, gate_ref, xraw_ref, bcraw_ref, dtraw_ref, mixed_ref,
-):
-    length = u_ref.shape[1]
-    wide = ch_ref.shape[1]
+def split_three(value):
+    lanes = lax.broadcasted_iota(jnp.int32, (value.shape[0], LANES), 1)
+    result = jnp.zeros((value.shape[0], LANES), F32)
+    for k in range(3):
+        part = value.astype(BF16).astype(F32)
+        result = jnp.where(lanes == k, part, result)
+        value = value - part
+    return result.astype(BF16)
+
+
+def selection(ids_ref):
+    rows = lax.broadcasted_iota(jnp.int32, (LANES, LANES), 0)
+    columns = lax.broadcasted_iota(jnp.int32, (LANES, LANES), 1)
+    target = jnp.full((LANES, LANES), -1, jnp.int32)
+    for i in range(3):
+        here = (columns >= 2 * i) & (columns < 2 * i + 2)
+        target = jnp.where(here, columns + 2 * (ids_ref[i] - i), target)
+    return (rows == target).astype(F32)
+
+
+def pair_lanes(ids_ref, i):
+    return pl.ds(pl.multiple_of(ids_ref[i] * LANES, LANES), LANES)
+
+
+def load_params(refs):
+    if len(refs) == 2:
+        ids_ref, pack_ref = refs
+        sel = selection(ids_ref)
+        ch = jnp.concatenate([pack_ref[:, pair_lanes(ids_ref, i)] for i in range(3)], axis=1)
+        rows = [pack_ref[7:8, at : at + LANES] for at in (DT_AT, RATE_AT)]
+        dtp = dot(stacked(rows, 8), sel, precision=HIGHEST)
+        return pack_ref[7:8, :GAIN_END], ch, pack_ref[:, INNER:XBC], dtp, sel.astype(BF16)
+    gain_ref, ch_ref, bc_ref, dtp_ref = refs
+    return gain_ref[...], ch_ref[...], bc_ref[...], dtp_ref[...], None
+
+
+def forward_kernel(heads, n_params, with_grad, *refs):
+    u_ref, w_ref, wo_ref, *refs = refs
+    gain, ch, bc, dtp, sel = load_params(refs[:n_params])
+    refs = refs[n_params:]
+    if with_grad:
+        h_ref, *refs = refs
+    out_ref, sums_ref, normed_ref, gate_ref, xraw_ref, bcraw_ref, dtraw_ref, mixed_ref = refs
+    length, width = u_ref.shape[1:]
+    wide = ch.shape[1]
     blocks = length // SPAN
     rows = u_ref[0].astype(F32)
     scale = lax.rsqrt(jnp.mean(rows * rows, axis=-1, keepdims=True) + NORM_EPS)
-    normed = (rows * scale * gain_ref[...]).astype(BF16)
+    normed = (rows * scale * gain).astype(BF16)
     normed_ref[0] = normed
     gate = dot(normed, w_ref[:, :wide])
     gate_ref[0] = gate
@@ -112,13 +154,16 @@
     xraw_ref[0] = x_raw
     rest = dot(normed, w_ref[:, 2 * wide :]).astype(BF16)
     bcraw_ref[0] = rest[:, :SHARED]
-    dtraw_ref[0] = rest[:, SHARED:]
-    conv_x = conv_sum(x_raw.astype(F32), ch_ref[...])
+    dt_raw = rest[:, SHARED:]
+    if sel is not None:
+        dt_raw = dot(dt_raw, sel).astype(BF16)
+    dtraw_ref[0] = dt_raw
+    conv_x = conv_sum(x_raw.astype(F32), ch)
     act_x = (conv_x * sigmoid(conv_x)).astype(BF16)
-    conv_bc = conv_sum(rest[:, :SHARED].astype(F32), bc_ref[...])
+    conv_bc = conv_sum(rest[:, :SHARED].astype(F32), bc)
     act_bc = (conv_bc * sigmoid(conv_bc)).astype(BF16)
-    step, _ = step_sizes(rest[:, SHARED:].astype(F32), dtp_ref[0:1])
-    rate = jnp.exp(dtp_ref[1:2])
+    step, _ = step_sizes(dt_raw.astype(F32), dtp[0:1])
+    rate = jnp.exp(dtp[1:2])
     causal = triangles()
     ones = causal.astype(F32)
     lower = low_half()
@@ -153,30 +198,57 @@
             if len(parts) == 1:
                 parts.append(jnp.zeros_like(parts[0]))
             within = jnp.where(lower, parts[0], parts[1])
-            mixed = within + ch_ref[5:6, lanes] * x_pair.astype(F32)
+            mixed = within + ch[5:6, lanes] * x_pair.astype(F32)
             mixed_ref[0, span, lanes] = mixed.astype(BF16)
     gated = mixed_ref[0].astype(F32) * (gate * sigmoid(gate))
-    ss_ref[0] = jnp.broadcast_to(jnp.sum(gated * gated, axis=-1, keepdims=True), ss_ref.shape[1:])
-    out_ref[0] = dot((gated * ch_ref[6:7]).astype(BF16), wo_ref[...]).astype(BF16)
-
-
-def backward_kernel(
-    heads, h_ref, aux_ref, gate_ref, xraw_ref, bcraw_ref, dtraw_ref, mixed_ref,
-    w_ref, ch_ref, bc_ref, dtp_ref, wo_ref,
-    dn_ref, pg_ref, no_ref, gch_ref, gbc_ref, gdt_ref,
-    dmix_s, dx_s, dbc_s, ddt_s,
-):
-    length = h_ref.shape[1]
-    wide = ch_ref.shape[1]
+    square = jnp.sum(gated * gated, axis=-1, keepdims=True)
+    scaled = gated * ch[6:7]
+    out_ref[0, :, :width] = dot(scaled.astype(BF16), wo_ref[...]).astype(BF16)
+    if sel is None:
+        sums_ref[0] = jnp.broadcast_to(square, sums_ref.shape[1:])
+        return
+    out_ref[0, :, width:] = split_three(square)
+    if with_grad:
+        grad_no = dot_nt(h_ref[0], wo_ref[...])
+        cross = jnp.sum(grad_no * scaled, axis=-1, keepdims=True)
+        lane_ids = lax.broadcasted_iota(jnp.int32, (length, LANES), 1)
+        both = jnp.where(lane_ids == 0, square, jnp.where(lane_ids == 1, cross, 0.0))
+        sums_ref[0] = both.T[:8]
+    else:
+        sums_ref[0] = jnp.zeros(sums_ref.shape[1:], F32)
+
+
+def backward_kernel(heads, n_params, aux_kind, *refs):
+    h_ref, *refs = refs
+    if aux_kind != "columns":
+        aux_ref, *refs = refs
+    gate_ref, xraw_ref, bcraw_ref, dtraw_ref, mixed_ref, w_ref, wo_ref, *refs = refs
+    _, ch, bc, dtp, sel = load_params(refs[:n_params])
+    param_refs, refs = refs[:n_params], refs[n_params:]
+    dn_ref, pg_ref, no_ref, *sum_refs = refs[:-4]
+    dmix_s, dx_s, dbc_s, ddt_s = refs[-4:]
+    length, width = dn_ref.shape[1:]
+    wide = ch.shape[1]
     blocks = length // SPAN
-    scale, rdot = aux_ref[0, :, 0:1], aux_ref[0, :, 1:2]
+    h_rows = h_ref[0, :, :width]
+    if aux_kind == "columns":
+        aux = h_ref[0, :, width:].astype(F32)
+        scale = aux[:, 0:1] + aux[:, 1:2] + aux[:, 2:3]
+        rdot = aux[:, 3:4] + aux[:, 4:5] + aux[:, 5:6]
+    elif aux_kind == "rows":
+        sums = aux_ref[0]
+        aux = jnp.concatenate([sums, jnp.zeros((LANES - 8, length), F32)], axis=0).T
+        scale = lax.rsqrt(aux[:, 0:1] * (1.0 / INNER) + NORM_EPS)
+        rdot = aux[:, 1:2] * scale
+    else:
+        scale, rdot = aux_ref[0, :, 0:1], aux_ref[0, :, 1:2]
     gate = gate_ref[0]
     mixed = mixed_ref[0].astype(F32)
     sig = sigmoid(gate)
     silu = gate * sig
     gated = mixed * silu
-    gain = ch_ref[6:7]
-    grad_no = dot_nt(h_ref[0], wo_ref[...])
+    gain = ch[6:7]
+    grad_no = dot_nt(h_rows, wo_ref[...])
     grad_g = scale * (gain * grad_no) - gated * (scale * scale * (1.0 / INNER) * rdot)
     scaled = gated * scale
     no_ref[0] = (scaled * gain).astype(BF16)
@@ -186,14 +258,14 @@
 
     x_raw = xraw_ref[0].astype(F32)
     bc_raw = bcraw_ref[0].astype(F32)
-    conv_x = conv_sum(x_raw, ch_ref[...])
+    conv_x = conv_sum(x_raw, ch)
     sig_x = sigmoid(conv_x)
     act_x = (conv_x * sig_x).astype(BF16)
-    conv_bc = conv_sum(bc_raw, bc_ref[...])
+    conv_bc = conv_sum(bc_raw, bc)
     sig_bc = sigmoid(conv_bc)
     act_bc = (conv_bc * sig_bc).astype(BF16)
-    step, slope = step_sizes(dtraw_ref[0].astype(F32), dtp_ref[0:1])
-    rate = jnp.exp(dtp_ref[1:2])
+    step, slope = step_sizes(dtraw_ref[0].astype(F32), dtp[0:1])
+    rate = jnp.exp(dtp[1:2])
     causal = triangles()
     ones = causal.astype(F32)
     lower = low_half()
@@ -281,7 +353,7 @@
             if len(parts) == 1:
                 parts.append(jnp.zeros_like(parts[0]))
             grad_x = jnp.where(lower, parts[0], parts[1])
-            dx_s[span, lanes] = grad_x + ch_ref[5:6, lanes] * grad_pair.astype(F32)
+            dx_s[span, lanes] = grad_x + ch[5:6, lanes] * grad_pair.astype(F32)
         col_sums = stacked(col_rows, LANES).T
         low_scores = grad_scores.astype(BF16)
         dbc_s[span, :STATE] = grad_b + dot_tn(low_scores, c_out)
@@ -294,32 +366,52 @@
 
     skip_row = jnp.sum(dmix_s[...].astype(F32) * act_x.astype(F32), axis=0, keepdims=True)
     grad_conv = dx_s[...] * (sig_x * (1.0 + conv_x * (1.0 - sig_x)))
-    grad_raw, ch_rows = conv_back(grad_conv, x_raw, ch_ref[...])
+    grad_raw, ch_rows = conv_back(grad_conv, x_raw, ch)
     pg_ref[0, :, wide : 2 * wide] = grad_raw.astype(BF16)
     grad_conv = dbc_s[...] * (sig_bc * (1.0 + conv_bc * (1.0 - sig_bc)))
-    grad_raw, bc_rows = conv_back(grad_conv, bc_raw, bc_ref[...])
+    grad_raw, bc_rows = conv_back(grad_conv, bc_raw, bc)
     pg_ref[0, :, 2 * wide : 2 * wide + SHARED] = grad_raw.astype(BF16)
     grad_dt = ddt_s[...] * slope
-    pg_ref[0, :, 2 * wide + SHARED :] = grad_dt.astype(BF16)
+    low_dt = grad_dt.astype(BF16)
+    if sel is not None:
+        low_dt = dot_nt(low_dt, sel).astype(BF16)
+    pg_ref[0, :, 2 * wide + SHARED :] = low_dt
     dn_ref[0] = dot_nt(pg_ref[0], w_ref[...]).astype(BF16)
-    grads = (
-        (gch_ref, ch_rows + [skip_row, gain_row]),
-        (gbc_ref, bc_rows),
-        (gdt_ref, [jnp.sum(grad_dt, axis=0, keepdims=True), rate_row * rate]),
-    )
-    for ref, rows in grads:
-        value = stacked(rows, 8)
-
-        @pl.when(pl.program_id(0) == 0)
+    by_channel = stacked(ch_rows + [skip_row, gain_row], 8)
+    by_shared = stacked(bc_rows, 8)
+    by_head = stacked([jnp.sum(grad_dt, axis=0, keepdims=True), rate_row * rate], 8)
+    first = pl.program_id(0) == 0
+    if sel is not None:
+        by_head = lax.dot_general(
+            by_head, sel.astype(F32), (((1,), (1,)), ((), ())),
+            preferred_element_type=F32, precision=HIGHEST,
+        )
+        ids_ref, (sum_ref,) = param_refs[0], sum_refs
+
+        @pl.when(first)
+        def _():
+            sum_ref[...] = jnp.zeros_like(sum_ref)
+
+        for i in range(3):
+            sum_ref[:, pair_lanes(ids_ref, i)] += by_channel[:, i * LANES : (i + 1) * LANES]
+        sum_ref[:, INNER:XBC] += by_shared
+        sum_ref[7:8, DT_AT : DT_AT + LANES] += by_head[0:1]
+        sum_ref[7:8, RATE_AT : RATE_AT + LANES] += by_head[1:2]
+        return
+    for ref, value in zip(sum_refs, (by_channel, by_shared, by_head)):
+
+        @pl.when(first)
         def _(ref=ref, value=value):
             ref[...] = value
 
-        @pl.when(pl.program_id(0) > 0)
+        @pl.when(jnp.logical_not(first))
         def _(ref=ref, value=value):
             ref[...] += value
 
 
 def whole_spec(array):
+    if array.dtype == jnp.int32:
+        return pl.BlockSpec(memory_space=pltpu.SMEM)
     return pl.BlockSpec(array.shape, lambda i: (0,) * array.ndim)
 
 
@@ -327,42 +419,52 @@
     return pl.BlockSpec((1, length, width), lambda i: (i, 0, 0))
 
 
+def block_spec(array):
+    return pl.BlockSpec((1,) + array.shape[1:], lambda i: (i, 0, 0))
+
+
 PARAMS = dict(vmem_limit_bytes=60 * 1024 * 1024)
 
 
-def run_forward(heads, rows, layer):
+def run_forward(heads, wide, rows, w, wo, params, grad_rows=None):
     count, length, width = rows.shape
-    wide = layer["ch"].shape[1]
-    constants = [layer[k] for k in ("gain", "w", "ch", "bc", "dtp", "wo")]
+    compact = len(params) == 2
+    constants = [w, wo, *params]
+    given = [] if grad_rows is None else [grad_rows]
     outs = [
-        (width, BF16), (LANES, F32), (width, BF16), (wide, F32),
-        (wide, BF16), (SHARED, BF16), (LANES, BF16), (wide, BF16),
+        (length, width + LANES if compact else width, BF16),
+        (8, length, F32) if compact else (length, LANES, F32),
+        (length, width, BF16), (length, wide, F32),
+        (length, wide, BF16), (length, SHARED, BF16), (length, LANES, BF16), (length, wide, BF16),
     ]
     return pl.pallas_call(
-        partial(forward_kernel, heads),
+        partial(forward_kernel, heads, len(params), grad_rows is not None),
         grid=(count,),
-        out_shape=[jax.ShapeDtypeStruct((count, length, n), t) for n, t in outs],
-        in_specs=[row_spec(length, width)] + [whole_spec(c) for c in constants],
-        out_specs=[row_spec(length, n) for n, _ in outs],
+        out_shape=[jax.ShapeDtypeStruct((count, r, n), t) for r, n, t in outs],
+        in_specs=[block_spec(rows)]
+        + [whole_spec(c) for c in constants]
+        + [block_spec(g) for g in given],
+        out_specs=[row_spec(r, n) for r, n, _ in outs],
         compiler_params=pltpu.CompilerParams(**PARAMS),
         name="forward",
-    )(rows, *constants)
-
-
-def run_backward(heads, grad_rows, aux, saved, layer):
-    count, length, width = grad_rows.shape
-    wide = layer["ch"].shape[1]
-    columns = layer["w"].shape[1]
-    given = [grad_rows, aux, *saved]
-    constants = [layer[k] for k in ("w", "ch", "bc", "dtp", "wo")]
+    )(rows, *constants, *given)
+
+
+def run_backward(heads, wide, grad_rows, aux, aux_kind, saved, w, wo, params):
+    count, length, _ = grad_rows.shape
+    width, columns = w.shape
+    given = [grad_rows] + ([] if aux is None else [aux]) + list(saved)
+    constants = [w, wo, *params]
     outs = [(width, BF16), (columns, BF16), (wide, BF16)]
     sums = [(8, wide), (8, SHARED), (8, LANES)]
+    if len(params) == 2:
+        sums = [params[1].shape]
     return pl.pallas_call(
-        partial(backward_kernel, heads),
+        partial(backward_kernel, heads, len(params), aux_kind),
         grid=(count,),
         out_shape=[jax.ShapeDtypeStruct((count, length, n), t) for n, t in outs]
         + [jax.ShapeDtypeStruct(s, F32) for s in sums],
-        in_specs=[row_spec(length, g.shape[2]) for g in given] + [whole_spec(c) for c in constants],
+        in_specs=[block_spec(g) for g in given] + [whole_spec(c) for c in constants],
         out_specs=[row_spec(length, n) for n, _ in outs]
         + [pl.BlockSpec(s, lambda i: (0, 0)) for s in sums],
         scratch_shapes=[
@@ -413,6 +515,851 @@
     pads = [(0, 0)] * array.ndim
     pads[axis] = (0, size - array.shape[axis])
     return jnp.pad(array, pads)
+
+
+MESH = pl.DeviceIdType.MESH
+ANY = pl.BlockSpec(memory_space=pl.ANY)
+VMEM = pl.BlockSpec(memory_space=pltpu.VMEM)
+DMA = pltpu.SemaphoreType.DMA
+
+
+class Spot:
+    def __init__(self):
+        self.s, self.q, self.z = (lax.axis_index(a) for a in ("section", "seq", "fsdp"))
+        self.half, self.lo = self.z // 2, self.z % 2
+        self.mate, self.twin = self.z + 1 - 2 * self.lo, (self.z + 2) % 4
+        self.around = [None, self.q + 1 - 2 * (self.q % 2), (self.q + 2) % 4, 3 - self.q]
+        self.sibling = (1 - self.s, self.q, self.z)
+        self.at_mate, self.at_twin = (self.s, self.q, self.mate), (self.s, self.q, self.twin)
+
+    def plane(self, k):
+        return (self.s, self.around[k], self.z)
+
+    def column(self, z):
+        return (self.s, self.q, z)
+
+    def pair(self, half, i):
+        odd, third = self.q % 2, self.q // 2 * 3
+        return 12 * half + third + [2 * odd, 1 + 6 * odd, 6 + 2 * odd][i]
+
+
+def greet(places):
+    barrier = pltpu.get_barrier_semaphore()
+    for place in places:
+        pl.semaphore_signal(barrier, inc=1, device_id=place, device_id_type=MESH)
+    pl.semaphore_wait(barrier, len(places))
+
+
+def remote(src, dst, send_sem, recv_sem, place):
+    return pltpu.make_async_remote_copy(
+        src_ref=src, dst_ref=dst, send_sem=send_sem, recv_sem=recv_sem, device_id=place, device_id_type=MESH
+    )
+
+
+class Spread:
+    SEMS = [DMA((7,)), DMA((7,)), DMA]
+
+    def __init__(self, spot, own, all_rows, sems):
+        self.spot, self.own, self.all = spot, own, all_rows
+        self.send, self.recv, self.local = sems
+
+    def copy(self, j):
+        spot = self.spot
+        slot = self.all.at[spot.half, spot.q]
+        if j == 3:
+            return remote(self.own, slot, self.send.at[3], self.recv.at[3], spot.at_twin)
+        if j < 3:
+            return remote(self.own, slot, self.send.at[j], self.recv.at[j], spot.plane(j + 1))
+        slot = self.all.at[1 - spot.half, spot.q]
+        return remote(slot, slot, self.send.at[j], self.recv.at[j], spot.plane(j - 3))
+
+    def here(self):
+        return pltpu.make_async_copy(self.own, self.all.at[self.spot.half, self.spot.q], self.local)
+
+    def start(self):
+        for j in (3, 0, 1, 2):
+            self.copy(j).start()
+        self.here().start()
+
+    def forward(self):
+        self.copy(3).wait_recv()
+        for j in (4, 5, 6):
+            self.copy(j).start()
+
+    def finish(self):
+        for j in (0, 1, 2, 4, 5, 6):
+            self.copy(j).wait_recv()
+        for j in range(7):
+            self.copy(j).wait_send()
+        self.here().wait()
+
+
+class Sum:
+    @staticmethod
+    def scratch(rows, columns):
+        return [
+            pltpu.VMEM((3, 2, rows, columns), BF16),
+            pltpu.VMEM((2, rows, columns), BF16),
+            pltpu.VMEM((2, rows, columns), BF16),
+            DMA((7,)),
+            DMA((7,)),
+            DMA((2,)),
+        ]
+
+    def __init__(self, spot, parts, width, scratch):
+        self.spot, self.parts, self.width = spot, parts, width
+        self.recv_rows, self.own, self.twin_rows, self.send, self.recv, self.local = scratch
+
+    def copy(self, k, i):
+        spot = self.spot
+        half = (1 - spot.half) if i == 0 else spot.half
+        j = 3 * i + k - 1
+        return remote(
+            self.parts.at[half, spot.around[k]], self.recv_rows.at[k - 1, i],
+            self.send.at[j], self.recv.at[j], spot.plane(k),
+        )
+
+    def here(self, i):
+        half = (1 - self.spot.half) if i == 0 else self.spot.half
+        return pltpu.make_async_copy(
+            self.parts.at[half, self.spot.q], self.own.at[i], self.local.at[i]
+        )
+
+    def across(self):
+        return remote(
+            self.twin_rows.at[0], self.twin_rows.at[1], self.send.at[6], self.recv.at[6], self.spot.at_twin
+        )
+
+    def start(self):
+        for i in range(2):
+            for k in (1, 2, 3):
+                self.copy(k, i).start()
+            self.here(i).start()
+
+    def plane_total(self, i):
+        self.here(i).wait()
+        total = self.own[i].astype(F32)
+        for k in (1, 2, 3):
+            self.copy(k, i).wait_recv()
+            total += self.recv_rows[k - 1, i].astype(F32)
+        return total
+
+    def forward(self):
+        total = self.plane_total(0)
+        width = self.width
+        self.twin_rows[0, :, :width] = total[:, :width].astype(BF16)
+        if total.shape[1] > width:
+            column = jnp.sum(total[:, width:], axis=1, keepdims=True)
+            self.twin_rows[0, :, width:] = split_three(column)
+        self.across().start()
+
+    def finish(self):
+        total = self.plane_total(1)
+        self.across().wait_recv()
+        total += self.twin_rows[1].astype(F32)
+        return total
+
+    def close(self):
+        for i in range(2):
+            for k in (1, 2, 3):
+                self.copy(k, i).wait_send()
+        self.across().wait_send()
+
+
+class Weights:
+    LOCAL = 20
+
+    @staticmethod
+    def scratch(rows, columns):
+        return [pltpu.VMEM((rows, columns), BF16), DMA((Weights.LOCAL,)), DMA((24,)), DMA((24,))]
+
+    def __init__(self, spot, layer, w_in, dt_in, w_out, tile, tile_out, scratch):
+        self.spot, self.layer = spot, layer
+        self.w_in, self.dt_in, self.w_out, self.tile, self.tile_out = w_in, dt_in, w_out, tile, tile_out
+        self.stage, self.local, self.send, self.recv = scratch
+        self.rows = w_in.shape[0]
+        self.others = 2 * (1 - spot.half)
+        self.gateway = 2 - spot.half
+        self.is_gateway = (spot.z == 1) | (spot.z == 2)
+
+    def at_source(self, step):
+        pl.when(self.spot.s == self.layer)(step)
+
+    def block(self, z):
+        return self.tile.at[pl.ds(z * self.rows, self.rows)]
+
+    def staged(self, own):
+        spot = self.spot
+        half = spot.half if own else 1 - spot.half
+        target = self.block(spot.z) if own else self.stage
+        jobs = []
+        for i in range(3):
+            for part in range(2):
+                at = part * INNER + LANES * spot.pair(half, i)
+                source = self.w_in.at[:, pl.ds(pl.multiple_of(at, LANES), LANES)]
+                jobs.append((source, target.at[:, pl.ds((3 * part + i) * LANES, LANES)]))
+        jobs.append((self.w_in.at[:, pl.ds(2 * INNER, SHARED)], target.at[:, pl.ds(6 * LANES, SHARED)]))
+        jobs.append((self.dt_in, target.at[:, pl.ds(6 * LANES + SHARED, LANES)]))
+        first = 0 if own else len(jobs)
+        return [
+            pltpu.make_async_copy(a, b, self.local.at[first + n]) for n, (a, b) in enumerate(jobs)
+        ]
+
+    def out_rows(self, i):
+        at = (self.spot.pair(self.spot.half, i) % 6) * LANES
+        source = self.w_out.at[pl.ds(pl.multiple_of(at, LANES), LANES)]
+        return source, self.tile_out.at[pl.ds(i * LANES, LANES)]
+
+    def owns(self, i):
+        return self.spot.lo == [0, self.spot.q % 2, 1][i]
+
+    def out_local(self, i):
+        return pltpu.make_async_copy(*self.out_rows(i), self.local.at[16 + i])
+
+    def out_to(self, i, sibling, from_tile=False):
+        source, target = self.out_rows(i)
+        j = 8 + 3 * sibling + i
+        place = self.spot.sibling if sibling else self.spot.at_mate
+        return remote(target if from_tile else source, target, self.send.at[j], self.recv.at[j], place)
+
+    def own_to_mate(self):
+        block = self.block(self.spot.z)
+        return remote(block, block, self.send.at[0], self.recv.at[0], self.spot.at_mate)
+
+    def stage_to_gateway(self):
+        j = 1 + self.spot.lo
+        place = self.spot.column(self.gateway)
+        return remote(self.stage, self.block(self.spot.z), self.send.at[1], self.recv.at[j], place)
+
+    def passed(self, n):
+        block = self.block(self.others + n)
+        return remote(block, block, self.send.at[2 + n], self.recv.at[1 + n], self.spot.at_mate)
+
+    def to_sibling(self, n):
+        z = [self.spot.z, self.spot.mate, self.others, self.others + 1][n]
+        block = self.block(z)
+        return remote(block, block, self.send.at[4 + n], self.recv.at[4 + n], self.spot.sibling)
+
+    def begin(self):
+        @self.at_source
+        def _():
+            for copy in self.staged(True) + self.staged(False):
+                copy.start()
+            for i in range(3):
+                pl.when(self.owns(i))(lambda i=i: self.out_local(i).start())
+
+    def start(self):
+        @self.at_source
+        def _():
+            for copy in self.staged(True):
+                copy.wait()
+            self.own_to_mate().start()
+            self.to_sibling(0).start()
+            for copy in self.staged(False):
+                copy.wait()
+            self.stage_to_gateway().start()
+            for i in range(3):
+
+                @pl.when(self.owns(i))
+                def _(i=i):
+                    self.out_to(i, 0).start()
+                    self.out_to(i, 1).start()
+
+    def relay_mate(self):
+        @self.at_source
+        def _():
+            self.own_to_mate().wait_recv()
+            self.to_sibling(1).start()
+
+    def relay_others(self):
+        @self.at_source
+        def _():
+            for n in range(2):
+                self.passed(n).wait_recv()
+                pl.when(self.is_gateway)(lambda n=n: self.passed(n).start())
+                self.to_sibling(2 + n).start()
+            for i in range(3):
+
+                @pl.when(jnp.logical_not(self.owns(i)))
+                def _(i=i):
+                    self.out_to(i, 0).wait_recv()
+                    self.out_to(i, 1, True).start()
+
+    def finish(self):
+        @self.at_source
+        def _():
+            self.own_to_mate().wait_send()
+            self.stage_to_gateway().wait_send()
+            for n in range(2):
+                pl.when(self.is_gateway)(lambda n=n: self.passed(n).wait_send())
+            for n in range(4):
+                self.to_sibling(n).wait_send()
+            for i in range(3):
+                self.out_to(i, 1).wait_send()
+
+                @pl.when(self.owns(i))
+                def _(i=i):
+                    self.out_to(i, 0).wait_send()
+                    self.out_local(i).wait()
+
+        @pl.when(self.spot.s != self.layer)
+        def _():
+            for n in range(4):
+                self.to_sibling(n).wait_recv()
+            for i in range(3):
+                self.out_to(i, 1).wait_recv()
+
+
+def take(refs, counts):
+    refs = list(refs)
+    return [[refs.pop(0) for _ in range(n)] for n in counts]
+
+
+def all_places(spot):
+    places = [spot.plane(k) for k in (1, 2, 3)]
+    places += [spot.column((spot.z + k) % 4) for k in (1, 2, 3)]
+    return places + [spot.sibling]
+
+
+def open_kernel(*refs):
+    ins, outs, weight_s, spread_a, spread_b, (pack_send, pack_recv, pack_local) = take(
+        refs, (6, 5, 4, 3, 3, 3)
+    )
+    w_in, dt_in, w_out, pack, tokens, cotangent = ins
+    tile, tile_out, packs, all_tokens, all_cot = outs
+    spot = Spot()
+    weights = Weights(spot, 0, w_in, dt_in, w_out, tile, tile_out, weight_s)
+    rows = Spread(spot, tokens.at[spot.s], all_tokens, spread_a)
+    grads = Spread(spot, cotangent.at[spot.s], all_cot, spread_b)
+    pack_here = pltpu.make_async_copy(pack, packs.at[spot.s], pack_local)
+    pack_there = remote(pack, packs.at[spot.s], pack_send, pack_recv, spot.sibling)
+    weights.begin()
+    greet(all_places(spot))
+    rows.start()
+    pack_here.start()
+    pack_there.start()
+    weights.start()
+    rows.forward()
+    weights.relay_mate()
+    grads.start()
+    weights.relay_others()
+    grads.forward()
+    rows.finish()
+    grads.finish()
+    weights.finish()
+    pack_here.wait()
+    pack_there.wait()
+
+
+def middle_kernel(*refs):
+    ins, outs, weight_s, sum_s, spread_s = take(refs, (5, 6, 4, 6, 3))
+    w_in, dt_in, w_out, parts, rows_in = ins
+    tile, tile_out, all_rows, branch, scales, rows_out = outs
+    spot = Spot()
+    weights = Weights(spot, 1, w_in, dt_in, w_out, tile, tile_out, weight_s)
+    total = Sum(spot, parts, rows_in.shape[1], sum_s)
+    spread = Spread(spot, rows_out, all_rows, spread_s)
+    weights.begin()
+    greet(all_places(spot))
+    total.start()
+    weights.start()
+    total.forward()
+    layer_rows(total.finish(), rows_in, branch, scales, rows_out)
+    spread.start()
+    weights.relay_mate()
+    spread.forward()
+    weights.relay_others()
+    spread.finish()
+    total.close()
+    weights.finish()
+
+
+def layer_rows(total, rows_in, branch, scales, rows_out):
+    width = rows_in.shape[1]
+    square = jnp.sum(total[:, width:], axis=1, keepdims=True)
+    scale = lax.rsqrt(square * (1.0 / INNER) + NORM_EPS)
+    part = total[:, :width] * scale
+    rows_out[...] = (rows_in[...].astype(F32) + part).astype(BF16)
+    if branch is not None:
+        branch[...] = part
+        scales[...] = jnp.broadcast_to(scale, scales.shape)
+
+
+def sums_kernel(mine_ref, total_ref, others, send, recv):
+    spot = Spot()
+    places = [spot.plane(k) for k in (1, 2, 3)]
+    places += [(spot.s, spot.around[k], spot.twin) for k in (1, 2, 3)] + [spot.at_twin]
+    greet(places)
+    copies = [
+        remote(mine_ref, others.at[j], send.at[j], recv.at[j], place) for j, place in enumerate(places)
+    ]
+    for copy in copies:
+        copy.start()
+    total = mine_ref[...]
+    for j, copy in enumerate(copies):
+        copy.wait_recv()
+        total += others[j]
+    total_ref[...] = total
+    for copy in copies:
+        copy.wait_send()
+
+
+def norm_back(total, rows_in, gain, grad_out):
+    rows = rows_in[...].astype(F32)
+    scale = lax.rsqrt(jnp.mean(rows * rows, axis=-1, keepdims=True) + NORM_EPS)
+    scaled = rows * scale
+    pulled = total * gain
+    inner = jnp.mean(pulled * scaled, axis=-1, keepdims=True)
+    grad = scale * (pulled - scaled * inner) + grad_out[...].astype(F32)
+    return grad, jnp.sum(total * scaled, axis=0, keepdims=True)
+
+
+def turn_kernel(*refs):
+    ins, outs, sum_s, last_s, spread_s, (payload,) = take(refs, (8, 4, 6, 6, 3, 1))
+    parts, last_parts, rows_in, grad_out, packs, branch, scales, last_in = ins
+    all_rows, grad_rows, grad_gain, last_rows = outs
+    spot = Spot()
+    width = rows_in.shape[1]
+    total = Sum(spot, parts, width, sum_s)
+    last = Sum(spot, last_parts, width, last_s)
+    spread = Spread(spot, payload, all_rows, spread_s)
+    greet([spot.plane(k) for k in (1, 2, 3)] + [spot.at_twin])
+    total.start()
+    total.forward()
+    grad, gain_row = norm_back(total.finish(), rows_in, packs[1, 7:8, :width], grad_out)
+    low = grad.astype(BF16)
+    grad_rows[...] = low
+    grad_gain[...] = stacked([gain_row], 8)
+    cross = jnp.sum(low.astype(F32) * branch[...], axis=1, keepdims=True)
+    payload[:, :width] = low
+    lanes = lax.broadcasted_iota(jnp.int32, (rows_in.shape[0], LANES), 1)
+    first = split_three(scales[:, 0:1]).astype(F32)
+    second = pltpu.roll(split_three(cross).astype(F32), 3, 1)
+    payload[:, width:] = jnp.where(lanes < 3, first, second).astype(BF16)
+    spread.start()
+    last.start()
+    spread.forward()
+    last.forward()
+    spread.finish()
+    layer_rows(last.finish(), last_in, None, None, last_rows)
+    total.close()
+    last.close()
+
+
+def add_rows(target, sources, chunk=64):
+    @pl.loop(0, target.shape[0] // chunk)
+    def _(n):
+        rows = pl.ds(pl.multiple_of(n * chunk, chunk), chunk)
+        total = sources[0][rows, :].astype(F32)
+        for source in sources[1:]:
+            total += source[rows, :].astype(F32)
+        target[rows, :] = total.astype(target.dtype)
+
+
+class Grads:
+    @staticmethod
+    def scratch(shard, columns, wide, width):
+        half = columns - SHARED - LANES
+        return [
+            pltpu.VMEM((2, 4 * shard, columns), BF16),
+            pltpu.VMEM((2, wide, width), BF16),
+            pltpu.VMEM((3, shard, columns), BF16),
+            pltpu.VMEM((wide, width), BF16),
+            pltpu.VMEM((2, shard, half), BF16),
+            pltpu.VMEM((4, shard, columns - half), BF16),
+            pltpu.VMEM((shard, columns - half), BF16),
+            pltpu.VMEM((6, 8, XBC), F32),
+            DMA((4,)),
+            DMA((68,)),
+            DMA((68,)),
+        ]
+
+    def __init__(self, spot, w_grads, wo_grads, final, final_out, scratch):
+        self.spot, self.w_grads, self.wo_grads = spot, w_grads, wo_grads
+        self.final, self.final_out = final, final_out
+        (
+            self.cores, self.cores_out, self.planes, self.mate_out, self.reduced, self.shared,
+            self.shared_sum, self.small, self.local, self.send, self.recv,
+        ) = scratch
+        self.rows = self.planes.shape[1]
+        self.others = 2 * (1 - spot.half)
+
+    def block(self, z):
+        return pl.ds(pl.multiple_of(z * self.rows, self.rows), self.rows)
+
+    def core_copy(self, layer, n):
+        if n == 4:
+            source, target = self.wo_grads[layer], self.cores_out.at[1]
+        else:
+            z = [self.others, self.others + 1, self.spot.mate, self.spot.z][n]
+            source = self.w_grads[layer].at[self.block(z)]
+            target = self.cores.at[1, self.block(z)]
+        return remote(source, target, self.send.at[n], self.recv.at[n], self.spot.sibling)
+
+    def own_copy(self, layer, n):
+        pair = [(self.w_grads[layer], self.cores.at[0]), (self.wo_grads[layer], self.cores_out.at[0])][n]
+        return pltpu.make_async_copy(*pair, self.local.at[n])
+
+    def begin(self):
+        for s in range(2):
+
+            @pl.when(self.spot.s == s)
+            def _(s=s):
+                for n in range(5):
+                    self.core_copy(1 - s, n).start()
+                for n in range(2):
+                    self.own_copy(s, n).start()
+
+    def plane_copy(self, n):
+        spot = self.spot
+        if n == 2:
+            slot, place, j = self.planes.at[2], spot.at_mate, 7
+            source = self.cores.at[0, self.block(spot.mate)]
+        else:
+            slot, place, j = self.planes.at[spot.lo], spot.column(self.others + n), 5 + spot.lo
+            source = self.cores.at[0, self.block(self.others + n)]
+        return remote(source, slot, self.send.at[5 + n], self.recv.at[j], place)
+
+    def came(self, n):
+        slot = self.planes.at[n]
+        return remote(slot, slot, self.send.at[5 + n], self.recv.at[5 + n], self.spot.at_mate)
+
+    def owns(self, i, k=0):
+        odd = self.spot.q % 2
+        if k % 2:
+            odd = 1 - odd
+        return self.spot.lo == [0, odd, 1][i]
+
+    def out_rows(self, i):
+        return pl.ds(i * LANES, LANES)
+
+    def mate_copy(self, i):
+        rows = self.out_rows(i)
+        return remote(
+            self.cores_out.at[0, rows], self.mate_out.at[rows],
+            self.send.at[8 + i], self.recv.at[8 + i], self.spot.at_mate,
+        )
+
+    def to_planes(self):
+        for n in range(2):
+            self.own_copy(0, n).wait()
+        for n, z in enumerate((self.others, self.others + 1, self.spot.mate, self.spot.z)):
+            self.core_copy(0, n).wait_recv()
+            rows = self.block(z)
+            own, sibling = self.cores.at[0, rows], self.cores.at[1, rows]
+            add_rows(own, [own, sibling])
+            if n < 3:
+                self.plane_copy(n).start()
+        self.core_copy(0, 4).wait_recv()
+        add_rows(self.cores_out.at[0], [self.cores_out.at[0], self.cores_out.at[1]])
+        for i in range(3):
+            pl.when(jnp.logical_not(self.owns(i)))(lambda i=i: self.mate_copy(i).start())
+
+    def around_copy(self, k, n):
+        i, part, pair = n // 6, n // 3 % 2, n % 3
+        half = self.spot.half if i == 0 else 1 - self.spot.half
+        at = part * INNER + LANES * self.spot.pair(half, pair)
+        source = self.reduced.at[i, :, pl.ds((3 * part + pair) * LANES, LANES)]
+        target = self.final.at[:, pl.ds(pl.multiple_of(at, LANES), LANES)]
+        if k == 0:
+            return pltpu.make_async_copy(source, target, self.send.at[11 + n])
+        j = 11 + 12 * k + n
+        return remote(source, target, self.send.at[j], self.recv.at[j], self.spot.plane(k))
+
+    def shared_copy(self, k):
+        return remote(
+            self.shared.at[0], self.shared.at[k], self.send.at[58 + k], self.recv.at[58 + k], self.spot.plane(k)
+        )
+
+    def out_target(self, i):
+        at = (self.spot.pair(self.spot.half, i) % 6) * LANES
+        return self.final_out.at[pl.ds(pl.multiple_of(at, LANES), LANES)]
+
+    def out_copy(self, k, i, sems):
+        source = self.cores_out.at[0, self.out_rows(i)]
+        if k == 0:
+            return pltpu.make_async_copy(source, self.out_target(i), sems[0].at[i])
+        j = 3 * k + i
+        return remote(source, self.out_target(i), sems[0].at[j], sems[1].at[j], self.spot.plane(k))
+
+    def around(self, out_sems):
+        half = self.reduced.shape[2]
+        self.came(2).wait_recv()
+        own = self.cores.at[0, self.block(self.spot.z)]
+        add_rows(own, [own, self.planes.at[2]])
+        for n in range(2):
+            self.came(n).wait_recv()
+
+        @pl.loop(0, self.rows // 64)
+        def _(n):
+            rows = pl.ds(pl.multiple_of(n * 64, 64), 64)
+            own = self.cores[0, pl.ds(pl.multiple_of(self.spot.z * self.rows + n * 64, 64), 64), :].astype(F32)
+            other = self.planes[0, rows, :].astype(F32) + self.planes[1, rows, :].astype(F32)
+            self.reduced[0, rows, :] = own[:, :half].astype(BF16)
+            self.reduced[1, rows, :] = other[:, :half].astype(BF16)
+            self.shared[0, rows, :] = (own[:, half:] + other[:, half:]).astype(BF16)
+
+        for k in (1, 2, 3):
+            self.shared_copy(k).start()
+        for n in range(12):
+            for k in (1, 2, 3, 0):
+                self.around_copy(k, n).start()
+        for i in range(3):
+
+            @pl.when(self.owns(i))
+            def _(i=i):
+                rows = self.out_rows(i)
+                self.mate_copy(i).wait_recv()
+                total = self.cores_out[0, rows, :].astype(F32) + self.mate_out[rows, :].astype(F32)
+                self.cores_out[0, rows, :] = total.astype(BF16)
+                for k in (1, 2, 3, 0):
+                    self.out_copy(k, i, out_sems).start()
+
+    def small_copy(self, n):
+        spot = self.spot
+        place = [spot.sibling, spot.at_mate, spot.at_twin, spot.plane(1), spot.plane(2)][n]
+        return remote(
+            self.small.at[0], self.small.at[1 + n], self.send.at[62 + n], self.recv.at[62 + n], place
+        )
+
+    def finish(self, out_sems):
+        for k in (1, 2, 3):
+            self.shared_copy(k).wait_recv()
+
+        @pl.loop(0, self.rows // 64)
+        def _(n):
+            rows = pl.ds(pl.multiple_of(n * 64, 64), 64)
+            a, b, c, d = (self.shared[k, rows, :].astype(F32) for k in range(4))
+            self.shared_sum[rows, :] = ((a + b) + (c + d)).astype(BF16)
+
+        tail = self.final.at[:, pl.ds(2 * INNER, self.shared_sum.shape[1])]
+        copy = pltpu.make_async_copy(self.shared_sum, tail, self.local.at[2])
+        copy.start()
+        for n in range(12):
+            for k in (1, 2, 3):
+                self.around_copy(k, n).wait_recv()
+            self.around_copy(0, n).wait()
+        for k in (1, 2, 3):
+            for i in range(3):
+                pl.when(self.owns(i, k))(lambda k=k, i=i: self.out_copy(k, i, out_sems).wait_recv())
+        copy.wait()
+        for n in range(5):
+            self.core_copy(0, n).wait_send()
+        for n in range(3):
+            self.plane_copy(n).wait_send()
+        for k in (1, 2, 3):
+            self.shared_copy(k).wait_send()
+            for n in range(12):
+                self.around_copy(k, n).wait_send()
+        for i in range(3):
+
+            @pl.when(self.owns(i))
+            def _(i=i):
+                for k in (1, 2, 3):
+                    self.out_copy(k, i, out_sems).wait_send()
+                self.out_copy(0, i, out_sems).wait()
+
+            pl.when(jnp.logical_not(self.owns(i)))(lambda i=i: self.mate_copy(i).wait_send())
+
+
+def close_kernel(*refs):
+    ins, outs, sum_s, grads_s, (grad_rows, small_in, send, recv, local, out_send, out_recv) = take(
+        refs, (14, 5, 6, 11, 7)
+    )
+    parts, rows_in, grad_out, packs, first_rows, last_rows, last_grad, *rest = ins
+    w_grads, wo_grads, (small_0, small_1, gain_1) = rest[:2], rest[2:4], rest[4:]
+    home_rows, home_grads, final, final_out, small_out = outs
+    spot = Spot()
+    width = rows_in.shape[1]
+    total = Sum(spot, parts, width, sum_s)
+    grads = Grads(spot, w_grads, wo_grads, final, final_out, grads_s)
+    out_sems = (out_send, out_recv)
+    greet(all_places(spot))
+    grads.begin()
+    total.start()
+    grads.to_planes()
+    total.forward()
+    grad, gain_row = norm_back(total.finish(), rows_in, packs[0, 7:8, :width], grad_out)
+    grad_rows[...] = grad.astype(BF16)
+    layers = ((first_rows, grad_rows), (last_rows, last_grad))
+
+    def home_copies(s):
+        copies = []
+        for n, target in enumerate((home_rows, home_grads)):
+            copies.append(remote(layers[1 - s][n], target.at[s], send.at[n], recv.at[n], spot.sibling))
+            copies.append(pltpu.make_async_copy(layers[s][n], target.at[s], local.at[n]))
+        return copies
+
+    small_in[0] = small_0[...]
+    small_in[1] = small_1[...]
+    small_in[0, 7:8, :width] = gain_row
+    small_in[1, 7:8, :width] = gain_1[0:1]
+    grads.small[0] = small_in[1 - spot.s]
+    grads.small_copy(0).start()
+    for s in range(2):
+
+        @pl.when(spot.s == s)
+        def _(s=s):
+            for copy in home_copies(s):
+                copy.start()
+
+    grads.around(out_sems)
+    grads.small_copy(0).wait()
+    running = small_in[spot.s] + grads.small[1]
+    for n in range(1, 5):
+        grads.small[0] = running
+        grads.small_copy(n).start()
+        grads.small_copy(n).wait()
+        running = running + grads.small[1 + n]
+    small_out[...] = running
+    grads.finish(out_sems)
+    for s in range(2):
+
+        @pl.when(spot.s == s)
+        def _(s=s):
+            for copy in home_copies(s):
+                copy.wait()
+
+    total.close()
+
+
+def comm_call(kernel, collective, ins, in_specs, outs, out_specs, scratch, name):
+    return pl.pallas_call(
+        kernel,
+        out_shape=[jax.ShapeDtypeStruct(s, t) for s, t in outs],
+        in_specs=in_specs,
+        out_specs=out_specs,
+        scratch_shapes=scratch,
+        compiler_params=pltpu.CompilerParams(
+            collective_id=collective, has_side_effects=True, vmem_limit_bytes=60 * 1024 * 1024
+        ),
+        name=name,
+    )(*ins)
+
+
+def fast_shards(
+    tokens, cotangent, norm_gain, w_in, conv_weight, conv_bias, dt_bias, a_log, skip_gain, gate_gain, w_out
+):
+    section, place, half = lax.axis_index("section"), lax.axis_index("seq"), lax.axis_index("fsdp") // 2
+    span, width = tokens.shape[2:]
+    heads = HEADS // 8
+    wide = heads * HEADDIM
+    columns = 2 * wide + SHARED + LANES
+    shard = w_in.shape[1]
+    odd, third = place % 2, place // 2 * 3
+    ids = 12 * half + third + jnp.stack([2 * odd, 1 + 6 * odd, 6 + 2 * odd]).astype(jnp.int32)
+    dt_in = widened(w_in[0, :, INNER + XBC :], 1, LANES)
+    last_row = jnp.concatenate(
+        [norm_gain, widened(dt_bias, 1, LANES), widened(a_log, 1, LANES)], axis=1
+    )
+    pack = jnp.concatenate(
+        [
+            conv_weight[0],
+            conv_bias,
+            widened(jnp.repeat(skip_gain[0], HEADDIM)[None], 1, XBC),
+            widened(gate_gain, 1, XBC),
+            widened(last_row, 1, XBC),
+        ]
+    )
+    group = (2, 4, span, width)
+    weight_outs = [((width, columns), BF16), ((wide, width), BF16)]
+    weight_s = Weights.scratch(shard, columns)
+    payload = width + LANES
+    tile, tile_out, packs, all_rows, all_cot = comm_call(
+        open_kernel, 1,
+        [w_in[0], dt_in, w_out[0], pack, tokens[:, 0], cotangent[:, 0]], [ANY] * 6,
+        weight_outs + [((2, 8, XBC), F32), (group, BF16), (group, BF16)], [ANY] * 5,
+        weight_s + Spread.SEMS + Spread.SEMS + [DMA, DMA, DMA], "open",
+    )
+    own_rows = [lax.dynamic_index_in_dim(tokens[:, 0], section, 0, False)]
+    own_cot = lax.dynamic_index_in_dim(cotangent[:, 0], section, 0, False)
+
+    def joined(rows):
+        return rows.reshape(2, 4 * span, rows.shape[-1])
+
+    def cut(rows):
+        return rows.reshape(2, 4, span, rows.shape[-1])
+
+    tiles = [(tile, tile_out)]
+    parts, _, normed, *kept = run_forward(
+        heads, wide, joined(all_rows), tile, tile_out, (ids, packs[0])
+    )
+    saved = [(normed, kept)]
+    tile, tile_out, all_rows, branch, scales, rows = comm_call(
+        middle_kernel, 2,
+        [w_in[0], dt_in, w_out[0], cut(parts), own_rows[0]], [ANY] * 4 + [VMEM],
+        weight_outs
+        + [(group, BF16), ((span, width), F32), ((span, LANES), F32), ((span, width), BF16)],
+        [ANY] * 3 + [VMEM] * 3,
+        weight_s + Sum.scratch(span, payload) + Spread.SEMS, "middle",
+    )
+    own_rows.append(rows)
+    tiles.append((tile, tile_out))
+    last_parts, sums, normed, *kept = run_forward(
+        heads, wide, joined(all_rows), tile, tile_out, (ids, packs[1]), joined(all_cot)
+    )
+    saved.append((normed, kept))
+    sums = comm_call(
+        sums_kernel, 3, [sums], [VMEM], [(sums.shape, F32)], [VMEM],
+        [pltpu.VMEM((7,) + sums.shape, F32), DMA((7,)), DMA((7,))], "sums",
+    )[0]
+    w_grads, wo_grads, small = [None, None], [None, None], [None, None]
+
+    def products(l, proj_grad, normed_out, grads):
+        w_grads[l] = dot_tn(saved[l][0].reshape(-1, width), proj_grad.reshape(-1, columns)).astype(BF16)
+        wo_grads[l] = dot_tn(normed_out.reshape(-1, wide), grads.reshape(-1, width)).astype(BF16)
+
+    parts, proj_grad, normed_out, small[1] = run_backward(
+        heads, wide, joined(all_cot), sums, "rows", saved[1][1], *tiles[1], (ids, packs[1])
+    )
+    products(1, proj_grad, normed_out, joined(all_cot))
+    rows_spec = ((span, width), BF16)
+    all_grads, last_grad, gain_1, last_rows = comm_call(
+        turn_kernel, 4,
+        [cut(parts), cut(last_parts), own_rows[1], own_cot, packs, branch, scales, own_rows[1]],
+        [ANY, ANY] + [VMEM] * 6,
+        [((2, 4, span, payload), BF16), rows_spec, ((8, width), F32), rows_spec], [ANY] + [VMEM] * 3,
+        Sum.scratch(span, width) + Sum.scratch(span, payload) + Spread.SEMS
+        + [pltpu.VMEM((span, payload), BF16)], "turn",
+    )
+    all_grads = joined(all_grads)
+    parts, proj_grad, normed_out, small[0] = run_backward(
+        heads, wide, all_grads, None, "columns", saved[0][1], *tiles[0], (ids, packs[0])
+    )
+    products(0, proj_grad, normed_out, all_grads[..., :width])
+    final_columns = 2 * INNER + SHARED + LANES
+    home_rows, home_grads, final, final_out, small = comm_call(
+        close_kernel, 5,
+        [
+            cut(parts), own_rows[0], last_grad, packs, own_rows[1], last_rows, last_grad,
+            *w_grads, *wo_grads, *small, gain_1,
+        ],
+        [ANY] + [VMEM] * 6 + [ANY] * 4 + [VMEM] * 3,
+        [
+            ((2, span, width), BF16), ((2, span, width), BF16),
+            ((shard, final_columns), BF16), (w_out.shape[1:], BF16), ((8, XBC), F32),
+        ],
+        [ANY] * 4 + [VMEM],
+        Sum.scratch(span, width) + Grads.scratch(shard, columns, wide, width)
+        + [
+            pltpu.VMEM((span, width), BF16), pltpu.VMEM((2, 8, XBC), F32),
+            DMA((2,)), DMA((2,)), DMA((2,)), DMA((12,)), DMA((12,)),
+        ],
+        "close",
+    )
+    return (
+        home_rows[None, :, None],
+        home_grads[None, :, None],
+        small[7:8, :width],
+        final[None, :, : INNER + XBC + HEADS].astype(F32),
+        small[None, :CONV],
+        small[CONV : CONV + 1],
+        small[7:8, DT_AT : DT_AT + HEADS],
+        small[7:8, RATE_AT : RATE_AT + HEADS],
+        small[5:6, :INNER].reshape(1, HEADS, HEADDIM).sum(-1),
+        small[6:7, :INNER],
+        final_out[None].astype(F32),
+    )
 
 
 def shards(
@@ -471,12 +1418,7 @@
     params = []
     for l in range(layers):
         ch, bc, dtp, gain = jnp.split(smalls[l], cuts)
-        params.append(
-            dict(
-                gain=gain[None], w=w_tiles[l], wo=wo_tiles[l],
-                ch=ch.reshape(8, -1), bc=bc.reshape(8, -1), dtp=dtp.reshape(8, -1),
-            )
-        )
+        params.append((gain[None], ch.reshape(8, -1), bc.reshape(8, -1), dtp.reshape(8, -1)))
 
     def gather_rows(own_rows):
         rows = lax.all_gather(own_rows, "seq", axis=0, tiled=True)
@@ -498,7 +1440,9 @@
     inputs, outputs, branch, saved, scales = [own_tokens], [], [], [], []
     for l in range(layers):
         rows = gather_rows(inputs[l])
-        parts, square, normed, *kept = run_forward(heads, rows, params[l])
+        parts, square, normed, *kept = run_forward(
+            heads, wide, rows, w_tiles[l], wo_tiles[l], params[l]
+        )
         saved.append((normed, kept))
         total = sum_rows(parts).astype(F32)
         square = sum_rows(square)[:, :1]
@@ -517,7 +1461,7 @@
         aux = gather_rows(aux)
         normed, kept = saved[l]
         parts, proj_grad, normed_out, g_ch, g_bc, g_dt = run_backward(
-            heads, all_grads, aux, kept, params[l]
+            heads, wide, all_grads, aux, "lanes", kept, w_tiles[l], wo_tiles[l], params[l]
         )
         w_grads[l] = dot_tn(normed.reshape(-1, width), proj_grad.reshape(-1, proj_grad.shape[-1])).astype(BF16)
         wo_grads[l] = dot_tn(normed_out.reshape(-1, wide), all_grads.reshape(-1, width)).astype(BF16)
@@ -526,7 +1470,7 @@
         scale = lax.rsqrt(jnp.mean(rows * rows, axis=-1, keepdims=True) + NORM_EPS)
         scaled = rows * scale
         g_gain = jnp.sum(grad_normed * scaled, axis=0)
-        pulled = grad_normed * params[l]["gain"]
+        pulled = grad_normed * params[l][0]
         inner = jnp.mean(pulled * scaled, axis=-1, keepdims=True)
         grad = scale * (pulled - scaled * inner) + grad_rows.astype(F32)
         grad_rows = grad.astype(BF16)
@@ -610,8 +1554,9 @@
 
 
 def solution(mesh):
+    shape = tuple(mesh.shape[a] for a in ("section", "seq", "fsdp"))
     return jax.shard_map(
-        shards,
+        fast_shards if shape == (2, 4, 4) else shards,
         mesh=mesh,
         in_specs=(
             P(None, "fsdp", "seq", None),

time: 1140 us -> 544 us (0.48)
  waiting for transfers between devices: 771 us -> 0 us
  Pallas kernels: 21.5 us -> 490 us
  blocking collectives: 162 us -> 0 us
  local copies, waits for them, and re-layouts: 95 us -> 28 us
  other arithmetic: 44.5 us -> 11 us
  between operations: 15.4 us -> 0.96 us
  starting transfers between devices: 12.6 us -> 0 us
    pallas_call x2 -> x9, Pallas kernels: 21.5 us -> 490 us  [the longest x5 438 us: comm_call(): pl.pallas_call(kernel, out_shape=[jax.ShapeDtypeStruct(s, t) for s, t in...]
    reduce_scatter x15 -> x0, waiting for transfers between devices: 414 us -> none  [the longest x6 189 us: sum_rows(): lax.psum_scatter(parts, 'fsdp', scatter_dimension=0, axis_index_groups=pl...]
    all_gather x9 -> x0, waiting for transfers between devices: 230 us -> none  [the longest x4 107 us: gather_rows(): lax.all_gather(rows, 'fsdp', axis=0, axis_index_groups=plan.peer_groups)]
    all_gather x9 -> x0, blocking collectives: 119 us -> none  [the longest x6 63.7 us: gather_rows(): rows = lax.all_gather(own_rows, 'seq', axis=0, tiled=True)]
    psum x1 -> x0, waiting for transfers between devices: 108 us -> none  [shards(): smalls = lax.psum(jnp.stack(small_grads), ('section', 'seq', 'fsdp'))]
    psum x1 -> x0, blocking collectives: 33.2 us -> none  [shards(): lax.psum(w_grad[..., 2 * wide:2 * wide + SHARED].sum(0), 'seq')]
    pallas_call x2 -> x0, local copies, waits for them, and re-layouts: 25.7 us -> none  [run_backward(): pl.pallas_call(partial(backward_kernel, heads), grid=(count,), out_shape=...]
    all_to_all x2 -> x0, waiting for transfers between devices: 16.5 us -> none  [the longest x1 16.5 us: shards(): tile = lax.all_to_all(tile, 'fsdp', 0, 0, tiled=True).reshape(width, -1)]
  transfers between devices with their start and end apart: 27 -> 0, of which waited for: 24 -> 0; matrix products, arithmetic and copies ran while one was open for 7% -> 0% of each run, Pallas kernels for 0% -> 0%
where the time goes in v2:
time: 544 us
  Pallas kernels  490 us (90%)
  local copies, waits for them, and re-layouts  28 us (5%)
  matrix products  13.9 us (3%)
  other arithmetic  11 us (2%)
    pallas_call x5, Pallas kernels, comm_call(): pl.pallas_call(kernel, out_shape=[jax.ShapeDtypeStruct(s, t) for s, t in...  438 us
    pallas_call x2, Pallas kernels, run_backward(): pl.pallas_call(partial(backward_kernel, heads, len(params), aux_kind), gr...  28.7 us
    pallas_call x2, Pallas kernels, run_forward(): pl.pallas_call(partial(forward_kernel, heads, len(params), grad_rows is n...  23.3 us
    unnamed x42, local copies, waits for them, and re-layouts  20 us
    dot_general x4, matrix products, dot(): lax.dot_general(left, right, (contract, ((), ())), preferred_element_type...  13.9 us

profile of v2, /device:TPU:0, one launch (start us, length us, event | category | flops | bytes accessed | tf_op | source)
XLA Modules:
  0.0 543.5 jit_solution(6237599415762591477)
XLA Ops:
  0.7 0.6 add_add_fusion.refs_3_.refs_9_.refs_8_
  1.3 7.6 %copy.22 = bf16[1,384,6448]{2,1,0:T(8,128)(2,1)} copy(bf16[1,384,6448]{1,2,0:T(8,128)(2,1)} %param.14) | data formatting | bytes 9904128 | tf_op args[3]
  8.9 0.9 slice_bitcast_fusion.2
  9.8 0.7 pad.22.refs_1_
  10.5 0.1 broadcast_in_dim_reshape.3
  10.8 0.7 concatenate.7.refs_3_
  11.5 81.2 %open.1 = (bf16[1536,1152]{1,0:T(8,128)(2,1)}, bf16[384,1536]{1,0:T(8,128)(2,1)}, f32[2,8,3328]{2,1,0:T(8,128)}, bf16[2,4,64,1536]{3,2,1,0:T(8,128)(2,1)}, bf16[2,4,64,1536]{3,2,1,0:T(8,128)(2,1)}) custom-call(bf16[384,6448]{1,0:T(8,128)(2,1)} %bitcast.63, bf16[384,128]{1,0:T(8,128)(2,1)} %pad.22.refs_1_, bf16[768,1536]{1,0:T(8,128)(2,1)} %bitcast.65, ...), custom_call_target="tpu_custom_call" | custom-call | tf_op jit(solution)/shard_map/open/pallas_call | solution.py:1227
  92.7 1.6 slice_bitcast_fusion
  94.4 11.1 %forward.2 = (bf16[2,256,1664]{2,1,0:T(8,128)(2,1)}, f32[2,8,256]{2,1,0:T(8,128)}, bf16[2,256,1536]{2,1,0:T(8,128)(2,1)}, f32[2,256,384]{2,1,0:T(8,128)}, bf16[2...) custom-call(bf16[2,256,1536]{2,1,0:T(8,128)(2,1)} %bitcast.77, ...), custom_call_target="tpu_custom_call" | custom-call | tf_op jit(solution)/shard_map/forward/pallas_call | solution.py:440
  105.5 0.8 dynamic-slice_bitcast_fusion
  106.3 83.6 %middle.1 = (bf16[1536,1152]{1,0:T(8,128)(2,1)}, bf16[384,1536]{1,0:T(8,128)(2,1)}, bf16[2,4,64,1536]{3,2,1,0:T(8,128)(2,1)}, f32[64,1536]{1,0:T(8,128)}, f32[64,128]{1,0:T(8,128)}, /*index=5*/bf16[64,1536]{1,0:T(8,128)(2,1)}) custom-call(bf16[384,6448]{1,0:T(8,128)(2,1)} %bitcast.64, bf16[384,128]{1,0:T(8,128)(2,1)} %pad.22.refs_1_, ...), custom_call_target="tpu_custom_call" | custom-call | tf_op jit(solution)/shard_map/middle/pallas_call | solution.py:1227
  189.9 12.2 %forward.3 = (bf16[2,256,1664]{2,1,0:T(8,128)(2,1)}, f32[2,8,256]{2,1,0:T(8,128)}, bf16[2,256,1536]{2,1,0:T(8,128)(2,1)}, f32[2,256,384]{2,1,0:T(8,128)}, bf16[2...) custom-call(bf16[2,256,1536]{2,1,0:T(8,128)(2,1)} %bitcast.76, ...), custom_call_target="tpu_custom_call" | custom-call | tf_op jit(solution)/shard_map/forward/pallas_call | solution.py:440
  202.1 12.5 %sums.1.refs_1_ = f32[2,8,256]{2,1,0:T(8,128)} custom-call(f32[2,8,256]{2,1,0:T(8,128)} %get-tuple-element.63.mine_ref), custom_call_target="tpu_custom_call" | custom-call | tf_op jit(solution)/shard_map/sums/pallas_call | solution.py:1227
  214.7 14.2 %backward.2 = (bf16[2,256,1536]{2,1,0:T(8,128)(2,1)}, bf16[2,256,1152]{2,1,0:T(8,128)(2,1)}, bf16[2,256,384]{2,1,0:T(8,128)(2,1)}, f32[8,3328]{1,0:T(8,128)}) custom-call(bf16[2,256,1536]{2,1,0:T(8,128)(2,1)} %bitcast.68, f32[2,8,256]{2,1,0:T(8,128)} %sums.1.refs_1_, f32[2,256,384]{2,1,0:T(8,128)} %get-tuple-element.64.refs_2_, ...), custom_call_target="tpu_custom_call" | custom-call | tf_op jit(solution)/shard_map/backward/pallas_call | solution.py:462
  228.9 2.8 convolution_convert_fusion.refs_10_
  231.7 60.7 %turn.1 = (bf16[2,4,64,1664]{3,2,1,0:T(8,128)(2,1)}, bf16[64,1536]{1,0:T(8,128)(2,1)}, f32[8,1536]{1,0:T(8,128)}, bf16[64,1536]{1,0:T(8,128)(2,1)}) custom-call(bf16[2,4,64,1536]{3,2,1,0:T(8,128)(2,1)} %bitcast.75, bf16[2,4,64,1664]{3,2,1,0:T(8,128)(2,1)} %bitcast.73, bf16[64,1536]{1,0:T(8,128)(2,1)} %get-tuple-element.71.refs_2_.refs_7_.refs_4_, ...), custom_call_target="tpu_custom_call" | custom-call | tf_op jit(solution)/shard_map/turn/pallas_call | solution.py:1227
  292.4 14.5 %backward.3 = (bf16[2,256,1536]{2,1,0:T(8,128)(2,1)}, bf16[2,256,1152]{2,1,0:T(8,128)(2,1)}, bf16[2,256,384]{2,1,0:T(8,128)(2,1)}, f32[8,3328]{1,0:T(8,128)}) custom-call(bf16[2,256,1664]{2,1,0:T(8,128)(2,1)} %bitcast.71, f32[2,256,384]{2,1,0:T(8,128)} %get-tuple-element.75.refs_1_, bf16[2,256,384]{2,1,0:T(8,128)(2,1)} %get-tuple-element.76.refs_2_, ...), custom_call_target="tpu_custom_call" | custom-call | tf_op jit(solution)/shard_map/backward/pallas_call | solution.py:462
  306.9 3.0 fusion.2.refs_9_
  309.9 4.1 fusion.1.refs_8_
  314.0 4.1 fusion.refs_7_
  318.0 199.7 %close.1 = (bf16[2,64,1536]{2,1,0:T(8,128)(2,1)}, bf16[2,64,1536]{2,1,0:T(8,128)(2,1)}, bf16[384,6528]{1,0:T(8,128)(2,1)}, bf16[768,1536]{1,0:T(8,128)(2,1)}, f32[8,3328]{1,0:T(8,128)}) custom-call(bf16[2,4,64,1536]{3,2,1,0:T(8,128)(2,1)} %bitcast.74, bf16[64,1536]{1,0:T(8,128)(2,1)} %get-tuple-element.115.refs_4_.refs_1_, ...), custom_call_target="tpu_custom_call" | custom-call | tf_op jit(solution)/shard_map/close/pallas_call | solution.py:1227
  517.8 6.9 %bitcast_convert_fusion = f32[1,384,6448]{2,1,0:T(8,128)} fusion(bf16[384,6528]{1,0:T(8,128)(2,1)} %get-tuple-element.95), kind=kLoop, calls=%fused_computation.4 | loop fusion | flops 2476032 | bytes 14856192 | tf_op jit(solution)/shard_map/convert_element_type | solution.py:1354
  524.7 10.8 %copy.29 = f32[1,384,6448]{1,2,0:T(8,128)} copy(f32[1,384,6448]{2,1,0:T(8,128)} %bitcast_convert_fusion) | data formatting | bytes 19808256
  535.5 2.8 bitcast_convert_fusion.1
  538.3 0.6 slice_bitcast_fusion.3
  539.0 0.6 fusion.6
  539.7 0.6 reduce_sum.11
  540.3 0.6 slice.45
  540.9 0.6 slice.42
  541.5 0.5 fusion.7
  542.0 0.7 copy.35
  542.8 0.7 copy.36
  (44 shorter events, 0.3 us)
Async XLA Ops:
  1.3 9.2 %copy-start.12 = (f32[1,48]{1,0:T(1,128)S(1)}, f32[1,48]{1,0:T(1,128)}, u32[]{:S(2)}) copy-start(f32[1,48]{1,0:T(1,128)} %param.19) | copy-start | bytes 580
  1.3 9.4 %copy-start.11 = (f32[1,1536]{1,0:T(1,128)S(1)}, f32[1,1536]{1,0:T(1,128)}, u32[]{:S(2)}) copy-start(f32[1,1536]{1,0:T(1,128)} %param.13) | copy-start | bytes 18436
  1.3 9.4 %copy-start.13 = (f32[1,48]{1,0:T(1,128)S(1)}, f32[1,48]{1,0:T(1,128)}, u32[]{:S(2)}) copy-start(f32[1,48]{1,0:T(1,128)} %param.18) | copy-start | bytes 580
  1.3 9.4 %copy-start.14 = (f32[1,48]{1,0:T(1,128)S(1)}, f32[1,48]{1,0:T(1,128)}, u32[]{:S(2)}) copy-start(f32[1,48]{1,0:T(1,128)} %param.17) | copy-start | bytes 580
  1.3 9.4 %copy-start.10 = (f32[1,3072]{1,0:T(1,128)S(1)}, f32[1,3072]{1,0:T(1,128)}, u32[]{:S(2)}) copy-start(f32[1,3072]{1,0:T(1,128)} %param.20) | copy-start | bytes 36868
  1.3 9.4 %copy-start.8 = (f32[1,4,3328]{2,1,0:T(4,128)S(1)}, f32[1,4,3328]{2,1,0:T(4,128)}, u32[]{:S(2)}) copy-start(f32[1,4,3328]{2,1,0:T(4,128)} %param.15) | copy-start | bytes 159748
  1.3 9.4 %copy-start.9 = (f32[1,3328]{1,0:T(1,128)S(1)}, f32[1,3328]{1,0:T(1,128)}, u32[]{:S(2)}) copy-start(f32[1,3328]{1,0:T(1,128)} %param.16) | copy-start | bytes 39940
  94.4 11.1 %copy-start.3 = (bf16[2,1,64,1536]{3,2,1,0:T(8,128)(2,1)S(1)}, bf16[2,1,64,1536]{3,2,1,0:T(8,128)(2,1)}, u32[]{:S(2)}) copy-start(bf16[2,1,64,1536]{3,2,1,0:T(8,128)(2,1)} %param.11) | copy-start | bytes 1179652
  94.4 11.1 %copy-start.4 = (bf16[2,1,64,1536]{3,2,1,0:T(8,128)(2,1)S(1)}, bf16[2,1,64,1536]{3,2,1,0:T(8,128)(2,1)}, u32[]{:S(2)}) copy-start(bf16[2,1,64,1536]{3,2,1,0:T(8,128)(2,1)} %param.12) | copy-start | bytes 1179652
  214.7 14.2 %copy-start = (bf16[2,4,64,1536]{3,2,1,0:T(8,128)(2,1)S(1)}, bf16[2,4,64,1536]{3,2,1,0:T(8,128)(2,1)}, u32[]{:S(2)}) copy-start(bf16[2,4,64,1536]{3,2,1,0:T(8,128)(2,1)} %get-tuple-element.54) | copy-start | bytes 4718596
  292.4 14.5 %copy-start.2 = (bf16[2,4,64,1664]{3,2,1,0:T(8,128)(2,1)S(1)}, bf16[2,4,64,1664]{3,2,1,0:T(8,128)(2,1)}, u32[]{:S(2)}) copy-start(bf16[2,4,64,1664]{3,2,1,0:T(8,128)(2,1)} %get-tuple-element.74) | copy-start | bytes 5111812
  306.9 3.0 copy-start.16
  306.9 3.0 copy-start.17
  309.9 4.1 copy-start.15
  309.9 4.1 copy-start.18
  524.7 10.8 %copy-start.1 = (bf16[768,1536]{1,0:T(8,128)(2,1)S(1)}, bf16[768,1536]{1,0:T(8,128)(2,1)}, u32[]{:S(2)}) copy-start(bf16[768,1536]{1,0:T(8,128)(2,1)} %get-tuple-element.96) | copy-start | bytes 7077892
  535.5 2.9 copy-start.7
  535.5 6.5 %copy-start.6 = (bf16[2,64,1536]{2,1,0:T(8,128)(2,1)S(1)}, bf16[2,64,1536]{2,1,0:T(8,128)(2,1)}, u32[]{:S(2)}) copy-start(bf16[2,64,1536]{2,1,0:T(8,128)(2,1)} %get-tuple-element.92) | copy-start | bytes 1179652
  535.5 7.3 %copy-start.5 = (bf16[2,64,1536]{2,1,0:T(8,128)(2,1)S(1)}, bf16[2,64,1536]{2,1,0:T(8,128)(2,1)}, u32[]{:S(2)}) copy-start(bf16[2,64,1536]{2,1,0:T(8,128)(2,1)} %get-tuple-element.93) | copy-start | bytes 1179652

commit v3 on v2

--- a/solution.py
+++ b/solution.py
@@ -16,6 +16,8 @@
 XBC = 3328
 SHARED = 2 * STATE
 LANES = 128
+THIRD = 192
+PIECE = 256
 GAIN_END = 1536
 DT_AT = 1536
 RATE_AT = DT_AT + LANES
@@ -109,27 +111,27 @@
 
 
 def selection(ids_ref):
-    rows = lax.broadcasted_iota(jnp.int32, (LANES, LANES), 0)
-    columns = lax.broadcasted_iota(jnp.int32, (LANES, LANES), 1)
-    target = jnp.full((LANES, LANES), -1, jnp.int32)
-    for i in range(3):
-        here = (columns >= 2 * i) & (columns < 2 * i + 2)
-        target = jnp.where(here, columns + 2 * (ids_ref[i] - i), target)
+    rows = lax.broadcasted_iota(jnp.int32, (HEADS, LANES), 0)
+    columns = lax.broadcasted_iota(jnp.int32, (HEADS, LANES), 1)
+    target = jnp.full((HEADS, LANES), -1, jnp.int32)
+    for j in range(2):
+        here = (columns >= 3 * j) & (columns < 3 * j + 3)
+        target = jnp.where(here, columns + 3 * (ids_ref[j] - j), target)
     return (rows == target).astype(F32)
 
 
-def pair_lanes(ids_ref, i):
-    return pl.ds(pl.multiple_of(ids_ref[i] * LANES, LANES), LANES)
+def piece_lanes(ids_ref, j):
+    return pl.ds(pl.multiple_of(ids_ref[j] * PIECE, PIECE), PIECE)
 
 
 def load_params(refs):
     if len(refs) == 2:
         ids_ref, pack_ref = refs
         sel = selection(ids_ref)
-        ch = jnp.concatenate([pack_ref[:, pair_lanes(ids_ref, i)] for i in range(3)], axis=1)
-        rows = [pack_ref[7:8, at : at + LANES] for at in (DT_AT, RATE_AT)]
+        ch = jnp.concatenate([pack_ref[:, piece_lanes(ids_ref, j)][:, :THIRD] for j in range(2)], axis=1)
+        rows = [pack_ref[7:8, at : at + HEADS] for at in (DT_AT, RATE_AT)]
         dtp = dot(stacked(rows, 8), sel, precision=HIGHEST)
-        return pack_ref[7:8, :GAIN_END], ch, pack_ref[:, INNER:XBC], dtp, sel.astype(BF16)
+        return pack_ref[7:8, :GAIN_END], ch, pack_ref[:, -SHARED:], dtp, sel.astype(BF16)
     gain_ref, ch_ref, bc_ref, dtp_ref = refs
     return gain_ref[...], ch_ref[...], bc_ref[...], dtp_ref[...], None
 
@@ -148,11 +150,11 @@
     scale = lax.rsqrt(jnp.mean(rows * rows, axis=-1, keepdims=True) + NORM_EPS)
     normed = (rows * scale * gain).astype(BF16)
     normed_ref[0] = normed
-    gate = dot(normed, w_ref[:, :wide])
+    gate = dot_nt(normed, w_ref[:wide])
     gate_ref[0] = gate
-    x_raw = dot(normed, w_ref[:, wide : 2 * wide]).astype(BF16)
+    x_raw = dot_nt(normed, w_ref[wide : 2 * wide]).astype(BF16)
     xraw_ref[0] = x_raw
-    rest = dot(normed, w_ref[:, 2 * wide :]).astype(BF16)
+    rest = dot_nt(normed, w_ref[2 * wide :]).astype(BF16)
     bcraw_ref[0] = rest[:, :SHARED]
     dt_raw = rest[:, SHARED:]
     if sel is not None:
@@ -376,7 +378,7 @@
     if sel is not None:
         low_dt = dot_nt(low_dt, sel).astype(BF16)
     pg_ref[0, :, 2 * wide + SHARED :] = low_dt
-    dn_ref[0] = dot_nt(pg_ref[0], w_ref[...]).astype(BF16)
+    dn_ref[0] = dot(pg_ref[0], w_ref[...]).astype(BF16)
     by_channel = stacked(ch_rows + [skip_row, gain_row], 8)
     by_shared = stacked(bc_rows, 8)
     by_head = stacked([jnp.sum(grad_dt, axis=0, keepdims=True), rate_row * rate], 8)
@@ -392,11 +394,13 @@
         def _():
             sum_ref[...] = jnp.zeros_like(sum_ref)
 
-        for i in range(3):
-            sum_ref[:, pair_lanes(ids_ref, i)] += by_channel[:, i * LANES : (i + 1) * LANES]
-        sum_ref[:, INNER:XBC] += by_shared
-        sum_ref[7:8, DT_AT : DT_AT + LANES] += by_head[0:1]
-        sum_ref[7:8, RATE_AT : RATE_AT + LANES] += by_head[1:2]
+        for j in range(2):
+            part = by_channel[:, j * THIRD : (j + 1) * THIRD]
+            part = jnp.concatenate([part, jnp.zeros((8, PIECE - THIRD), F32)], axis=1)
+            sum_ref[:, piece_lanes(ids_ref, j)] += part
+        sum_ref[:, -SHARED:] += by_shared
+        sum_ref[7:8, DT_AT : DT_AT + HEADS] += by_head[0:1]
+        sum_ref[7:8, RATE_AT : RATE_AT + HEADS] += by_head[1:2]
         return
     for ref, value in zip(sum_refs, (by_channel, by_shared, by_head)):
 
@@ -452,7 +456,7 @@
 
 def run_backward(heads, wide, grad_rows, aux, aux_kind, saved, w, wo, params):
     count, length, _ = grad_rows.shape
-    width, columns = w.shape
+    columns, width = w.shape
     given = [grad_rows] + ([] if aux is None else [aux]) + list(saved)
     constants = [w, wo, *params]
     outs = [(width, BF16), (columns, BF16), (wide, BF16)]
@@ -538,9 +542,8 @@
     def column(self, z):
         return (self.s, self.q, z)
 
-    def pair(self, half, i):
-        odd, third = self.q % 2, self.q // 2 * 3
-        return 12 * half + third + [2 * odd, 1 + 6 * odd, 6 + 2 * odd][i]
+    def piece(self, half, j):
+        return 8 * half + 4 * j + self.q
 
 
 def greet(places):
@@ -554,6 +557,22 @@
     return pltpu.make_async_remote_copy(
         src_ref=src, dst_ref=dst, send_sem=send_sem, recv_sem=recv_sem, device_id=place, device_id_type=MESH
     )
+
+
+class Home:
+    def __init__(self, src, buffer, dst, sems):
+        self.load = pltpu.make_async_copy(src, buffer, sems[0])
+        self.store = pltpu.make_async_copy(buffer, dst, sems[1])
+
+    def begin(self):
+        self.load.start()
+
+    def go_on(self):
+        self.load.wait()
+        self.store.start()
+
+    def end(self):
+        self.store.wait()
 
 
 class Spread:
@@ -632,9 +651,9 @@
 
     def start(self):
         for i in range(2):
-            for k in (1, 2, 3):
-                self.copy(k, i).start()
             self.here(i).start()
+        for k in (1, 2, 3):
+            self.copy(k, 0).start()
 
     def plane_total(self, i):
         self.here(i).wait()
@@ -645,6 +664,9 @@
         return total
 
     def forward(self):
+        for k in (1, 2, 3):
+            self.copy(k, 0).wait_send()
+            self.copy(k, 1).start()
         total = self.plane_total(0)
         width = self.width
         self.twin_rows[0, :, :width] = total[:, :width].astype(BF16)
@@ -660,24 +682,33 @@
         return total
 
     def close(self):
-        for i in range(2):
-            for k in (1, 2, 3):
-                self.copy(k, i).wait_send()
+        for k in (1, 2, 3):
+            self.copy(k, 1).wait_send()
         self.across().wait_send()
 
 
+def tile_parts(spot, half):
+    parts = []
+    for part in range(2):
+        for j in range(2):
+            at = part * INNER + THIRD * spot.piece(half, j)
+            parts.append((pl.multiple_of(at, 64), (2 * part + j) * THIRD, THIRD))
+    return parts + [(2 * INNER, 4 * THIRD, SHARED + HEADS)]
+
+
 class Weights:
-    LOCAL = 20
+    PARTS = 5
 
     @staticmethod
-    def scratch(rows, columns):
-        return [pltpu.VMEM((rows, columns), BF16), DMA((Weights.LOCAL,)), DMA((24,)), DMA((24,))]
-
-    def __init__(self, spot, layer, w_in, dt_in, w_out, tile, tile_out, scratch):
+    def scratch(columns, shard, width):
+        buffers = [pltpu.VMEM((columns, shard), BF16), pltpu.VMEM((THIRD, width), BF16)]
+        return buffers + [DMA((4,)), DMA((43,)), DMA((43,))]
+
+    def __init__(self, spot, layer, w_in, w_out, tile, tile_out, scratch):
         self.spot, self.layer = spot, layer
-        self.w_in, self.dt_in, self.w_out, self.tile, self.tile_out = w_in, dt_in, w_out, tile, tile_out
-        self.stage, self.local, self.send, self.recv = scratch
-        self.rows = w_in.shape[0]
+        self.w_in, self.w_out, self.tile, self.tile_out = w_in, w_out, tile, tile_out
+        self.buffer, self.out_buffer, self.local, self.send, self.recv = scratch
+        self.shard = w_in.shape[1]
         self.others = 2 * (1 - spot.half)
         self.gateway = 2 - spot.half
         self.is_gateway = (spot.z == 1) | (spot.z == 2)
@@ -685,129 +716,124 @@
     def at_source(self, step):
         pl.when(self.spot.s == self.layer)(step)
 
-    def block(self, z):
-        return self.tile.at[pl.ds(z * self.rows, self.rows)]
-
-    def staged(self, own):
-        spot = self.spot
-        half = spot.half if own else 1 - spot.half
-        target = self.block(spot.z) if own else self.stage
-        jobs = []
-        for i in range(3):
-            for part in range(2):
-                at = part * INNER + LANES * spot.pair(half, i)
-                source = self.w_in.at[:, pl.ds(pl.multiple_of(at, LANES), LANES)]
-                jobs.append((source, target.at[:, pl.ds((3 * part + i) * LANES, LANES)]))
-        jobs.append((self.w_in.at[:, pl.ds(2 * INNER, SHARED)], target.at[:, pl.ds(6 * LANES, SHARED)]))
-        jobs.append((self.dt_in, target.at[:, pl.ds(6 * LANES + SHARED, LANES)]))
-        first = 0 if own else len(jobs)
-        return [
-            pltpu.make_async_copy(a, b, self.local.at[first + n]) for n, (a, b) in enumerate(jobs)
-        ]
-
-    def out_rows(self, i):
-        at = (self.spot.pair(self.spot.half, i) % 6) * LANES
-        source = self.w_out.at[pl.ds(pl.multiple_of(at, LANES), LANES)]
-        return source, self.tile_out.at[pl.ds(i * LANES, LANES)]
-
-    def owns(self, i):
-        return self.spot.lo == [0, self.spot.q % 2, 1][i]
-
-    def out_local(self, i):
-        return pltpu.make_async_copy(*self.out_rows(i), self.local.at[16 + i])
-
-    def out_to(self, i, sibling, from_tile=False):
-        source, target = self.out_rows(i)
-        j = 8 + 3 * sibling + i
-        place = self.spot.sibling if sibling else self.spot.at_mate
-        return remote(target if from_tile else source, target, self.send.at[j], self.recv.at[j], place)
-
-    def own_to_mate(self):
-        block = self.block(self.spot.z)
-        return remote(block, block, self.send.at[0], self.recv.at[0], self.spot.at_mate)
-
-    def stage_to_gateway(self):
-        j = 1 + self.spot.lo
-        place = self.spot.column(self.gateway)
-        return remote(self.stage, self.block(self.spot.z), self.send.at[1], self.recv.at[j], place)
-
-    def passed(self, n):
-        block = self.block(self.others + n)
-        return remote(block, block, self.send.at[2 + n], self.recv.at[1 + n], self.spot.at_mate)
-
-    def to_sibling(self, n):
-        z = [self.spot.z, self.spot.mate, self.others, self.others + 1][n]
-        block = self.block(z)
-        return remote(block, block, self.send.at[4 + n], self.recv.at[4 + n], self.spot.sibling)
+    def source(self, half, n):
+        first, _, size = tile_parts(self.spot, half)[n]
+        return self.w_in.at[pl.ds(first, size)]
+
+    def target(self, z, n):
+        _, first, size = tile_parts(self.spot, 0)[n]
+        columns = pl.ds(pl.multiple_of(z * self.shard, LANES), self.shard)
+        return self.tile.at[pl.ds(first, size), columns]
+
+    def load(self, n):
+        part = self.buffer.at[pl.ds(*tile_parts(self.spot, 0)[n][1:])]
+        return pltpu.make_async_copy(self.source(self.spot.half, n), part, self.send.at[n])
+
+    def store(self):
+        columns = pl.ds(pl.multiple_of(self.spot.z * self.shard, LANES), self.shard)
+        return pltpu.make_async_copy(self.buffer, self.tile.at[:, columns], self.local.at[0])
+
+    def out_home(self):
+        return Home(
+            self.out_source(), self.out_buffer, self.out_part(self.spot.lo),
+            (self.local.at[1], self.local.at[2]),
+        )
+
+    def to_mate(self, n):
+        source, target = self.source(self.spot.half, n), self.target(self.spot.z, n)
+        return remote(source, target, self.send.at[n], self.recv.at[n], self.spot.at_mate)
+
+    def to_gateway(self, n):
+        source, target = self.source(1 - self.spot.half, n), self.target(self.spot.z, n)
+        j = 5 + 5 * self.spot.lo + n
+        return remote(source, target, self.send.at[5 + n], self.recv.at[j], self.spot.column(self.gateway))
+
+    def passed(self, c, n):
+        part = self.target(self.others + c, n)
+        j = 5 * c + n
+        return remote(part, part, self.send.at[10 + j], self.recv.at[5 + j], self.spot.at_mate)
+
+    def to_sibling(self, b, n):
+        j = 20 + 5 * b + n
+        part = self.target([self.spot.z, self.spot.mate, self.others, self.others + 1][b], n)
+        source = self.source(self.spot.half, n) if b == 0 else part
+        return remote(source, part, self.send.at[j], self.recv.at[j], self.spot.sibling)
+
+    def out_part(self, lo):
+        return self.tile_out.at[pl.ds(pl.multiple_of(lo * THIRD, 64), THIRD)]
+
+    def out_source(self):
+        return self.w_out.at[pl.ds(pl.multiple_of(self.spot.q * THIRD, 64), THIRD)]
+
+    def out_to(self, n):
+        part = self.out_part(self.spot.lo if n < 2 else 1 - self.spot.lo)
+        place = self.spot.sibling if n else self.spot.at_mate
+        source = self.out_source() if n < 2 else part
+        return remote(source, part, self.send.at[40 + n], self.recv.at[40 + n], place)
+
+    def send_part(self, n):
+        if n < self.PARTS:
+            self.to_gateway(n).start()
+            self.to_mate(n).start()
+        elif n == self.PARTS:
+            self.out_to(0).start()
 
     def begin(self):
         @self.at_source
         def _():
-            for copy in self.staged(True) + self.staged(False):
-                copy.start()
-            for i in range(3):
-                pl.when(self.owns(i))(lambda i=i: self.out_local(i).start())
+            for n in range(self.PARTS):
+                self.load(n).start()
+            self.out_home().begin()
 
     def start(self):
         @self.at_source
         def _():
-            for copy in self.staged(True):
-                copy.wait()
-            self.own_to_mate().start()
-            self.to_sibling(0).start()
-            for copy in self.staged(False):
-                copy.wait()
-            self.stage_to_gateway().start()
-            for i in range(3):
-
-                @pl.when(self.owns(i))
-                def _(i=i):
-                    self.out_to(i, 0).start()
-                    self.out_to(i, 1).start()
-
-    def relay_mate(self):
+            for n in range(self.PARTS):
+                self.load(n).wait()
+            for n in range(self.PARTS):
+                self.to_gateway(n).start()
+                self.to_mate(n).start()
+            self.out_to(0).start()
+            for n in range(self.PARTS):
+                self.to_sibling(0, n).start()
+            self.out_to(1).start()
+            self.store().start()
+            self.out_home().go_on()
+
+    def step(self, n):
         @self.at_source
         def _():
-            self.own_to_mate().wait_recv()
-            self.to_sibling(1).start()
-
-    def relay_others(self):
-        @self.at_source
-        def _():
-            for n in range(2):
-                self.passed(n).wait_recv()
-                pl.when(self.is_gateway)(lambda n=n: self.passed(n).start())
-                self.to_sibling(2 + n).start()
-            for i in range(3):
-
-                @pl.when(jnp.logical_not(self.owns(i)))
-                def _(i=i):
-                    self.out_to(i, 0).wait_recv()
-                    self.out_to(i, 1, True).start()
+            for b in range(2):
+                self.passed(b, n).wait_recv()
+                pl.when(self.is_gateway)(lambda b=b: self.passed(b, n).start())
+                self.to_sibling(2 + b, n).start()
+            self.to_mate(n).wait_recv()
+            self.to_sibling(1, n).start()
 
     def finish(self):
         @self.at_source
         def _():
-            self.own_to_mate().wait_send()
-            self.stage_to_gateway().wait_send()
-            for n in range(2):
-                pl.when(self.is_gateway)(lambda n=n: self.passed(n).wait_send())
-            for n in range(4):
-                self.to_sibling(n).wait_send()
-            for i in range(3):
-                self.out_to(i, 1).wait_send()
-
-                @pl.when(self.owns(i))
-                def _(i=i):
-                    self.out_to(i, 0).wait_send()
-                    self.out_local(i).wait()
+            self.out_to(0).wait_recv()
+            self.out_to(2).start()
+            for n in range(self.PARTS):
+                self.to_gateway(n).wait_send()
+                self.to_mate(n).wait_send()
+                for c in range(2):
+                    pl.when(self.is_gateway)(lambda c=c, n=n: self.passed(c, n).wait_send())
+                for b in range(4):
+                    self.to_sibling(b, n).wait_send()
+            self.store().wait()
+            self.out_home().end()
+            for n in range(3):
+                self.out_to(n).wait_send()
 
         @pl.when(self.spot.s != self.layer)
         def _():
-            for n in range(4):
-                self.to_sibling(n).wait_recv()
-            for i in range(3):
-                self.out_to(i, 1).wait_recv()
+            for b in range(4):
+                for n in range(self.PARTS):
+                    self.to_sibling(b, n).wait_recv()
+            for n in (1, 2):
+                self.out_to(n).wait_recv()
 
 
 def take(refs, counts):
@@ -822,28 +848,41 @@
 
 
 def open_kernel(*refs):
-    ins, outs, weight_s, spread_a, spread_b, (pack_send, pack_recv, pack_local) = take(
-        refs, (6, 5, 4, 3, 3, 3)
-    )
-    w_in, dt_in, w_out, pack, tokens, cotangent = ins
+    ins, outs, weight_s, spread_a, spread_b, (own_tokens, own_cot, own_pack, load, *pack_sems) = take(
+        refs, (5, 5, 5, 3, 3, 7)
+    )
+    w_in, w_out, pack, tokens, cotangent = ins
     tile, tile_out, packs, all_tokens, all_cot = outs
     spot = Spot()
-    weights = Weights(spot, 0, w_in, dt_in, w_out, tile, tile_out, weight_s)
-    rows = Spread(spot, tokens.at[spot.s], all_tokens, spread_a)
-    grads = Spread(spot, cotangent.at[spot.s], all_cot, spread_b)
-    pack_here = pltpu.make_async_copy(pack, packs.at[spot.s], pack_local)
-    pack_there = remote(pack, packs.at[spot.s], pack_send, pack_recv, spot.sibling)
+    weights = Weights(spot, 0, w_in, w_out, tile, tile_out, weight_s)
+    rows = Spread(spot, own_tokens, all_tokens, spread_a)
+    grads = Spread(spot, own_cot, all_cot, spread_b)
+    loads = [
+        pltpu.make_async_copy(src, dst, load.at[n])
+        for n, (src, dst) in enumerate(
+            ((tokens.at[spot.s], own_tokens), (cotangent.at[spot.s], own_cot), (pack, own_pack))
+        )
+    ]
+    pack_here = pltpu.make_async_copy(own_pack, packs.at[spot.s], pack_sems[0])
+    pack_there = remote(own_pack, packs.at[spot.s], pack_sems[1], pack_sems[2], spot.sibling)
+    for copy in loads:
+        copy.start()
     weights.begin()
     greet(all_places(spot))
+    for copy in loads:
+        copy.wait()
     rows.start()
+    weights.start()
     pack_here.start()
     pack_there.start()
-    weights.start()
     rows.forward()
-    weights.relay_mate()
     grads.start()
-    weights.relay_others()
+    weights.step(0)
+    weights.step(1)
+    weights.step(2)
     grads.forward()
+    weights.step(3)
+    weights.step(4)
     rows.finish()
     grads.finish()
     weights.finish()
@@ -852,11 +891,11 @@
 
 
 def middle_kernel(*refs):
-    ins, outs, weight_s, sum_s, spread_s = take(refs, (5, 6, 4, 6, 3))
-    w_in, dt_in, w_out, parts, rows_in = ins
+    ins, outs, weight_s, sum_s, spread_s = take(refs, (4, 6, 5, 6, 3))
+    w_in, w_out, parts, rows_in = ins
     tile, tile_out, all_rows, branch, scales, rows_out = outs
     spot = Spot()
-    weights = Weights(spot, 1, w_in, dt_in, w_out, tile, tile_out, weight_s)
+    weights = Weights(spot, 1, w_in, w_out, tile, tile_out, weight_s)
     total = Sum(spot, parts, rows_in.shape[1], sum_s)
     spread = Spread(spot, rows_out, all_rows, spread_s)
     weights.begin()
@@ -864,11 +903,14 @@
     total.start()
     weights.start()
     total.forward()
+    weights.step(0)
     layer_rows(total.finish(), rows_in, branch, scales, rows_out)
     spread.start()
-    weights.relay_mate()
+    weights.step(1)
+    weights.step(2)
     spread.forward()
-    weights.relay_others()
+    weights.step(3)
+    weights.step(4)
     spread.finish()
     total.close()
     weights.finish()
@@ -914,17 +956,294 @@
     return grad, jnp.sum(total * scaled, axis=0, keepdims=True)
 
 
+def add_rows(target, sources, chunk=64):
+    @pl.loop(0, target.shape[0] // chunk)
+    def _(n):
+        rows = pl.ds(pl.multiple_of(n * chunk, chunk), chunk)
+        total = sources[0][rows, :].astype(F32)
+        for source in sources[1:]:
+            total += source[rows, :].astype(F32)
+        target[rows, :] = total.astype(target.dtype)
+
+
+class GradsAcross:
+    ORDER = (4, 0, 1, 2, 3, 5)
+
+    @staticmethod
+    def scratch(shard, columns, wide, width):
+        return [
+            pltpu.VMEM((2, columns, width), BF16),
+            pltpu.VMEM((2, wide, width), BF16),
+            pltpu.VMEM((3, columns, shard), BF16),
+            pltpu.VMEM((THIRD, width), BF16),
+            DMA((6,)),
+            DMA((22,)),
+            DMA((22,)),
+        ]
+
+    @staticmethod
+    def results(shard, width):
+        return [((2, 4 * THIRD, shard), BF16), ((SHARED + HEADS, shard), BF16), ((THIRD, width), BF16)]
+
+    def __init__(self, spot, layer, w_grad, wo_grad, results, scratch):
+        self.spot, self.layer, self.w_grad, self.wo_grad = spot, layer, w_grad, wo_grad
+        self.reduced, self.shared, self.out = results
+        self.cores, self.cores_out, self.planes, self.mate_out, self.local, self.send, self.recv = scratch
+        self.shard = self.planes.shape[2]
+        self.others = 2 * (1 - spot.half)
+
+    def here(self, step):
+        pl.when(self.spot.s == self.layer)(step)
+
+    def rows(self, n):
+        _, first, size = tile_parts(self.spot, 0)[n]
+        return pl.ds(first, size)
+
+    def columns(self, z):
+        return pl.ds(pl.multiple_of(z * self.shard, LANES), self.shard)
+
+    def pair(self, n, slot):
+        if n == 5:
+            return self.wo_grad, self.cores_out.at[slot]
+        return self.w_grad.at[self.rows(n)], self.cores.at[slot, self.rows(n)]
+
+    def core_copy(self, n):
+        source, target = self.pair(n, 1)
+        return remote(source, target, self.send.at[n], self.recv.at[n], self.spot.sibling)
+
+    def own_copy(self, n):
+        return pltpu.make_async_copy(*self.pair(n, 0), self.local.at[n])
+
+    def begin(self):
+        @self.here
+        def _():
+            for n in self.ORDER:
+                self.own_copy(n).start()
+
+        @pl.when(self.spot.s != self.layer)
+        def _():
+            for at, n in enumerate(self.ORDER):
+                if at >= 2:
+                    self.core_copy(self.ORDER[at - 2]).wait_send()
+                self.core_copy(n).start()
+            for n in self.ORDER[-2:]:
+                self.core_copy(n).wait_send()
+
+    def plane_copy(self, c, n):
+        spot, rows = self.spot, self.rows(n)
+        z = spot.mate if c == 2 else self.others + c
+        slot = 2 if c == 2 else spot.lo
+        place = spot.at_mate if c == 2 else spot.column(z)
+        return remote(
+            self.cores.at[0, rows, self.columns(z)], self.planes.at[slot, rows],
+            self.send.at[6 + 3 * n + c], self.recv.at[6 + 3 * n + slot], place,
+        )
+
+    def came(self, c, n):
+        part = self.planes.at[c, self.rows(n)]
+        j = 6 + 3 * n + c
+        return remote(part, part, self.send.at[j], self.recv.at[j], self.spot.at_mate)
+
+    def out_rows(self, lo):
+        return pl.ds(pl.multiple_of(lo * THIRD, 64), THIRD)
+
+    def mate_copy(self):
+        source = self.cores_out.at[0, self.out_rows(1 - self.spot.lo)]
+        return remote(source, self.mate_out, self.send.at[21], self.recv.at[21], self.spot.at_mate)
+
+    def sent(self, n):
+        @self.here
+        def _():
+            for c in range(3):
+                self.plane_copy(c, n).wait_send()
+
+    def to_planes(self, n):
+        @self.here
+        def _():
+            self.own_copy(n).wait()
+            self.core_copy(n).wait_recv()
+            if n == 5:
+                add_rows(self.cores_out.at[0], [self.cores_out.at[0], self.cores_out.at[1]])
+                self.mate_copy().start()
+                return
+            own, sibling = self.cores.at[0, self.rows(n)], self.cores.at[1, self.rows(n)]
+            add_rows(own, [own, sibling], 48 if n < 4 else 16)
+            for c in range(3):
+                self.plane_copy(c, n).start()
+
+    def gather(self, n):
+        @self.here
+        def _():
+            if n == 5:
+                self.mate_copy().wait_recv()
+                add_rows(self.out, [self.cores_out.at[0, self.out_rows(self.spot.lo)], self.mate_out], 48)
+                return
+            for c in range(3):
+                self.came(c, n).wait_recv()
+            _, first, size = tile_parts(self.spot, 0)[n]
+            mine = self.columns(self.spot.z)
+            chunk = 48 if n < 4 else 16
+
+            @pl.loop(0, size // chunk)
+            def _(r):
+                rows = pl.ds(pl.multiple_of(first + r * chunk, 16), chunk)
+                own = self.cores[0, rows, mine].astype(F32) + self.planes[2, rows, :].astype(F32)
+                other = self.planes[0, rows, :].astype(F32) + self.planes[1, rows, :].astype(F32)
+                if n < 4:
+                    self.reduced[0, rows, :] = own.astype(BF16)
+                    self.reduced[1, rows, :] = other.astype(BF16)
+                else:
+                    rows = pl.ds(pl.multiple_of(r * chunk, 16), chunk)
+                    self.shared[rows, :] = (own + other).astype(BF16)
+
+    def finish(self):
+        @self.here
+        def _():
+            self.mate_copy().wait_send()
+
+
+class GradsAround:
+    @staticmethod
+    def scratch(shard):
+        return [
+            pltpu.VMEM((4, SHARED + HEADS, shard), BF16),
+            DMA((11,)),
+            DMA((34,)),
+            DMA((34,)),
+        ]
+
+    def __init__(self, spot, results, final, final_out, scratch):
+        self.spot, self.final, self.final_out = spot, final, final_out
+        self.reduced, self.shared, self.out = results
+        self.sums, self.local, self.send, self.recv = scratch
+
+    def region(self, k, i, n):
+        q = self.spot.q if k == 0 else self.spot.around[k]
+        half = self.spot.half if i == 0 else 1 - self.spot.half
+        at = n // 2 * INNER + THIRD * (8 * half + 4 * (n % 2) + q)
+        return self.final.at[pl.ds(pl.multiple_of(at, 64), THIRD)]
+
+    def copy(self, k, i, n):
+        source = self.reduced.at[i, pl.ds(n * THIRD, THIRD)]
+        target = self.region(0, i, n)
+        j = 4 * i + n
+        if k == 0:
+            return pltpu.make_async_copy(source, target, self.local.at[j])
+        if k < 3:
+            j += 8 * (k - 1)
+            return remote(source, target, self.send.at[j], self.recv.at[j], self.spot.plane(k))
+        source = target = self.region(1 if i == 0 else 2, i, n)
+        place = self.spot.plane(2 if i == 0 else 1)
+        return remote(source, target, self.send.at[16 + j], self.recv.at[16 + j], place)
+
+    def send_part(self, n):
+        for i in range(2):
+            for k in (1, 2, 0):
+                self.copy(k, i, n).start()
+
+    def pass_part(self, n):
+        for i in range(2):
+            self.copy(1 + i, i, n).wait_recv()
+            self.copy(3, i, n).start()
+
+    def out_region(self, k, i):
+        q = self.spot.q if k == 0 else self.spot.around[k]
+        size = THIRD if i is None else THIRD // 2
+        at = q * THIRD + (0 if i is None else i * size)
+        return self.final_out.at[pl.ds(pl.multiple_of(at, 32), size)]
+
+    def out_copy(self, k, i=None):
+        target = self.out_region(0, None)
+        if k == 0:
+            return pltpu.make_async_copy(self.out, target, self.local.at[8])
+        if k < 3:
+            return remote(self.out, target, self.send.at[23 + k], self.recv.at[23 + k], self.spot.plane(k))
+        part = self.out_region(1 + i, i)
+        return remote(part, part, self.send.at[26 + i], self.recv.at[26 + i], self.spot.plane(2 - i))
+
+    def send_out(self):
+        for k in (1, 2, 0):
+            self.out_copy(k).start()
+
+    def pass_out(self):
+        for i in range(2):
+            self.out_copy(1 + i).wait_recv()
+            self.out_copy(3, i).start()
+
+    def shared_copy(self, k):
+        source = self.shared if k == 1 else self.sums.at[1]
+        target = self.sums.at[0 if k == 1 else 2]
+        return remote(source, target, self.send.at[27 + k], self.recv.at[27 + k], self.spot.plane(k))
+
+    def shared_home(self):
+        tail = self.final.at[pl.ds(2 * INNER, SHARED + HEADS)]
+        return pltpu.make_async_copy(self.sums.at[3], tail, self.local.at[9])
+
+    def shared_step(self, n):
+        if n > 0:
+            self.shared_copy(n).wait_recv()
+            sources = [self.shared, self.sums.at[0]] if n == 1 else [self.sums.at[1], self.sums.at[2]]
+            add_rows(self.sums.at[1 if n == 1 else 3], sources, 16)
+        if n < 2:
+            self.shared_copy(n + 1).start()
+        else:
+            self.shared_home().start()
+
+    def finish(self):
+        for i in range(2):
+            for n in range(4):
+                self.copy(2 - i, i, n).wait_recv()
+                self.copy(3, i, n).wait_recv()
+                for k in (1, 2, 3):
+                    self.copy(k, i, n).wait_send()
+                self.copy(0, i, n).wait()
+            self.out_copy(3, i).wait_recv()
+            self.out_copy(3, i).wait_send()
+        for k in (1, 2):
+            self.out_copy(k).wait_send()
+            self.shared_copy(k).wait_send()
+        self.out_copy(0).wait()
+        self.shared_home().wait()
+
+
+class SmallSum:
+    @staticmethod
+    def scratch(pack):
+        return [pltpu.VMEM((6, 8, pack), F32), DMA((5,)), DMA((5,))]
+
+    def __init__(self, spot, scratch):
+        self.spot = spot
+        self.small, self.send, self.recv = scratch
+
+    def copy(self, n):
+        spot = self.spot
+        place = [spot.sibling, spot.at_mate, spot.at_twin, spot.plane(1), spot.plane(2)][n]
+        return remote(self.small.at[0], self.small.at[1 + n], self.send.at[n], self.recv.at[n], place)
+
+    def start(self, n, value):
+        self.small[0] = value
+        self.copy(n).start()
+
+    def end(self, n):
+        self.copy(n).wait()
+        return self.small[1 + n]
+
+
 def turn_kernel(*refs):
-    ins, outs, sum_s, last_s, spread_s, (payload,) = take(refs, (8, 4, 6, 6, 3, 1))
-    parts, last_parts, rows_in, grad_out, packs, branch, scales, last_in = ins
-    all_rows, grad_rows, grad_gain, last_rows = outs
+    ins, outs, sum_s, last_s, spread_s, across_s, (payload,) = take(refs, (10, 7, 6, 6, 3, 7, 1))
+    parts, last_parts, rows_in, grad_out, packs, branch, scales, last_in, w_grad, wo_grad = ins
+    all_rows, grad_rows, grad_gain, last_rows, *results = outs
     spot = Spot()
     width = rows_in.shape[1]
     total = Sum(spot, parts, width, sum_s)
     last = Sum(spot, last_parts, width, last_s)
     spread = Spread(spot, payload, all_rows, spread_s)
-    greet([spot.plane(k) for k in (1, 2, 3)] + [spot.at_twin])
+    across = GradsAcross(spot, 1, w_grad, wo_grad, results, across_s)
+    greet(all_places(spot))
     total.start()
+    across.begin()
+    across.to_planes(4)
+    across.to_planes(0)
     total.forward()
     grad, gain_row = norm_back(total.finish(), rows_in, packs[1, 7:8, :width], grad_out)
     low = grad.astype(BF16)
@@ -939,246 +1258,66 @@
     spread.start()
     last.start()
     spread.forward()
+    for n in (1, 2, 3, 5):
+        across.to_planes(n)
     last.forward()
     spread.finish()
+    for n in GradsAcross.ORDER:
+        across.gather(n)
     layer_rows(last.finish(), last_in, None, None, last_rows)
+    for n in range(5):
+        across.sent(n)
+    across.finish()
     total.close()
     last.close()
 
 
-def add_rows(target, sources, chunk=64):
-    @pl.loop(0, target.shape[0] // chunk)
-    def _(n):
-        rows = pl.ds(pl.multiple_of(n * chunk, chunk), chunk)
-        total = sources[0][rows, :].astype(F32)
-        for source in sources[1:]:
-            total += source[rows, :].astype(F32)
-        target[rows, :] = total.astype(target.dtype)
-
-
-class Grads:
-    @staticmethod
-    def scratch(shard, columns, wide, width):
-        half = columns - SHARED - LANES
-        return [
-            pltpu.VMEM((2, 4 * shard, columns), BF16),
-            pltpu.VMEM((2, wide, width), BF16),
-            pltpu.VMEM((3, shard, columns), BF16),
-            pltpu.VMEM((wide, width), BF16),
-            pltpu.VMEM((2, shard, half), BF16),
-            pltpu.VMEM((4, shard, columns - half), BF16),
-            pltpu.VMEM((shard, columns - half), BF16),
-            pltpu.VMEM((6, 8, XBC), F32),
-            DMA((4,)),
-            DMA((68,)),
-            DMA((68,)),
-        ]
-
-    def __init__(self, spot, w_grads, wo_grads, final, final_out, scratch):
-        self.spot, self.w_grads, self.wo_grads = spot, w_grads, wo_grads
-        self.final, self.final_out = final, final_out
-        (
-            self.cores, self.cores_out, self.planes, self.mate_out, self.reduced, self.shared,
-            self.shared_sum, self.small, self.local, self.send, self.recv,
-        ) = scratch
-        self.rows = self.planes.shape[1]
-        self.others = 2 * (1 - spot.half)
-
-    def block(self, z):
-        return pl.ds(pl.multiple_of(z * self.rows, self.rows), self.rows)
-
-    def core_copy(self, layer, n):
-        if n == 4:
-            source, target = self.wo_grads[layer], self.cores_out.at[1]
-        else:
-            z = [self.others, self.others + 1, self.spot.mate, self.spot.z][n]
-            source = self.w_grads[layer].at[self.block(z)]
-            target = self.cores.at[1, self.block(z)]
-        return remote(source, target, self.send.at[n], self.recv.at[n], self.spot.sibling)
-
-    def own_copy(self, layer, n):
-        pair = [(self.w_grads[layer], self.cores.at[0]), (self.wo_grads[layer], self.cores_out.at[0])][n]
-        return pltpu.make_async_copy(*pair, self.local.at[n])
-
-    def begin(self):
-        for s in range(2):
-
-            @pl.when(self.spot.s == s)
-            def _(s=s):
-                for n in range(5):
-                    self.core_copy(1 - s, n).start()
-                for n in range(2):
-                    self.own_copy(s, n).start()
-
-    def plane_copy(self, n):
-        spot = self.spot
-        if n == 2:
-            slot, place, j = self.planes.at[2], spot.at_mate, 7
-            source = self.cores.at[0, self.block(spot.mate)]
-        else:
-            slot, place, j = self.planes.at[spot.lo], spot.column(self.others + n), 5 + spot.lo
-            source = self.cores.at[0, self.block(self.others + n)]
-        return remote(source, slot, self.send.at[5 + n], self.recv.at[j], place)
-
-    def came(self, n):
-        slot = self.planes.at[n]
-        return remote(slot, slot, self.send.at[5 + n], self.recv.at[5 + n], self.spot.at_mate)
-
-    def owns(self, i, k=0):
-        odd = self.spot.q % 2
-        if k % 2:
-            odd = 1 - odd
-        return self.spot.lo == [0, odd, 1][i]
-
-    def out_rows(self, i):
-        return pl.ds(i * LANES, LANES)
-
-    def mate_copy(self, i):
-        rows = self.out_rows(i)
-        return remote(
-            self.cores_out.at[0, rows], self.mate_out.at[rows],
-            self.send.at[8 + i], self.recv.at[8 + i], self.spot.at_mate,
-        )
-
-    def to_planes(self):
-        for n in range(2):
-            self.own_copy(0, n).wait()
-        for n, z in enumerate((self.others, self.others + 1, self.spot.mate, self.spot.z)):
-            self.core_copy(0, n).wait_recv()
-            rows = self.block(z)
-            own, sibling = self.cores.at[0, rows], self.cores.at[1, rows]
-            add_rows(own, [own, sibling])
-            if n < 3:
-                self.plane_copy(n).start()
-        self.core_copy(0, 4).wait_recv()
-        add_rows(self.cores_out.at[0], [self.cores_out.at[0], self.cores_out.at[1]])
-        for i in range(3):
-            pl.when(jnp.logical_not(self.owns(i)))(lambda i=i: self.mate_copy(i).start())
-
-    def around_copy(self, k, n):
-        i, part, pair = n // 6, n // 3 % 2, n % 3
-        half = self.spot.half if i == 0 else 1 - self.spot.half
-        at = part * INNER + LANES * self.spot.pair(half, pair)
-        source = self.reduced.at[i, :, pl.ds((3 * part + pair) * LANES, LANES)]
-        target = self.final.at[:, pl.ds(pl.multiple_of(at, LANES), LANES)]
-        if k == 0:
-            return pltpu.make_async_copy(source, target, self.send.at[11 + n])
-        j = 11 + 12 * k + n
-        return remote(source, target, self.send.at[j], self.recv.at[j], self.spot.plane(k))
-
-    def shared_copy(self, k):
-        return remote(
-            self.shared.at[0], self.shared.at[k], self.send.at[58 + k], self.recv.at[58 + k], self.spot.plane(k)
-        )
-
-    def out_target(self, i):
-        at = (self.spot.pair(self.spot.half, i) % 6) * LANES
-        return self.final_out.at[pl.ds(pl.multiple_of(at, LANES), LANES)]
-
-    def out_copy(self, k, i, sems):
-        source = self.cores_out.at[0, self.out_rows(i)]
-        if k == 0:
-            return pltpu.make_async_copy(source, self.out_target(i), sems[0].at[i])
-        j = 3 * k + i
-        return remote(source, self.out_target(i), sems[0].at[j], sems[1].at[j], self.spot.plane(k))
-
-    def around(self, out_sems):
-        half = self.reduced.shape[2]
-        self.came(2).wait_recv()
-        own = self.cores.at[0, self.block(self.spot.z)]
-        add_rows(own, [own, self.planes.at[2]])
-        for n in range(2):
-            self.came(n).wait_recv()
-
-        @pl.loop(0, self.rows // 64)
-        def _(n):
-            rows = pl.ds(pl.multiple_of(n * 64, 64), 64)
-            own = self.cores[0, pl.ds(pl.multiple_of(self.spot.z * self.rows + n * 64, 64), 64), :].astype(F32)
-            other = self.planes[0, rows, :].astype(F32) + self.planes[1, rows, :].astype(F32)
-            self.reduced[0, rows, :] = own[:, :half].astype(BF16)
-            self.reduced[1, rows, :] = other[:, :half].astype(BF16)
-            self.shared[0, rows, :] = (own[:, half:] + other[:, half:]).astype(BF16)
-
-        for k in (1, 2, 3):
-            self.shared_copy(k).start()
-        for n in range(12):
-            for k in (1, 2, 3, 0):
-                self.around_copy(k, n).start()
-        for i in range(3):
-
-            @pl.when(self.owns(i))
-            def _(i=i):
-                rows = self.out_rows(i)
-                self.mate_copy(i).wait_recv()
-                total = self.cores_out[0, rows, :].astype(F32) + self.mate_out[rows, :].astype(F32)
-                self.cores_out[0, rows, :] = total.astype(BF16)
-                for k in (1, 2, 3, 0):
-                    self.out_copy(k, i, out_sems).start()
-
-    def small_copy(self, n):
-        spot = self.spot
-        place = [spot.sibling, spot.at_mate, spot.at_twin, spot.plane(1), spot.plane(2)][n]
-        return remote(
-            self.small.at[0], self.small.at[1 + n], self.send.at[62 + n], self.recv.at[62 + n], place
-        )
-
-    def finish(self, out_sems):
-        for k in (1, 2, 3):
-            self.shared_copy(k).wait_recv()
-
-        @pl.loop(0, self.rows // 64)
-        def _(n):
-            rows = pl.ds(pl.multiple_of(n * 64, 64), 64)
-            a, b, c, d = (self.shared[k, rows, :].astype(F32) for k in range(4))
-            self.shared_sum[rows, :] = ((a + b) + (c + d)).astype(BF16)
-
-        tail = self.final.at[:, pl.ds(2 * INNER, self.shared_sum.shape[1])]
-        copy = pltpu.make_async_copy(self.shared_sum, tail, self.local.at[2])
-        copy.start()
-        for n in range(12):
-            for k in (1, 2, 3):
-                self.around_copy(k, n).wait_recv()
-            self.around_copy(0, n).wait()
-        for k in (1, 2, 3):
-            for i in range(3):
-                pl.when(self.owns(i, k))(lambda k=k, i=i: self.out_copy(k, i, out_sems).wait_recv())
-        copy.wait()
-        for n in range(5):
-            self.core_copy(0, n).wait_send()
-        for n in range(3):
-            self.plane_copy(n).wait_send()
-        for k in (1, 2, 3):
-            self.shared_copy(k).wait_send()
-            for n in range(12):
-                self.around_copy(k, n).wait_send()
-        for i in range(3):
-
-            @pl.when(self.owns(i))
-            def _(i=i):
-                for k in (1, 2, 3):
-                    self.out_copy(k, i, out_sems).wait_send()
-                self.out_copy(0, i, out_sems).wait()
-
-            pl.when(jnp.logical_not(self.owns(i)))(lambda i=i: self.mate_copy(i).wait_send())
-
-
 def close_kernel(*refs):
-    ins, outs, sum_s, grads_s, (grad_rows, small_in, send, recv, local, out_send, out_recv) = take(
-        refs, (14, 5, 6, 11, 7)
-    )
-    parts, rows_in, grad_out, packs, first_rows, last_rows, last_grad, *rest = ins
-    w_grads, wo_grads, (small_0, small_1, gain_1) = rest[:2], rest[2:4], rest[4:]
+    ins, outs, sum_s, across_s, results, around_s, small_s, rest = take(refs, (15, 5, 6, 7, 3, 4, 3, 6))
+    parts, rows_in, grad_out, packs, first_rows, last_rows, last_grad, *ins = ins
+    w_grad, wo_grad, small_0, small_1, gain_1, *last_results = ins
     home_rows, home_grads, final, final_out, small_out = outs
+    grad_rows, small_in, send, recv, local, load = rest
     spot = Spot()
     width = rows_in.shape[1]
     total = Sum(spot, parts, width, sum_s)
-    grads = Grads(spot, w_grads, wo_grads, final, final_out, grads_s)
-    out_sems = (out_send, out_recv)
+    across = GradsAcross(spot, 0, w_grad, wo_grad, results, across_s)
+    around = GradsAround(spot, results, final, final_out, around_s)
+    small = SmallSum(spot, small_s)
+    first_core, last_core = pl.when(spot.s == 0), pl.when(spot.s == 1)
+    loads = [
+        pltpu.make_async_copy(src, dst, load.at[n]) for n, (src, dst) in enumerate(zip(last_results, results))
+    ]
+
+    @last_core
+    def _():
+        for copy in loads:
+            copy.start()
+
     greet(all_places(spot))
-    grads.begin()
     total.start()
-    grads.to_planes()
+    across.begin()
+
+    @last_core
+    def _():
+        for copy in loads:
+            copy.wait()
+        around.shared_step(0)
+        for n in range(4):
+            around.send_part(n)
+        around.send_out()
+
+    order = GradsAcross.ORDER
+    for n in order[:3]:
+        across.to_planes(n)
     total.forward()
+    for at in range(3, 6):
+        across.sent(order[at - 3])
+        across.to_planes(order[at])
+    across.gather(4)
+    first_core(lambda: around.shared_step(0))
+    across.gather(0)
+    first_core(lambda: around.send_part(0))
     grad, gain_row = norm_back(total.finish(), rows_in, packs[0, 7:8, :width], grad_out)
     grad_rows[...] = grad.astype(BF16)
     layers = ((first_rows, grad_rows), (last_rows, last_grad))
@@ -1194,8 +1333,7 @@
     small_in[1] = small_1[...]
     small_in[0, 7:8, :width] = gain_row
     small_in[1, 7:8, :width] = gain_1[0:1]
-    grads.small[0] = small_in[1 - spot.s]
-    grads.small_copy(0).start()
+    small.start(0, small_in[1 - spot.s])
     for s in range(2):
 
         @pl.when(spot.s == s)
@@ -1203,16 +1341,34 @@
             for copy in home_copies(s):
                 copy.start()
 
-    grads.around(out_sems)
-    grads.small_copy(0).wait()
-    running = small_in[spot.s] + grads.small[1]
-    for n in range(1, 5):
-        grads.small[0] = running
-        grads.small_copy(n).start()
-        grads.small_copy(n).wait()
-        running = running + grads.small[1 + n]
-    small_out[...] = running
-    grads.finish(out_sems)
+    across.gather(1)
+    first_core(lambda: around.send_part(1))
+    running = small_in[spot.s] + small.end(0)
+    small.start(1, running)
+    around.shared_step(1)
+    around.pass_part(0)
+    across.gather(2)
+    first_core(lambda: around.send_part(2))
+    running = running + small.end(1)
+    small.start(2, running)
+    around.pass_part(1)
+    across.gather(3)
+    first_core(lambda: around.send_part(3))
+    running = running + small.end(2)
+    small.start(3, running)
+    around.shared_step(2)
+    across.gather(5)
+    first_core(around.send_out)
+    around.pass_part(2)
+    running = running + small.end(3)
+    small.start(4, running)
+    around.pass_part(3)
+    around.pass_out()
+    small_out[...] = running + small.end(4)
+    around.finish()
+    for n in order[3:5]:
+        across.sent(n)
+    across.finish()
     for s in range(2):
 
         @pl.when(spot.s == s)
@@ -1244,32 +1400,34 @@
     span, width = tokens.shape[2:]
     heads = HEADS // 8
     wide = heads * HEADDIM
-    columns = 2 * wide + SHARED + LANES
+    columns = 2 * wide + SHARED + HEADS
     shard = w_in.shape[1]
-    odd, third = place % 2, place // 2 * 3
-    ids = 12 * half + third + jnp.stack([2 * odd, 1 + 6 * odd, 6 + 2 * odd]).astype(jnp.int32)
-    dt_in = widened(w_in[0, :, INNER + XBC :], 1, LANES)
+    ids = 8 * half + place + jnp.array([0, 4], jnp.int32)
+    rows_in = w_in[0].T
+    channels = jnp.concatenate(
+        [
+            conv_weight[0, :, :INNER], conv_bias[:, :INNER],
+            jnp.repeat(skip_gain[0], HEADDIM)[None], gate_gain,
+        ]
+    )
+    channels = widened(channels.reshape(7, -1, THIRD), 2, PIECE).reshape(7, -1)
+    shared = jnp.concatenate([conv_weight[0, :, INNER:], conv_bias[:, INNER:], jnp.zeros((2, SHARED))])
     last_row = jnp.concatenate(
         [norm_gain, widened(dt_bias, 1, LANES), widened(a_log, 1, LANES)], axis=1
     )
-    pack = jnp.concatenate(
-        [
-            conv_weight[0],
-            conv_bias,
-            widened(jnp.repeat(skip_gain[0], HEADDIM)[None], 1, XBC),
-            widened(gate_gain, 1, XBC),
-            widened(last_row, 1, XBC),
-        ]
-    )
+    pack = jnp.concatenate([channels, shared], axis=1)
+    pack = jnp.concatenate([pack, widened(last_row, 1, pack.shape[1])])
     group = (2, 4, span, width)
-    weight_outs = [((width, columns), BF16), ((wide, width), BF16)]
-    weight_s = Weights.scratch(shard, columns)
+    weight_outs = [((columns, width), BF16), ((wide, width), BF16)]
+    weight_s = Weights.scratch(columns, shard, width)
     payload = width + LANES
     tile, tile_out, packs, all_rows, all_cot = comm_call(
         open_kernel, 1,
-        [w_in[0], dt_in, w_out[0], pack, tokens[:, 0], cotangent[:, 0]], [ANY] * 6,
-        weight_outs + [((2, 8, XBC), F32), (group, BF16), (group, BF16)], [ANY] * 5,
-        weight_s + Spread.SEMS + Spread.SEMS + [DMA, DMA, DMA], "open",
+        [rows_in, w_out[0], pack, tokens[:, 0], cotangent[:, 0]], [ANY] * 5,
+        weight_outs + [((2,) + pack.shape, F32), (group, BF16), (group, BF16)], [ANY] * 5,
+        weight_s + Spread.SEMS + Spread.SEMS
+        + [pltpu.VMEM((span, width), BF16)] * 2 + [pltpu.VMEM(pack.shape, F32), DMA((3,)), DMA, DMA, DMA],
+        "open",
     )
     own_rows = [lax.dynamic_index_in_dim(tokens[:, 0], section, 0, False)]
     own_cot = lax.dynamic_index_in_dim(cotangent[:, 0], section, 0, False)
@@ -1287,7 +1445,7 @@
     saved = [(normed, kept)]
     tile, tile_out, all_rows, branch, scales, rows = comm_call(
         middle_kernel, 2,
-        [w_in[0], dt_in, w_out[0], cut(parts), own_rows[0]], [ANY] * 4 + [VMEM],
+        [rows_in, w_out[0], cut(parts), own_rows[0]], [ANY] * 3 + [VMEM],
         weight_outs
         + [(group, BF16), ((span, width), F32), ((span, LANES), F32), ((span, width), BF16)],
         [ANY] * 3 + [VMEM] * 3,
@@ -1306,7 +1464,7 @@
     w_grads, wo_grads, small = [None, None], [None, None], [None, None]
 
     def products(l, proj_grad, normed_out, grads):
-        w_grads[l] = dot_tn(saved[l][0].reshape(-1, width), proj_grad.reshape(-1, columns)).astype(BF16)
+        w_grads[l] = dot_tn(proj_grad.reshape(-1, columns), saved[l][0].reshape(-1, width)).astype(BF16)
         wo_grads[l] = dot_tn(normed_out.reshape(-1, wide), grads.reshape(-1, width)).astype(BF16)
 
     parts, proj_grad, normed_out, small[1] = run_backward(
@@ -1314,12 +1472,18 @@
     )
     products(1, proj_grad, normed_out, joined(all_cot))
     rows_spec = ((span, width), BF16)
-    all_grads, last_grad, gain_1, last_rows = comm_call(
+    results = GradsAcross.results(shard, width)
+    across_s = GradsAcross.scratch(shard, columns, wide, width)
+    all_grads, last_grad, gain_1, last_rows, *last_results = comm_call(
         turn_kernel, 4,
-        [cut(parts), cut(last_parts), own_rows[1], own_cot, packs, branch, scales, own_rows[1]],
-        [ANY, ANY] + [VMEM] * 6,
-        [((2, 4, span, payload), BF16), rows_spec, ((8, width), F32), rows_spec], [ANY] + [VMEM] * 3,
-        Sum.scratch(span, width) + Sum.scratch(span, payload) + Spread.SEMS
+        [
+            cut(parts), cut(last_parts), own_rows[1], own_cot, packs, branch, scales, own_rows[1],
+            w_grads[1], wo_grads[1],
+        ],
+        [ANY, ANY] + [VMEM] * 6 + [ANY] * 2,
+        [((2, 4, span, payload), BF16), rows_spec, ((8, width), F32), rows_spec] + results,
+        [ANY] + [VMEM] * 6,
+        Sum.scratch(span, width) + Sum.scratch(span, payload) + Spread.SEMS + across_s
         + [pltpu.VMEM((span, payload), BF16)], "turn",
     )
     all_grads = joined(all_grads)
@@ -1327,37 +1491,39 @@
         heads, wide, all_grads, None, "columns", saved[0][1], *tiles[0], (ids, packs[0])
     )
     products(0, proj_grad, normed_out, all_grads[..., :width])
-    final_columns = 2 * INNER + SHARED + LANES
     home_rows, home_grads, final, final_out, small = comm_call(
         close_kernel, 5,
         [
             cut(parts), own_rows[0], last_grad, packs, own_rows[1], last_rows, last_grad,
-            *w_grads, *wo_grads, *small, gain_1,
+            w_grads[0], wo_grads[0], *small, gain_1, *last_results,
         ],
-        [ANY] + [VMEM] * 6 + [ANY] * 4 + [VMEM] * 3,
+        [ANY] + [VMEM] * 6 + [ANY] * 2 + [VMEM] * 3 + [ANY] * 3,
         [
             ((2, span, width), BF16), ((2, span, width), BF16),
-            ((shard, final_columns), BF16), (w_out.shape[1:], BF16), ((8, XBC), F32),
+            ((2 * INNER + SHARED + HEADS, shard), BF16), (w_out.shape[1:], BF16), (pack.shape, F32),
         ],
         [ANY] * 4 + [VMEM],
-        Sum.scratch(span, width) + Grads.scratch(shard, columns, wide, width)
+        Sum.scratch(span, width) + across_s + [pltpu.VMEM(*r) for r in results]
+        + GradsAround.scratch(shard) + SmallSum.scratch(pack.shape[1])
         + [
-            pltpu.VMEM((span, width), BF16), pltpu.VMEM((2, 8, XBC), F32),
-            DMA((2,)), DMA((2,)), DMA((2,)), DMA((12,)), DMA((12,)),
+            pltpu.VMEM((span, width), BF16), pltpu.VMEM((2,) + pack.shape, F32),
+            DMA((2,)), DMA((2,)), DMA((2,)), DMA((3,)),
         ],
         "close",
     )
+    by_channel = small[:7, :-SHARED].reshape(7, -1, PIECE)[:, :, :THIRD].reshape(7, INNER)
+    conv_rows = jnp.concatenate([by_channel[: CONV + 1], small[: CONV + 1, -SHARED:]], axis=1)
     return (
         home_rows[None, :, None],
         home_grads[None, :, None],
         small[7:8, :width],
-        final[None, :, : INNER + XBC + HEADS].astype(F32),
-        small[None, :CONV],
-        small[CONV : CONV + 1],
+        final.astype(F32).T[None],
+        conv_rows[None, :CONV],
+        conv_rows[CONV:],
         small[7:8, DT_AT : DT_AT + HEADS],
         small[7:8, RATE_AT : RATE_AT + HEADS],
-        small[5:6, :INNER].reshape(1, HEADS, HEADDIM).sum(-1),
-        small[6:7, :INNER],
+        by_channel[5].reshape(HEADS, HEADDIM).sum(-1)[None],
+        by_channel[6:7],
         final_out[None].astype(F32),
     )
 
@@ -1383,7 +1549,7 @@
     dt_part = widened(plan.take(shard[:, INNER + XBC :], 1, place), 2, LANES)
     tile = jnp.concatenate([gate_part, x_part, shared_part, dt_part], axis=2)
     tile = jnp.repeat(tile, plan.mates, axis=0)
-    tile = lax.all_to_all(tile, "fsdp", 0, 0, tiled=True).reshape(width, -1)
+    tile = lax.all_to_all(tile, "fsdp", 0, 0, tiled=True).reshape(width, -1).T
     w_tiles = lax.all_gather(tile, "section", axis=0)
     if plan.pieces == plan.mates:
         piece = w_out[0].reshape(plan.seq, -1, width)

time: 544 us -> 388 us (0.71)
  Pallas kernels: 490 us -> 343 us
  local copies, waits for them, and re-layouts: 28 us -> 14.1 us
    pallas_call x5, Pallas kernels: 438 us -> 292 us  [comm_call(): pl.pallas_call(kernel, out_shape=[jax.ShapeDtypeStruct(s, t) for s, t in...]
    unnamed x42 -> x23, local copies, waits for them, and re-layouts: 20 us -> 2.16 us
    convert_element_type x1 -> x0, other arithmetic: 6.91 us -> none  [fast_shards(): final[None, :, :INNER + XBC + HEADS].astype(F32)]
where the time goes in v3:
time: 388 us; the launch traced here: 387 us
  Pallas kernels  343 us (88%)
  other arithmetic  15.7 us (4%)
  local copies, waits for them, and re-layouts  14.1 us (4%)
  matrix products  13.2 us (3%)
    pallas_call x5, Pallas kernels, comm_call(): pl.pallas_call(kernel, out_shape=[jax.ShapeDtypeStruct(s, t) for s, t in...  292 us
    pallas_call x2, Pallas kernels, run_backward(): pl.pallas_call(partial(backward_kernel, heads, len(params), aux_kind), gr...  27.8 us
    pallas_call x2, Pallas kernels, run_forward(): pl.pallas_call(partial(forward_kernel, heads, len(params), grad_rows is n...  23.3 us
    dot_general x4, matrix products, dot(): lax.dot_general(left, right, (contract, ((), ())), preferred_element_type...  13.2 us

profile of v3, /device:TPU:0, one launch (start us, length us, event | category | flops | bytes accessed | tf_op | source)
XLA Modules:
  0.0 386.8 jit_solution(15083396033773562045)
XLA Ops:
  1.7 1.3 reduce.11
  3.0 0.7 slice.67
  3.7 0.7 slice_bitcast_fusion.2
  4.4 0.7 fusion.8
  5.2 1.4 reduce.10
  6.7 0.7 slice_reduce_fusion
  7.6 0.8 slice.64
  8.6 0.7 select_maximum_fusion.refs_2_
  9.3 1.8 dynamic-slice_bitcast_fusion
  11.1 56.1 %open.1 = (bf16[1072,1536]{1,0:T(8,128)(2,1)}, bf16[384,1536]{1,0:T(8,128)(2,1)}, f32[2,8,4352]{2,1,0:T(8,128)}, bf16[2,4,64,1536]{3,2,1,0:T(8,128)(2,1)}, bf16[2,4,64,1536]{3,2,1,0:T(8,128)(2,1)}) custom-call(bf16[6448,384]{1,0:T(8,128)(2,1)} %bitcast.68, bf16[768,1536]{1,0:T(8,128)(2,1)} %bitcast.70, f32[8,4352]{1,0:T(8,128)} %select_maximum_fusion.refs_2_, ...), custom_call_target="tpu_custom_call" | custom-call | tf_op jit(solution)/shard_map/open/pallas_call | solution.py:1383
  67.2 1.7 slice_bitcast_fusion
  68.9 11.0 %forward.2 = (bf16[2,256,1664]{2,1,0:T(8,128)(2,1)}, f32[2,8,256]{2,1,0:T(8,128)}, bf16[2,256,1536]{2,1,0:T(8,128)(2,1)}, f32[2,256,384]{2,1,0:T(8,128)}, bf16[2...) custom-call(bf16[2,256,1536]{2,1,0:T(8,128)(2,1)} %bitcast.79, ...), custom_call_target="tpu_custom_call" | custom-call | tf_op jit(solution)/shard_map/forward/pallas_call | solution.py:444
  80.0 59.4 %middle.1 = (bf16[1072,1536]{1,0:T(8,128)(2,1)}, bf16[384,1536]{1,0:T(8,128)(2,1)}, bf16[2,4,64,1536]{3,2,1,0:T(8,128)(2,1)}, f32[64,1536]{1,0:T(8,128)}, f32[64,128]{1,0:T(8,128)}, /*index=5*/bf16[64,1536]{1,0:T(8,128)(2,1)}) custom-call(bf16[6448,384]{1,0:T(8,128)(2,1)} %bitcast.69, bf16[768,1536]{1,0:T(8,128)(2,1)} %bitcast.71, ...), custom_call_target="tpu_custom_call" | custom-call | tf_op jit(solution)/shard_map/middle/pallas_call | solution.py:1383
  139.3 12.3 %forward.3 = (bf16[2,256,1664]{2,1,0:T(8,128)(2,1)}, f32[2,8,256]{2,1,0:T(8,128)}, bf16[2,256,1536]{2,1,0:T(8,128)(2,1)}, f32[2,256,384]{2,1,0:T(8,128)}, bf16[2...) custom-call(bf16[2,256,1536]{2,1,0:T(8,128)(2,1)} %bitcast.80, ...), custom_call_target="tpu_custom_call" | custom-call | tf_op jit(solution)/shard_map/forward/pallas_call | solution.py:444
  151.6 8.8 %sums.1.refs_1_ = f32[2,8,256]{2,1,0:T(8,128)} custom-call(f32[2,8,256]{2,1,0:T(8,128)} %get-tuple-element.66.mine_ref), custom_call_target="tpu_custom_call" | custom-call | tf_op jit(solution)/shard_map/sums/pallas_call | solution.py:1383
  160.5 13.9 %backward.2 = (bf16[2,256,1536]{2,1,0:T(8,128)(2,1)}, bf16[2,256,1072]{2,1,0:T(8,128)(2,1)}, bf16[2,256,384]{2,1,0:T(8,128)(2,1)}, f32[8,4352]{1,0:T(8,128)}) custom-call(bf16[2,256,1536]{2,1,0:T(8,128)(2,1)} %bitcast.73, f32[2,8,256]{2,1,0:T(8,128)} %sums.1.refs_1_, f32[2,256,384]{2,1,0:T(8,128)} %get-tuple-element.67.refs_2_, ...), custom_call_target="tpu_custom_call" | custom-call | tf_op jit(solution)/shard_map/backward/pallas_call | solution.py:466
  174.4 3.0 convolution_convert_fusion.refs_9_
  177.4 3.6 fusion.refs_8_
  181.0 62.9 %turn.1 = (bf16[2,4,64,1664]{3,2,1,0:T(8,128)(2,1)}, bf16[64,1536]{1,0:T(8,128)(2,1)}, f32[8,1536]{1,0:T(8,128)}, bf16[64,1536]{1,0:T(8,128)(2,1)}, bf16[2,768,3...) custom-call(bf16[2,4,64,1536]{3,2,1,0:T(8,128)(2,1)} %bitcast.82, ...), custom_call_target="tpu_custom_call" | custom-call | tf_op jit(solution)/shard_map/turn/pallas_call | solution.py:1383
  243.9 14.0 %backward.3 = (bf16[2,256,1536]{2,1,0:T(8,128)(2,1)}, bf16[2,256,1072]{2,1,0:T(8,128)(2,1)}, bf16[2,256,384]{2,1,0:T(8,128)(2,1)}, f32[8,4352]{1,0:T(8,128)}) custom-call(bf16[2,256,1664]{2,1,0:T(8,128)(2,1)} %bitcast.75, f32[2,256,384]{2,1,0:T(8,128)} %get-tuple-element.81.refs_1_, bf16[2,256,384]{2,1,0:T(8,128)(2,1)} %get-tuple-element.82.refs_2_, ...), custom_call_target="tpu_custom_call" | custom-call | tf_op jit(solution)/shard_map/backward/pallas_call | solution.py:466
  257.9 2.9 fusion.2.refs_8_
  260.9 3.6 fusion.1.refs_7_
  264.5 104.6 %close.1 = (bf16[2,64,1536]{2,1,0:T(8,128)(2,1)}, bf16[2,64,1536]{2,1,0:T(8,128)(2,1)}, bf16[6448,384]{1,0:T(8,128)(2,1)}, bf16[768,1536]{1,0:T(8,128)(2,1)}, f32[8,4352]{1,0:T(8,128)}) custom-call(bf16[2,4,64,1536]{3,2,1,0:T(8,128)(2,1)} %bitcast.81, bf16[64,1536]{1,0:T(8,128)(2,1)} %get-tuple-element.132.refs_3_.refs_1_, ...), custom_call_target="tpu_custom_call" | custom-call | tf_op jit(solution)/shard_map/close/pallas_call | solution.py:1383
  369.1 1.2 fusion.9
  370.3 1.4 slice.71
  371.7 0.7 slice.75
  372.4 0.9 slice.72
  373.4 0.7 slice.82
  376.1 4.6 %bitcast_convert_fusion = f32[1,768,1536]{2,1,0:T(8,128)} fusion(bf16[768,1536]{1,0:T(8,128)(2,1)} %get-tuple-element.102), kind=kLoop, calls=%fused_computation.8 | loop fusion | flops 1179648 | bytes 7077888 | tf_op jit(solution)/shard_map/convert_element_type | solution.py:1527
  380.8 4.5 %convert_bitcast_fusion = f32[1,384,6448]{1,2,0:T(8,128)} fusion(bf16[6448,384]{1,0:T(8,128)(2,1)S(1)} %copy-done.1), kind=kLoop, calls=%fused_computation | loop fusion | flops 2476032 | bytes 14856192 | tf_op jit(solution)/shard_map/broadcast_in_dim | solution.py:1520
  385.3 0.7 copy.42
  386.1 0.7 copy.43
  (37 shorter events, 3.7 us)
Async XLA Ops:
  160.5 13.9 %copy-start = (bf16[2,4,64,1536]{3,2,1,0:T(8,128)(2,1)S(1)}, bf16[2,4,64,1536]{3,2,1,0:T(8,128)(2,1)}, u32[]{:S(2)}) copy-start(bf16[2,4,64,1536]{3,2,1,0:T(8,128)(2,1)} %get-tuple-element.57) | copy-start | bytes 4718596
  174.3 3.1 copy-start.6
  174.4 3.1 copy-start.7
  243.9 14.0 %copy-start.2 = (bf16[2,4,64,1664]{3,2,1,0:T(8,128)(2,1)S(1)}, bf16[2,4,64,1664]{3,2,1,0:T(8,128)(2,1)}, u32[]{:S(2)}) copy-start(bf16[2,4,64,1664]{3,2,1,0:T(8,128)(2,1)} %get-tuple-element.80) | copy-start | bytes 5111812
  257.9 3.0 copy-start.5
  257.9 3.0 copy-start.8
  376.1 4.7 %copy-start.1 = (bf16[6448,384]{1,0:T(8,128)(2,1)S(1)}, bf16[6448,384]{1,0:T(8,128)(2,1)}, u32[]{:S(2)}) copy-start(bf16[6448,384]{1,0:T(8,128)(2,1)} %get-tuple-element.101) | copy-start | bytes 14856196
  380.8 4.5 %copy-start.4 = (bf16[2,64,1536]{2,1,0:T(8,128)(2,1)S(1)}, bf16[2,64,1536]{2,1,0:T(8,128)(2,1)}, u32[]{:S(2)}) copy-start(bf16[2,64,1536]{2,1,0:T(8,128)(2,1)} %get-tuple-element.98) | copy-start | bytes 1179652
  380.8 5.3 %copy-start.3 = (bf16[2,64,1536]{2,1,0:T(8,128)(2,1)S(1)}, bf16[2,64,1536]{2,1,0:T(8,128)(2,1)}, u32[]{:S(2)}) copy-start(bf16[2,64,1536]{2,1,0:T(8,128)(2,1)} %get-tuple-element.99) | copy-start | bytes 1179652

commit v4 on v3

--- a/solution.py
+++ b/solution.py
@@ -27,6 +27,11 @@
 F32 = jnp.float32
 
 
+def take(refs, counts):
+    refs = list(refs)
+    return [[refs.pop(0) for _ in range(n)] for n in counts]
+
+
 def dot(left, right, contract=((1,), (0,)), precision=None):
     return lax.dot_general(
         left, right, (contract, ((), ())), preferred_element_type=F32, precision=precision
@@ -110,25 +115,25 @@
     return result.astype(BF16)
 
 
-def selection(ids_ref):
+def selection(ids):
     rows = lax.broadcasted_iota(jnp.int32, (HEADS, LANES), 0)
     columns = lax.broadcasted_iota(jnp.int32, (HEADS, LANES), 1)
     target = jnp.full((HEADS, LANES), -1, jnp.int32)
     for j in range(2):
         here = (columns >= 3 * j) & (columns < 3 * j + 3)
-        target = jnp.where(here, columns + 3 * (ids_ref[j] - j), target)
+        target = jnp.where(here, columns + 3 * (ids[j] - j), target)
     return (rows == target).astype(F32)
 
 
-def piece_lanes(ids_ref, j):
-    return pl.ds(pl.multiple_of(ids_ref[j] * PIECE, PIECE), PIECE)
+def piece_lanes(ids, j):
+    return pl.ds(pl.multiple_of(ids[j] * PIECE, PIECE), PIECE)
 
 
 def load_params(refs):
     if len(refs) == 2:
-        ids_ref, pack_ref = refs
-        sel = selection(ids_ref)
-        ch = jnp.concatenate([pack_ref[:, piece_lanes(ids_ref, j)][:, :THIRD] for j in range(2)], axis=1)
+        ids, pack_ref = refs
+        sel = selection(ids)
+        ch = jnp.concatenate([pack_ref[:, piece_lanes(ids, j)][:, :THIRD] for j in range(2)], axis=1)
         rows = [pack_ref[7:8, at : at + HEADS] for at in (DT_AT, RATE_AT)]
         dtp = dot(stacked(rows, 8), sel, precision=HIGHEST)
         return pack_ref[7:8, :GAIN_END], ch, pack_ref[:, -SHARED:], dtp, sel.astype(BF16)
@@ -136,30 +141,31 @@
     return gain_ref[...], ch_ref[...], bc_ref[...], dtp_ref[...], None
 
 
-def forward_kernel(heads, n_params, with_grad, *refs):
+def forward_kernel(heads, *refs):
     u_ref, w_ref, wo_ref, *refs = refs
-    gain, ch, bc, dtp, sel = load_params(refs[:n_params])
-    refs = refs[n_params:]
-    if with_grad:
-        h_ref, *refs = refs
-    out_ref, sums_ref, normed_ref, gate_ref, xraw_ref, bcraw_ref, dtraw_ref, mixed_ref = refs
+    forward_rows(heads, load_params(refs[:4]), 0, u_ref, w_ref, wo_ref, None, refs[4:])
+
+
+def forward_rows(heads, params, i, u_ref, w_ref, wo_ref, h_ref, outs):
+    gain, ch, bc, dtp, sel = params
+    out_ref, sums_ref, normed_ref, gate_ref, xraw_ref, bcraw_ref, dtraw_ref, mixed_ref = outs
     length, width = u_ref.shape[1:]
     wide = ch.shape[1]
     blocks = length // SPAN
-    rows = u_ref[0].astype(F32)
+    rows = u_ref[i].astype(F32)
     scale = lax.rsqrt(jnp.mean(rows * rows, axis=-1, keepdims=True) + NORM_EPS)
     normed = (rows * scale * gain).astype(BF16)
-    normed_ref[0] = normed
+    normed_ref[i] = normed
     gate = dot_nt(normed, w_ref[:wide])
-    gate_ref[0] = gate
+    gate_ref[i] = gate
     x_raw = dot_nt(normed, w_ref[wide : 2 * wide]).astype(BF16)
-    xraw_ref[0] = x_raw
+    xraw_ref[i] = x_raw
     rest = dot_nt(normed, w_ref[2 * wide :]).astype(BF16)
-    bcraw_ref[0] = rest[:, :SHARED]
+    bcraw_ref[i] = rest[:, :SHARED]
     dt_raw = rest[:, SHARED:]
     if sel is not None:
         dt_raw = dot(dt_raw, sel).astype(BF16)
-    dtraw_ref[0] = dt_raw
+    dtraw_ref[i] = dt_raw
     conv_x = conv_sum(x_raw.astype(F32), ch)
     act_x = (conv_x * sigmoid(conv_x)).astype(BF16)
     conv_bc = conv_sum(rest[:, :SHARED].astype(F32), bc)
@@ -201,51 +207,63 @@
                 parts.append(jnp.zeros_like(parts[0]))
             within = jnp.where(lower, parts[0], parts[1])
             mixed = within + ch[5:6, lanes] * x_pair.astype(F32)
-            mixed_ref[0, span, lanes] = mixed.astype(BF16)
-    gated = mixed_ref[0].astype(F32) * (gate * sigmoid(gate))
+            mixed_ref[i, span, lanes] = mixed.astype(BF16)
+    gated = mixed_ref[i].astype(F32) * (gate * sigmoid(gate))
     square = jnp.sum(gated * gated, axis=-1, keepdims=True)
     scaled = gated * ch[6:7]
-    out_ref[0, :, :width] = dot(scaled.astype(BF16), wo_ref[...]).astype(BF16)
+    out_ref[i, :, :width] = dot(scaled.astype(BF16), wo_ref[...]).astype(BF16)
     if sel is None:
-        sums_ref[0] = jnp.broadcast_to(square, sums_ref.shape[1:])
+        sums_ref[i] = jnp.broadcast_to(square, sums_ref.shape[1:])
         return
-    out_ref[0, :, width:] = split_three(square)
-    if with_grad:
-        grad_no = dot_nt(h_ref[0], wo_ref[...])
+    out_ref[i, :, width:] = split_three(square)
+    if h_ref is not None:
+        grad_no = dot_nt(h_ref[i], wo_ref[...])
         cross = jnp.sum(grad_no * scaled, axis=-1, keepdims=True)
         lane_ids = lax.broadcasted_iota(jnp.int32, (length, LANES), 1)
         both = jnp.where(lane_ids == 0, square, jnp.where(lane_ids == 1, cross, 0.0))
-        sums_ref[0] = both.T[:8]
-    else:
-        sums_ref[0] = jnp.zeros(sums_ref.shape[1:], F32)
-
-
-def backward_kernel(heads, n_params, aux_kind, *refs):
-    h_ref, *refs = refs
-    if aux_kind != "columns":
-        aux_ref, *refs = refs
-    gate_ref, xraw_ref, bcraw_ref, dtraw_ref, mixed_ref, w_ref, wo_ref, *refs = refs
-    _, ch, bc, dtp, sel = load_params(refs[:n_params])
-    param_refs, refs = refs[:n_params], refs[n_params:]
-    dn_ref, pg_ref, no_ref, *sum_refs = refs[:-4]
-    dmix_s, dx_s, dbc_s, ddt_s = refs[-4:]
+        sums_ref[i] = both.T[:8]
+
+
+def backward_kernel(heads, *refs):
+    h_ref, aux_ref, *refs = refs
+    saved, (w_ref, wo_ref), params, outs, sum_refs, scratch = take(refs, (5, 2, 4, 3, 3, 4))
+    params = load_params(params)
+    aux = aux_ref[0, :, 0:1], aux_ref[0, :, 1:2]
+    sums = backward_rows(heads, params, 0, h_ref, aux, saved, w_ref, wo_ref, outs, scratch)
+    for ref, value in zip(sum_refs, sums):
+
+        @pl.when(pl.program_id(0) == 0)
+        def _(ref=ref, value=value):
+            ref[...] = value
+
+        @pl.when(pl.program_id(0) > 0)
+        def _(ref=ref, value=value):
+            ref[...] += value
+
+
+def aux_of_columns(h_ref, i, width):
+    aux = h_ref[i, :, width:].astype(F32)
+    return aux[:, 0:1] + aux[:, 1:2] + aux[:, 2:3], aux[:, 3:4] + aux[:, 4:5] + aux[:, 5:6]
+
+
+def aux_of_rows(sums):
+    aux = jnp.concatenate([sums, jnp.zeros((LANES - 8, sums.shape[1]), F32)], axis=0).T
+    scale = lax.rsqrt(aux[:, 0:1] * (1.0 / INNER) + NORM_EPS)
+    return scale, aux[:, 1:2] * scale
+
+
+def backward_rows(heads, params, i, h_ref, aux, saved, w_ref, wo_ref, outs, scratch):
+    _, ch, bc, dtp, sel = params
+    gate_ref, xraw_ref, bcraw_ref, dtraw_ref, mixed_ref = saved
+    dn_ref, pg_ref, no_ref = outs
+    dmix_s, dx_s, dbc_s, ddt_s = scratch
     length, width = dn_ref.shape[1:]
     wide = ch.shape[1]
     blocks = length // SPAN
-    h_rows = h_ref[0, :, :width]
-    if aux_kind == "columns":
-        aux = h_ref[0, :, width:].astype(F32)
-        scale = aux[:, 0:1] + aux[:, 1:2] + aux[:, 2:3]
-        rdot = aux[:, 3:4] + aux[:, 4:5] + aux[:, 5:6]
-    elif aux_kind == "rows":
-        sums = aux_ref[0]
-        aux = jnp.concatenate([sums, jnp.zeros((LANES - 8, length), F32)], axis=0).T
-        scale = lax.rsqrt(aux[:, 0:1] * (1.0 / INNER) + NORM_EPS)
-        rdot = aux[:, 1:2] * scale
-    else:
-        scale, rdot = aux_ref[0, :, 0:1], aux_ref[0, :, 1:2]
-    gate = gate_ref[0]
-    mixed = mixed_ref[0].astype(F32)
+    h_rows = h_ref[i, :, :width]
+    scale, rdot = aux
+    gate = gate_ref[i]
+    mixed = mixed_ref[i].astype(F32)
     sig = sigmoid(gate)
     silu = gate * sig
     gated = mixed * silu
@@ -253,20 +271,20 @@
     grad_no = dot_nt(h_rows, wo_ref[...])
     grad_g = scale * (gain * grad_no) - gated * (scale * scale * (1.0 / INNER) * rdot)
     scaled = gated * scale
-    no_ref[0] = (scaled * gain).astype(BF16)
+    no_ref[i] = (scaled * gain).astype(BF16)
     gain_row = jnp.sum(grad_no * scaled, axis=0, keepdims=True)
     dmix_s[...] = (grad_g * silu).astype(BF16)
-    pg_ref[0, :, :wide] = (grad_g * mixed * (sig * (1.0 + gate * (1.0 - sig)))).astype(BF16)
-
-    x_raw = xraw_ref[0].astype(F32)
-    bc_raw = bcraw_ref[0].astype(F32)
+    pg_ref[i, :, :wide] = (grad_g * mixed * (sig * (1.0 + gate * (1.0 - sig)))).astype(BF16)
+
+    x_raw = xraw_ref[i].astype(F32)
+    bc_raw = bcraw_ref[i].astype(F32)
     conv_x = conv_sum(x_raw, ch)
     sig_x = sigmoid(conv_x)
     act_x = (conv_x * sig_x).astype(BF16)
     conv_bc = conv_sum(bc_raw, bc)
     sig_bc = sigmoid(conv_bc)
     act_bc = (conv_bc * sig_bc).astype(BF16)
-    step, slope = step_sizes(dtraw_ref[0].astype(F32), dtp[0:1])
+    step, slope = step_sizes(dtraw_ref[i].astype(F32), dtp[0:1])
     rate = jnp.exp(dtp[1:2])
     causal = triangles()
     ones = causal.astype(F32)
@@ -369,53 +387,38 @@
     skip_row = jnp.sum(dmix_s[...].astype(F32) * act_x.astype(F32), axis=0, keepdims=True)
     grad_conv = dx_s[...] * (sig_x * (1.0 + conv_x * (1.0 - sig_x)))
     grad_raw, ch_rows = conv_back(grad_conv, x_raw, ch)
-    pg_ref[0, :, wide : 2 * wide] = grad_raw.astype(BF16)
+    pg_ref[i, :, wide : 2 * wide] = grad_raw.astype(BF16)
     grad_conv = dbc_s[...] * (sig_bc * (1.0 + conv_bc * (1.0 - sig_bc)))
     grad_raw, bc_rows = conv_back(grad_conv, bc_raw, bc)
-    pg_ref[0, :, 2 * wide : 2 * wide + SHARED] = grad_raw.astype(BF16)
+    pg_ref[i, :, 2 * wide : 2 * wide + SHARED] = grad_raw.astype(BF16)
     grad_dt = ddt_s[...] * slope
     low_dt = grad_dt.astype(BF16)
     if sel is not None:
         low_dt = dot_nt(low_dt, sel).astype(BF16)
-    pg_ref[0, :, 2 * wide + SHARED :] = low_dt
-    dn_ref[0] = dot(pg_ref[0], w_ref[...]).astype(BF16)
+    pg_ref[i, :, 2 * wide + SHARED :] = low_dt
+    dn_ref[i] = dot(pg_ref[i], w_ref[...]).astype(BF16)
     by_channel = stacked(ch_rows + [skip_row, gain_row], 8)
     by_shared = stacked(bc_rows, 8)
     by_head = stacked([jnp.sum(grad_dt, axis=0, keepdims=True), rate_row * rate], 8)
-    first = pl.program_id(0) == 0
     if sel is not None:
         by_head = lax.dot_general(
             by_head, sel.astype(F32), (((1,), (1,)), ((), ())),
             preferred_element_type=F32, precision=HIGHEST,
         )
-        ids_ref, (sum_ref,) = param_refs[0], sum_refs
-
-        @pl.when(first)
-        def _():
-            sum_ref[...] = jnp.zeros_like(sum_ref)
-
-        for j in range(2):
-            part = by_channel[:, j * THIRD : (j + 1) * THIRD]
-            part = jnp.concatenate([part, jnp.zeros((8, PIECE - THIRD), F32)], axis=1)
-            sum_ref[:, piece_lanes(ids_ref, j)] += part
-        sum_ref[:, -SHARED:] += by_shared
-        sum_ref[7:8, DT_AT : DT_AT + HEADS] += by_head[0:1]
-        sum_ref[7:8, RATE_AT : RATE_AT + HEADS] += by_head[1:2]
-        return
-    for ref, value in zip(sum_refs, (by_channel, by_shared, by_head)):
-
-        @pl.when(first)
-        def _(ref=ref, value=value):
-            ref[...] = value
-
-        @pl.when(jnp.logical_not(first))
-        def _(ref=ref, value=value):
-            ref[...] += value
+    return by_channel, by_shared, by_head
+
+
+def add_small(sum_ref, ids, by_channel, by_shared, by_head):
+    for j in range(2):
+        part = by_channel[:, j * THIRD : (j + 1) * THIRD]
+        part = jnp.concatenate([part, jnp.zeros((8, PIECE - THIRD), F32)], axis=1)
+        sum_ref[:, piece_lanes(ids, j)] += part
+    sum_ref[:, -SHARED:] += by_shared
+    sum_ref[7:8, DT_AT : DT_AT + HEADS] += by_head[0:1]
+    sum_ref[7:8, RATE_AT : RATE_AT + HEADS] += by_head[1:2]
 
 
 def whole_spec(array):
-    if array.dtype == jnp.int32:
-        return pl.BlockSpec(memory_space=pltpu.SMEM)
     return pl.BlockSpec(array.shape, lambda i: (0,) * array.ndim)
 
 
@@ -430,56 +433,52 @@
 PARAMS = dict(vmem_limit_bytes=60 * 1024 * 1024)
 
 
-def run_forward(heads, wide, rows, w, wo, params, grad_rows=None):
+def run_forward(heads, wide, rows, w, wo, params):
     count, length, width = rows.shape
-    compact = len(params) == 2
     constants = [w, wo, *params]
-    given = [] if grad_rows is None else [grad_rows]
     outs = [
-        (length, width + LANES if compact else width, BF16),
-        (8, length, F32) if compact else (length, LANES, F32),
-        (length, width, BF16), (length, wide, F32),
-        (length, wide, BF16), (length, SHARED, BF16), (length, LANES, BF16), (length, wide, BF16),
+        (width, BF16), (LANES, F32), (width, BF16), (wide, F32),
+        (wide, BF16), (SHARED, BF16), (LANES, BF16), (wide, BF16),
     ]
     return pl.pallas_call(
-        partial(forward_kernel, heads, len(params), grad_rows is not None),
+        partial(forward_kernel, heads),
         grid=(count,),
-        out_shape=[jax.ShapeDtypeStruct((count, r, n), t) for r, n, t in outs],
-        in_specs=[block_spec(rows)]
-        + [whole_spec(c) for c in constants]
-        + [block_spec(g) for g in given],
-        out_specs=[row_spec(r, n) for r, n, _ in outs],
+        out_shape=[jax.ShapeDtypeStruct((count, length, n), t) for n, t in outs],
+        in_specs=[block_spec(rows)] + [whole_spec(c) for c in constants],
+        out_specs=[row_spec(length, n) for n, _ in outs],
         compiler_params=pltpu.CompilerParams(**PARAMS),
         name="forward",
-    )(rows, *constants, *given)
-
-
-def run_backward(heads, wide, grad_rows, aux, aux_kind, saved, w, wo, params):
+    )(rows, *constants)
+
+
+def run_backward(heads, wide, grad_rows, aux, saved, w, wo, params):
     count, length, _ = grad_rows.shape
     columns, width = w.shape
-    given = [grad_rows] + ([] if aux is None else [aux]) + list(saved)
+    given = [grad_rows, aux, *saved]
     constants = [w, wo, *params]
     outs = [(width, BF16), (columns, BF16), (wide, BF16)]
     sums = [(8, wide), (8, SHARED), (8, LANES)]
-    if len(params) == 2:
-        sums = [params[1].shape]
     return pl.pallas_call(
-        partial(backward_kernel, heads, len(params), aux_kind),
+        partial(backward_kernel, heads),
         grid=(count,),
         out_shape=[jax.ShapeDtypeStruct((count, length, n), t) for n, t in outs]
         + [jax.ShapeDtypeStruct(s, F32) for s in sums],
         in_specs=[block_spec(g) for g in given] + [whole_spec(c) for c in constants],
         out_specs=[row_spec(length, n) for n, _ in outs]
         + [pl.BlockSpec(s, lambda i: (0, 0)) for s in sums],
-        scratch_shapes=[
-            pltpu.VMEM((length, wide), BF16),
-            pltpu.VMEM((length, wide), F32),
-            pltpu.VMEM((length, SHARED), F32),
-            pltpu.VMEM((length, LANES), F32),
-        ],
+        scratch_shapes=backward_scratch(length, wide),
         compiler_params=pltpu.CompilerParams(**PARAMS),
         name="backward",
     )(*given, *constants)
+
+
+def backward_scratch(length, wide):
+    return [
+        pltpu.VMEM((length, wide), BF16),
+        pltpu.VMEM((length, wide), F32),
+        pltpu.VMEM((length, SHARED), F32),
+        pltpu.VMEM((length, LANES), F32),
+    ]
 
 
 class Plan:
@@ -582,18 +581,22 @@
         self.spot, self.own, self.all = spot, own, all_rows
         self.send, self.recv, self.local = sems
 
+    def slot(self, half):
+        rows = self.own.shape[0]
+        return self.all.at[half, pl.ds(pl.multiple_of(self.spot.q * rows, rows), rows)]
+
     def copy(self, j):
         spot = self.spot
-        slot = self.all.at[spot.half, spot.q]
+        slot = self.slot(spot.half)
         if j == 3:
             return remote(self.own, slot, self.send.at[3], self.recv.at[3], spot.at_twin)
         if j < 3:
             return remote(self.own, slot, self.send.at[j], self.recv.at[j], spot.plane(j + 1))
-        slot = self.all.at[1 - spot.half, spot.q]
+        slot = self.slot(1 - spot.half)
         return remote(slot, slot, self.send.at[j], self.recv.at[j], spot.plane(j - 3))
 
     def here(self):
-        return pltpu.make_async_copy(self.own, self.all.at[self.spot.half, self.spot.q], self.local)
+        return pltpu.make_async_copy(self.own, self.slot(self.spot.half), self.local)
 
     def start(self):
         for j in (3, 0, 1, 2):
@@ -617,31 +620,30 @@
     @staticmethod
     def scratch(rows, columns):
         return [
+            pltpu.VMEM((2, 4 * rows, columns), BF16),
             pltpu.VMEM((3, 2, rows, columns), BF16),
-            pltpu.VMEM((2, rows, columns), BF16),
             pltpu.VMEM((2, rows, columns), BF16),
             DMA((7,)),
             DMA((7,)),
-            DMA((2,)),
         ]
 
-    def __init__(self, spot, parts, width, scratch):
-        self.spot, self.parts, self.width = spot, parts, width
-        self.recv_rows, self.own, self.twin_rows, self.send, self.recv, self.local = scratch
+    def __init__(self, spot, width, scratch):
+        self.spot, self.width = spot, width
+        self.parts, self.recv_rows, self.twin_rows, self.send, self.recv = scratch
+        self.rows = self.twin_rows.shape[1]
+
+    def half(self, i):
+        return 1 - self.spot.half + i * (2 * self.spot.half - 1)
+
+    def block(self, q):
+        return pl.ds(pl.multiple_of(q * self.rows, self.rows), self.rows)
 
     def copy(self, k, i):
         spot = self.spot
-        half = (1 - spot.half) if i == 0 else spot.half
         j = 3 * i + k - 1
         return remote(
-            self.parts.at[half, spot.around[k]], self.recv_rows.at[k - 1, i],
+            self.parts.at[self.half(i), self.block(spot.around[k])], self.recv_rows.at[k - 1, i],
             self.send.at[j], self.recv.at[j], spot.plane(k),
-        )
-
-    def here(self, i):
-        half = (1 - self.spot.half) if i == 0 else self.spot.half
-        return pltpu.make_async_copy(
-            self.parts.at[half, self.spot.q], self.own.at[i], self.local.at[i]
         )
 
     def across(self):
@@ -649,24 +651,18 @@
             self.twin_rows.at[0], self.twin_rows.at[1], self.send.at[6], self.recv.at[6], self.spot.at_twin
         )
 
-    def start(self):
-        for i in range(2):
-            self.here(i).start()
+    def start(self, i):
         for k in (1, 2, 3):
-            self.copy(k, 0).start()
+            self.copy(k, i).start()
 
     def plane_total(self, i):
-        self.here(i).wait()
-        total = self.own[i].astype(F32)
+        total = self.parts[self.half(i), self.block(self.spot.q), :].astype(F32)
         for k in (1, 2, 3):
             self.copy(k, i).wait_recv()
             total += self.recv_rows[k - 1, i].astype(F32)
         return total
 
     def forward(self):
-        for k in (1, 2, 3):
-            self.copy(k, 0).wait_send()
-            self.copy(k, 1).start()
         total = self.plane_total(0)
         width = self.width
         self.twin_rows[0, :, :width] = total[:, :width].astype(BF16)
@@ -682,8 +678,9 @@
         return total
 
     def close(self):
-        for k in (1, 2, 3):
-            self.copy(k, 1).wait_send()
+        for i in range(2):
+            for k in (1, 2, 3):
+                self.copy(k, i).wait_send()
         self.across().wait_send()
 
 
@@ -834,11 +831,6 @@
                     self.to_sibling(b, n).wait_recv()
             for n in (1, 2):
                 self.out_to(n).wait_recv()
-
-
-def take(refs, counts):
-    refs = list(refs)
-    return [[refs.pop(0) for _ in range(n)] for n in counts]
 
 
 def all_places(spot):
@@ -890,32 +882,6 @@
     pack_there.wait()
 
 
-def middle_kernel(*refs):
-    ins, outs, weight_s, sum_s, spread_s = take(refs, (4, 6, 5, 6, 3))
-    w_in, w_out, parts, rows_in = ins
-    tile, tile_out, all_rows, branch, scales, rows_out = outs
-    spot = Spot()
-    weights = Weights(spot, 1, w_in, w_out, tile, tile_out, weight_s)
-    total = Sum(spot, parts, rows_in.shape[1], sum_s)
-    spread = Spread(spot, rows_out, all_rows, spread_s)
-    weights.begin()
-    greet(all_places(spot))
-    total.start()
-    weights.start()
-    total.forward()
-    weights.step(0)
-    layer_rows(total.finish(), rows_in, branch, scales, rows_out)
-    spread.start()
-    weights.step(1)
-    weights.step(2)
-    spread.forward()
-    weights.step(3)
-    weights.step(4)
-    spread.finish()
-    total.close()
-    weights.finish()
-
-
 def layer_rows(total, rows_in, branch, scales, rows_out):
     width = rows_in.shape[1]
     square = jnp.sum(total[:, width:], axis=1, keepdims=True)
@@ -927,25 +893,6 @@
         scales[...] = jnp.broadcast_to(scale, scales.shape)
 
 
-def sums_kernel(mine_ref, total_ref, others, send, recv):
-    spot = Spot()
-    places = [spot.plane(k) for k in (1, 2, 3)]
-    places += [(spot.s, spot.around[k], spot.twin) for k in (1, 2, 3)] + [spot.at_twin]
-    greet(places)
-    copies = [
-        remote(mine_ref, others.at[j], send.at[j], recv.at[j], place) for j, place in enumerate(places)
-    ]
-    for copy in copies:
-        copy.start()
-    total = mine_ref[...]
-    for j, copy in enumerate(copies):
-        copy.wait_recv()
-        total += others[j]
-    total_ref[...] = total
-    for copy in copies:
-        copy.wait_send()
-
-
 def norm_back(total, rows_in, gain, grad_out):
     rows = rows_in[...].astype(F32)
     scale = lax.rsqrt(jnp.mean(rows * rows, axis=-1, keepdims=True) + NORM_EPS)
@@ -976,7 +923,6 @@
             pltpu.VMEM((2, wide, width), BF16),
             pltpu.VMEM((3, columns, shard), BF16),
             pltpu.VMEM((THIRD, width), BF16),
-            DMA((6,)),
             DMA((22,)),
             DMA((22,)),
         ]
@@ -985,10 +931,10 @@
     def results(shard, width):
         return [((2, 4 * THIRD, shard), BF16), ((SHARED + HEADS, shard), BF16), ((THIRD, width), BF16)]
 
-    def __init__(self, spot, layer, w_grad, wo_grad, results, scratch):
-        self.spot, self.layer, self.w_grad, self.wo_grad = spot, layer, w_grad, wo_grad
+    def __init__(self, spot, layer, results, scratch):
+        self.spot, self.layer = spot, layer
         self.reduced, self.shared, self.out = results
-        self.cores, self.cores_out, self.planes, self.mate_out, self.local, self.send, self.recv = scratch
+        self.cores, self.cores_out, self.planes, self.mate_out, self.send, self.recv = scratch
         self.shard = self.planes.shape[2]
         self.others = 2 * (1 - spot.half)
 
@@ -1002,32 +948,25 @@
     def columns(self, z):
         return pl.ds(pl.multiple_of(z * self.shard, LANES), self.shard)
 
-    def pair(self, n, slot):
+    def core_copy(self, n):
+        buffer, rows = (self.cores_out, pl.ds(0, self.cores_out.shape[1])) if n == 5 else (self.cores, self.rows(n))
+        return remote(
+            buffer.at[0, rows], buffer.at[1, rows], self.send.at[n], self.recv.at[n], self.spot.sibling
+        )
+
+    def product(self, n, proj_grad, normed, normed_out, h_rows):
+        def flat(value):
+            return value.reshape(-1, value.shape[-1])
+
+        width = self.cores.shape[2]
         if n == 5:
-            return self.wo_grad, self.cores_out.at[slot]
-        return self.w_grad.at[self.rows(n)], self.cores.at[slot, self.rows(n)]
-
-    def core_copy(self, n):
-        source, target = self.pair(n, 1)
-        return remote(source, target, self.send.at[n], self.recv.at[n], self.spot.sibling)
-
-    def own_copy(self, n):
-        return pltpu.make_async_copy(*self.pair(n, 0), self.local.at[n])
-
-    def begin(self):
-        @self.here
-        def _():
-            for n in self.ORDER:
-                self.own_copy(n).start()
-
-        @pl.when(self.spot.s != self.layer)
-        def _():
-            for at, n in enumerate(self.ORDER):
-                if at >= 2:
-                    self.core_copy(self.ORDER[at - 2]).wait_send()
-                self.core_copy(n).start()
-            for n in self.ORDER[-2:]:
-                self.core_copy(n).wait_send()
+            total = dot_tn(flat(normed_out[...]), flat(h_rows[:, :, :width]))
+            self.cores_out[0] = total.astype(BF16)
+        else:
+            _, first, size = tile_parts(self.spot, 0)[n]
+            total = dot_tn(flat(proj_grad[:, :, first : first + size]), flat(normed[...]))
+            self.cores[0, first : first + size, :] = total.astype(BF16)
+        pl.when(self.spot.s != self.layer)(lambda: self.core_copy(n).start())
 
     def plane_copy(self, c, n):
         spot, rows = self.spot, self.rows(n)
@@ -1060,7 +999,6 @@
     def to_planes(self, n):
         @self.here
         def _():
-            self.own_copy(n).wait()
             self.core_copy(n).wait_recv()
             if n == 5:
                 add_rows(self.cores_out.at[0], [self.cores_out.at[0], self.cores_out.at[1]])
@@ -1100,6 +1038,11 @@
         @self.here
         def _():
             self.mate_copy().wait_send()
+
+        @pl.when(self.spot.s != self.layer)
+        def _():
+            for n in self.ORDER:
+                self.core_copy(n).wait_send()
 
 
 class GradsAround:
@@ -1229,23 +1172,149 @@
         return self.small[1 + n]
 
 
-def turn_kernel(*refs):
-    ins, outs, sum_s, last_s, spread_s, across_s, (payload,) = take(refs, (10, 7, 6, 6, 3, 7, 1))
-    parts, last_parts, rows_in, grad_out, packs, branch, scales, last_in, w_grad, wo_grad = ins
-    all_rows, grad_rows, grad_gain, last_rows, *results = outs
+def loading(sources, targets, sems):
+    return [pltpu.make_async_copy(a, b, sems.at[n]) for n, (a, b) in enumerate(zip(sources, targets))]
+
+
+def saved_shapes(length, width, wide):
+    columns = ((width, BF16), (wide, F32), (wide, BF16), (SHARED, BF16), (LANES, BF16), (wide, BF16))
+    return [((2, length, n), t) for n, t in columns]
+
+
+def middle_kernel(heads, *refs):
+    ins, outs, kept, weight_s, sum_s, spread_s, layer_s, (store,) = take(refs, (7, 6, 6, 5, 5, 3, 11, 1))
+    w_in, w_out, *layer_ins, rows_in = ins
+    tile, tile_out, all_rows, branch, scales, rows_out = outs
+    u, w, wo, pack, *saved, load = layer_s
+    spot = Spot()
+    weights = Weights(spot, 1, w_in, w_out, tile, tile_out, weight_s)
+    total = Sum(spot, rows_in.shape[1], sum_s)
+    spread = Spread(spot, rows_out, all_rows, spread_s)
+    loads = loading(layer_ins[:3] + [layer_ins[3].at[0]], layer_s[:4], load)
+    for copy in loads:
+        copy.start()
+    weights.begin()
+    greet(all_places(spot))
+    weights.start()
+    for copy in loads:
+        copy.wait()
+    params = load_params(([spot.piece(spot.half, j) for j in range(2)], pack))
+
+    @pl.loop(0, 2)
+    def _(i):
+        forward_rows(heads, params, total.half(i), u, w, wo, None, [total.parts, None, *saved])
+        total.start(i)
+
+    stores = loading(saved, kept, store)
+    for copy in stores:
+        copy.start()
+    weights.step(0)
+    total.forward()
+    weights.step(1)
+    layer_rows(total.finish(), rows_in, branch, scales, rows_out)
+    spread.start()
+    weights.step(2)
+    spread.forward()
+    weights.step(3)
+    weights.step(4)
+    spread.finish()
+    total.close()
+    weights.finish()
+    for copy in stores:
+        copy.wait()
+
+
+class RowSums:
+    @staticmethod
+    def scratch(length):
+        shape = (2, 8, length)
+        return [pltpu.VMEM(shape, F32), pltpu.VMEM((7,) + shape, F32), DMA((14,)), DMA((14,))]
+
+    def __init__(self, spot, scratch):
+        self.mine, self.others, self.send, self.recv = scratch
+        self.places = [spot.plane(k) for k in (1, 2, 3)] + [spot.at_twin]
+        self.places += [(spot.s, spot.around[k], spot.twin) for k in (1, 2, 3)]
+
+    def copies(self, seq):
+        return [
+            remote(
+                self.mine.at[seq], self.others.at[j, seq],
+                self.send.at[2 * j + seq], self.recv.at[2 * j + seq], place,
+            )
+            for j, place in enumerate(self.places)
+        ]
+
+    def start(self, seq):
+        for copy in self.copies(seq):
+            copy.start()
+
+    def finish(self, seq):
+        total = self.mine[seq]
+        for j, copy in enumerate(self.copies(seq)):
+            copy.wait_recv()
+            total += self.others[j, seq]
+        for copy in self.copies(seq):
+            copy.wait_send()
+        self.mine[seq] = total
+
+
+def turn_kernel(heads, *refs):
+    ins, outs, sum_s, last_s, spread_s, across_s, row_s, back_s, layer_s, (h_rows, payload, *saved) = take(
+        refs, (9, 8, 5, 5, 3, 6, 4, 6, 5, 8)
+    )
+    layer_ins, (rows_in, grad_out, branch, scales) = take(ins, (5, 4))
+    all_rows, grad_rows, grad_gain, last_rows, *results, small = outs
+    u, w, wo, pack, load = layer_s
     spot = Spot()
     width = rows_in.shape[1]
-    total = Sum(spot, parts, width, sum_s)
-    last = Sum(spot, last_parts, width, last_s)
+    total = Sum(spot, width, sum_s)
+    last = Sum(spot, width, last_s)
     spread = Spread(spot, payload, all_rows, spread_s)
-    across = GradsAcross(spot, 1, w_grad, wo_grad, results, across_s)
-    greet(all_places(spot))
-    total.start()
-    across.begin()
+    across = GradsAcross(spot, 1, results, across_s)
+    sums = RowSums(spot, row_s)
+    loads = loading(
+        layer_ins[:3] + [layer_ins[3].at[1], layer_ins[4]], [u, w, wo, pack, h_rows], load
+    )
+    for copy in loads:
+        copy.start()
+    places = [spot.plane(k) for k in (1, 2, 3)] + [spot.column((spot.z + k) % 4) for k in (1, 2, 3)]
+    places += [(spot.s, spot.around[k], spot.twin) for k in (1, 2, 3)] + [spot.sibling]
+    greet(places)
+    for copy in loads:
+        copy.wait()
+    ids = [spot.piece(spot.half, j) for j in range(2)]
+    params = load_params((ids, pack))
+    small[...] = jnp.zeros_like(small)
+
+    @pl.loop(0, 2)
+    def _(i):
+        seq = last.half(i)
+        forward_rows(heads, params, seq, u, w, wo, h_rows, [last.parts, sums.mine, *saved])
+        sums.start(seq)
+        last.start(i)
+
+    proj_grad, normed_out, *scratch = back_s
+
+    @pl.loop(0, 2)
+    def _(i):
+        seq = total.half(i)
+        sums.finish(seq)
+        aux = aux_of_rows(sums.mine[seq])
+        outs = (total.parts, proj_grad, normed_out)
+        parts = backward_rows(heads, params, seq, h_rows, aux, saved[1:], w, wo, outs, scratch)
+        add_small(small, ids, *parts)
+        total.start(i)
+
+    def product(n):
+        across.product(n, proj_grad, saved[0], normed_out, h_rows)
+
+    last.forward()
+    product(4)
+    product(0)
+    total.forward()
     across.to_planes(4)
     across.to_planes(0)
-    total.forward()
-    grad, gain_row = norm_back(total.finish(), rows_in, packs[1, 7:8, :width], grad_out)
+    grad, gain_row = norm_back(total.finish(), rows_in, pack[7:8, :width], grad_out)
     low = grad.astype(BF16)
     grad_rows[...] = low
     grad_gain[...] = stacked([gain_row], 8)
@@ -1256,15 +1325,15 @@
     second = pltpu.roll(split_three(cross).astype(F32), 3, 1)
     payload[:, width:] = jnp.where(lanes < 3, first, second).astype(BF16)
     spread.start()
-    last.start()
+    for n in (1, 2, 3, 5):
+        product(n)
     spread.forward()
     for n in (1, 2, 3, 5):
         across.to_planes(n)
-    last.forward()
+    layer_rows(last.finish(), rows_in, None, None, last_rows)
     spread.finish()
     for n in GradsAcross.ORDER:
         across.gather(n)
-    layer_rows(last.finish(), last_in, None, None, last_rows)
     for n in range(5):
         across.sent(n)
     across.finish()
@@ -1272,16 +1341,22 @@
     last.close()
 
 
-def close_kernel(*refs):
-    ins, outs, sum_s, across_s, results, around_s, small_s, rest = take(refs, (15, 5, 6, 7, 3, 4, 3, 6))
-    parts, rows_in, grad_out, packs, first_rows, last_rows, last_grad, *ins = ins
-    w_grad, wo_grad, small_0, small_1, gain_1, *last_results = ins
+def close_kernel(heads, *refs):
+    ins, outs, sum_s, across_s, results, around_s, small_s, back_s, layer_s, rest = take(
+        refs, (19, 5, 5, 6, 3, 4, 3, 6, 11, 6)
+    )
+    layer_ins, (rows_in, last_rows, last_grad, small_1, gain_1), last_results = take(ins, (11, 5, 3))
     home_rows, home_grads, final, final_out, small_out = outs
     grad_rows, small_in, send, recv, local, load = rest
+    first_rows, *layer_ins = layer_ins
+    h_rows, w, wo, pack, normed, *saved, layer_load = layer_s
     spot = Spot()
     width = rows_in.shape[1]
-    total = Sum(spot, parts, width, sum_s)
-    across = GradsAcross(spot, 0, w_grad, wo_grad, results, across_s)
+    total = Sum(spot, width, sum_s)
+    across = GradsAcross(spot, 0, results, across_s)
+    layer_loads = loading(
+        layer_ins[:3] + [layer_ins[3].at[0]] + layer_ins[4:], layer_s[:-1], layer_load
+    )
     around = GradsAround(spot, results, final, final_out, around_s)
     small = SmallSum(spot, small_s)
     first_core, last_core = pl.when(spot.s == 0), pl.when(spot.s == 1)
@@ -1294,9 +1369,9 @@
         for copy in loads:
             copy.start()
 
+    for copy in layer_loads:
+        copy.start()
     greet(all_places(spot))
-    total.start()
-    across.begin()
 
     @last_core
     def _():
@@ -1307,10 +1382,34 @@
             around.send_part(n)
         around.send_out()
 
+    for copy in layer_loads:
+        copy.wait()
+    proj_grad, normed_out, *scratch = back_s
+    ids = [spot.piece(spot.half, j) for j in range(2)]
+    params = load_params((ids, pack))
+    small_in[...] = jnp.zeros_like(small_in)
+
+    @pl.loop(0, 2)
+    def _(i):
+        seq = total.half(i)
+        aux = aux_of_columns(h_rows, seq, width)
+        outs = (total.parts, proj_grad, normed_out)
+        sums = backward_rows(heads, params, seq, h_rows, aux, saved, w, wo, outs, scratch)
+        add_small(small_in.at[0], ids, *sums)
+        total.start(i)
+
     order = GradsAcross.ORDER
+
+    def product(n):
+        across.product(n, proj_grad, normed, normed_out, h_rows)
+
+    for n in order[:3]:
+        product(n)
     for n in order[:3]:
         across.to_planes(n)
     total.forward()
+    for n in order[3:]:
+        product(n)
     for at in range(3, 6):
         across.sent(order[at - 3])
         across.to_planes(order[at])
@@ -1318,7 +1417,7 @@
     first_core(lambda: around.shared_step(0))
     across.gather(0)
     first_core(lambda: around.send_part(0))
-    grad, gain_row = norm_back(total.finish(), rows_in, packs[0, 7:8, :width], grad_out)
+    grad, gain_row = norm_back(total.finish(), rows_in, pack[7:8, :width], last_grad)
     grad_rows[...] = grad.astype(BF16)
     layers = ((first_rows, grad_rows), (last_rows, last_grad))
 
@@ -1329,7 +1428,6 @@
             copies.append(pltpu.make_async_copy(layers[s][n], target.at[s], local.at[n]))
         return copies
 
-    small_in[0] = small_0[...]
     small_in[1] = small_1[...]
     small_in[0, 7:8, :width] = gain_row
     small_in[1, 7:8, :width] = gain_1[0:1]
@@ -1396,13 +1494,12 @@
 def fast_shards(
     tokens, cotangent, norm_gain, w_in, conv_weight, conv_bias, dt_bias, a_log, skip_gain, gate_gain, w_out
 ):
-    section, place, half = lax.axis_index("section"), lax.axis_index("seq"), lax.axis_index("fsdp") // 2
+    section = lax.axis_index("section")
     span, width = tokens.shape[2:]
     heads = HEADS // 8
     wide = heads * HEADDIM
     columns = 2 * wide + SHARED + HEADS
     shard = w_in.shape[1]
-    ids = 8 * half + place + jnp.array([0, 4], jnp.int32)
     rows_in = w_in[0].T
     channels = jnp.concatenate(
         [
@@ -1417,7 +1514,7 @@
     )
     pack = jnp.concatenate([channels, shared], axis=1)
     pack = jnp.concatenate([pack, widened(last_row, 1, pack.shape[1])])
-    group = (2, 4, span, width)
+    group = (2, 4 * span, width)
     weight_outs = [((columns, width), BF16), ((wide, width), BF16)]
     weight_s = Weights.scratch(columns, shard, width)
     payload = width + LANES
@@ -1429,82 +1526,57 @@
         + [pltpu.VMEM((span, width), BF16)] * 2 + [pltpu.VMEM(pack.shape, F32), DMA((3,)), DMA, DMA, DMA],
         "open",
     )
-    own_rows = [lax.dynamic_index_in_dim(tokens[:, 0], section, 0, False)]
+    own_tokens = lax.dynamic_index_in_dim(tokens[:, 0], section, 0, False)
     own_cot = lax.dynamic_index_in_dim(cotangent[:, 0], section, 0, False)
-
-    def joined(rows):
-        return rows.reshape(2, 4 * span, rows.shape[-1])
-
-    def cut(rows):
-        return rows.reshape(2, 4, span, rows.shape[-1])
-
-    tiles = [(tile, tile_out)]
-    parts, _, normed, *kept = run_forward(
-        heads, wide, joined(all_rows), tile, tile_out, (ids, packs[0])
-    )
-    saved = [(normed, kept)]
-    tile, tile_out, all_rows, branch, scales, rows = comm_call(
-        middle_kernel, 2,
-        [rows_in, w_out[0], cut(parts), own_rows[0]], [ANY] * 3 + [VMEM],
-        weight_outs
-        + [(group, BF16), ((span, width), F32), ((span, LANES), F32), ((span, width), BF16)],
-        [ANY] * 3 + [VMEM] * 3,
-        weight_s + Sum.scratch(span, payload) + Spread.SEMS, "middle",
-    )
-    own_rows.append(rows)
-    tiles.append((tile, tile_out))
-    last_parts, sums, normed, *kept = run_forward(
-        heads, wide, joined(all_rows), tile, tile_out, (ids, packs[1]), joined(all_cot)
-    )
-    saved.append((normed, kept))
-    sums = comm_call(
-        sums_kernel, 3, [sums], [VMEM], [(sums.shape, F32)], [VMEM],
-        [pltpu.VMEM((7,) + sums.shape, F32), DMA((7,)), DMA((7,))], "sums",
-    )[0]
-    w_grads, wo_grads, small = [None, None], [None, None], [None, None]
-
-    def products(l, proj_grad, normed_out, grads):
-        w_grads[l] = dot_tn(proj_grad.reshape(-1, columns), saved[l][0].reshape(-1, width)).astype(BF16)
-        wo_grads[l] = dot_tn(normed_out.reshape(-1, wide), grads.reshape(-1, width)).astype(BF16)
-
-    parts, proj_grad, normed_out, small[1] = run_backward(
-        heads, wide, joined(all_cot), sums, "rows", saved[1][1], *tiles[1], (ids, packs[1])
-    )
-    products(1, proj_grad, normed_out, joined(all_cot))
+    length = 4 * span
     rows_spec = ((span, width), BF16)
+    layer_s = [
+        pltpu.VMEM((2, length, width), BF16), pltpu.VMEM((columns, width), BF16),
+        pltpu.VMEM((wide, width), BF16), pltpu.VMEM(pack.shape, F32),
+    ]
+    kept_shapes = saved_shapes(length, width, wide)
+    kept_s = [pltpu.VMEM(*k) for k in kept_shapes]
+    back_s = [pltpu.VMEM((2, length, columns), BF16), pltpu.VMEM((2, length, wide), BF16)]
+    back_s += backward_scratch(length, wide)
     results = GradsAcross.results(shard, width)
     across_s = GradsAcross.scratch(shard, columns, wide, width)
-    all_grads, last_grad, gain_1, last_rows, *last_results = comm_call(
-        turn_kernel, 4,
+    sum_s = Sum.scratch(span, width)
+    first_tiles = [tile, tile_out]
+    tile, tile_out, all_rows, branch, scales, rows, *kept = comm_call(
+        partial(middle_kernel, heads), 2,
+        [rows_in, w_out[0], all_rows, tile, tile_out, packs, own_tokens], [ANY] * 6 + [VMEM],
+        weight_outs + [(group, BF16), ((span, width), F32), ((span, LANES), F32), rows_spec] + kept_shapes,
+        [ANY] * 3 + [VMEM] * 3 + [ANY] * 6,
+        weight_s + Sum.scratch(span, payload) + Spread.SEMS + layer_s + kept_s + [DMA((4,)), DMA((6,))],
+        "middle",
+    )
+    all_grads, last_grad, gain_1, last_rows, *last_results, small_1 = comm_call(
+        partial(turn_kernel, heads), 3,
+        [all_rows, tile, tile_out, packs, all_cot, rows, own_cot, branch, scales],
+        [ANY] * 5 + [VMEM] * 4,
+        [((2, length, payload), BF16), rows_spec, ((8, width), F32), rows_spec]
+        + results + [(pack.shape, F32)],
+        [ANY] + [VMEM] * 7,
+        sum_s + Sum.scratch(span, payload) + Spread.SEMS + across_s + RowSums.scratch(length) + back_s
+        + layer_s + [DMA((5,)), pltpu.VMEM((2, length, width), BF16), pltpu.VMEM((span, payload), BF16)]
+        + kept_s,
+        "turn",
+    )
+    home_rows, home_grads, final, final_out, small = comm_call(
+        partial(close_kernel, heads), 4,
         [
-            cut(parts), cut(last_parts), own_rows[1], own_cot, packs, branch, scales, own_rows[1],
-            w_grads[1], wo_grads[1],
+            rows, all_grads, *first_tiles, packs, *kept,
+            own_tokens, last_rows, last_grad, small_1, gain_1, *last_results,
         ],
-        [ANY, ANY] + [VMEM] * 6 + [ANY] * 2,
-        [((2, 4, span, payload), BF16), rows_spec, ((8, width), F32), rows_spec] + results,
-        [ANY] + [VMEM] * 6,
-        Sum.scratch(span, width) + Sum.scratch(span, payload) + Spread.SEMS + across_s
-        + [pltpu.VMEM((span, payload), BF16)], "turn",
-    )
-    all_grads = joined(all_grads)
-    parts, proj_grad, normed_out, small[0] = run_backward(
-        heads, wide, all_grads, None, "columns", saved[0][1], *tiles[0], (ids, packs[0])
-    )
-    products(0, proj_grad, normed_out, all_grads[..., :width])
-    home_rows, home_grads, final, final_out, small = comm_call(
-        close_kernel, 5,
-        [
-            cut(parts), own_rows[0], last_grad, packs, own_rows[1], last_rows, last_grad,
-            w_grads[0], wo_grads[0], *small, gain_1, *last_results,
-        ],
-        [ANY] + [VMEM] * 6 + [ANY] * 2 + [VMEM] * 3 + [ANY] * 3,
+        [VMEM] + [ANY] * 10 + [VMEM] * 5 + [ANY] * 3,
         [
             ((2, span, width), BF16), ((2, span, width), BF16),
             ((2 * INNER + SHARED + HEADS, shard), BF16), (w_out.shape[1:], BF16), (pack.shape, F32),
         ],
         [ANY] * 4 + [VMEM],
-        Sum.scratch(span, width) + across_s + [pltpu.VMEM(*r) for r in results]
-        + GradsAround.scratch(shard) + SmallSum.scratch(pack.shape[1])
+        sum_s + across_s + [pltpu.VMEM(*r) for r in results]
+        + GradsAround.scratch(shard) + SmallSum.scratch(pack.shape[1]) + back_s
+        + [pltpu.VMEM((2, length, payload), BF16)] + layer_s[1:] + kept_s + [DMA((10,))]
         + [
             pltpu.VMEM((span, width), BF16), pltpu.VMEM((2,) + pack.shape, F32),
             DMA((2,)), DMA((2,)), DMA((2,)), DMA((3,)),
@@ -1627,7 +1699,7 @@
         aux = gather_rows(aux)
         normed, kept = saved[l]
         parts, proj_grad, normed_out, g_ch, g_bc, g_dt = run_backward(
-            heads, wide, all_grads, aux, "lanes", kept, w_tiles[l], wo_tiles[l], params[l]
+            heads, wide, all_grads, aux, kept, w_tiles[l], wo_tiles[l], params[l]
         )
         w_grads[l] = dot_tn(normed.reshape(-1, width), proj_grad.reshape(-1, proj_grad.shape[-1])).astype(BF16)
         wo_grads[l] = dot_tn(normed_out.reshape(-1, wide), all_grads.reshape(-1, width)).astype(BF16)

time: 388 us -> 347 us (0.89)
  Pallas kernels: 343 us -> 318 us
  matrix products: 13.2 us -> 0 us
    pallas_call x4 -> x0, Pallas kernels: 51.1 us -> none  [the longest x2 27.8 us: run_backward(): pl.pallas_call(partial(backward_kernel, heads, len(params), aux_kind), gr...]
    pallas_call x5 -> x4, Pallas kernels: 292 us -> 318 us  [comm_call(): pl.pallas_call(kernel, out_shape=[jax.ShapeDtypeStruct(s, t) for s, t in...]
    dot_general x4 -> x0, matrix products: 13.2 us -> none  [dot(): lax.dot_general(left, right, (contract, ((), ())), preferred_element_type...]
where the time goes in v4:
time: 347 us
  Pallas kernels  318 us (92%)
  other arithmetic  15.2 us (4%)
  local copies, waits for them, and re-layouts  12.4 us (4%)
    pallas_call x4, Pallas kernels, comm_call(): pl.pallas_call(kernel, out_shape=[jax.ShapeDtypeStruct(s, t) for s, t in...  318 us

profile of v4, /device:TPU:0, one launch (start us, length us, event | category | flops | bytes accessed | tf_op | source)
XLA Modules:
  0.0 346.8 jit_solution(16592363240301175694)
XLA Ops:
  0.6 0.5 broadcast.43
  1.2 1.3 reduce.11
  2.5 0.7 slice.56
  3.2 0.7 slice_bitcast_fusion
  3.8 0.7 fusion.4
  4.6 0.1 broadcast_in_dim.29
  4.7 1.4 reduce.10
  6.1 0.7 slice_reduce_fusion
  6.9 0.1 broadcast_in_dim.30
  7.0 0.1 broadcast_in_dim.31
  7.1 0.8 slice.53
  7.9 0.1 concatenate.25
  8.0 0.1 copy.26
  8.1 0.7 select_maximum_fusion.refs_2_
  8.8 1.8 dynamic-slice_bitcast_fusion
  10.6 56.1 %open.1 = (bf16[1072,1536]{1,0:T(8,128)(2,1)}, bf16[384,1536]{1,0:T(8,128)(2,1)}, f32[2,8,4352]{2,1,0:T(8,128)}, bf16[2,256,1536]{2,1,0:T(8,128)(2,1)}, bf16[2,256,1536]{2,1,0:T(8,128)(2,1)}) custom-call(bf16[6448,384]{1,0:T(8,128)(2,1)} %bitcast.35, bf16[768,1536]{1,0:T(8,128)(2,1)} %bitcast.37, f32[8,4352]{1,0:T(8,128)} %select_maximum_fusion.refs_2_, ...), custom_call_target="tpu_custom_call" | custom-call | tf_op jit(solution)/shard_map/open/pallas_call | solution.py:1481
  66.7 56.6 %middle.1 = (bf16[1072,1536]{1,0:T(8,128)(2,1)}, bf16[384,1536]{1,0:T(8,128)(2,1)}, bf16[2,256,1536]{2,1,0:T(8,128)(2,1)}, f32[64,1536]{1,0:T(8,128)}, f32[64,12...) custom-call(bf16[6448,384]{1,0:T(8,128)(2,1)} %bitcast.36, ...), custom_call_target="tpu_custom_call" | custom-call | tf_op jit(solution)/shard_map/middle/pallas_call | solution.py:1481
  123.3 78.8 %turn.1 = (bf16[2,256,1664]{2,1,0:T(8,128)(2,1)}, bf16[64,1536]{1,0:T(8,128)(2,1)}, f32[8,1536]{1,0:T(8,128)}, bf16[64,1536]{1,0:T(8,128)(2,1)}, bf16[2,768,384]...) custom-call(bf16[2,256,1536]{2,1,0:T(8,128)(2,1)} %get-tuple-element.46.refs_0_, ...), custom_call_target="tpu_custom_call" | custom-call | tf_op jit(solution)/shard_map/turn/pallas_call | solution.py:1481
  202.1 127.0 %close.1 = (bf16[2,64,1536]{2,1,0:T(8,128)(2,1)}, bf16[2,64,1536]{2,1,0:T(8,128)(2,1)}, bf16[6448,384]{1,0:T(8,128)(2,1)}, bf16[768,1536]{1,0:T(8,128)(2,1)}, f32[8,4352]{1,0:T(8,128)}) custom-call(bf16[64,1536]{1,0:T(8,128)(2,1)} %get-tuple-element.45.refs_5_.refs_0_, bf16[2,256,1664]{2,1,0:T(8,128)(2,1)} %get-tuple-element.52.refs_1_, ...), custom_call_target="tpu_custom_call" | custom-call | tf_op jit(solution)/shard_map/close/pallas_call | solution.py:1481
  329.1 1.2 fusion.5
  330.3 1.4 slice.57
  331.7 0.7 slice.61
  332.4 0.9 slice.58
  333.4 0.7 slice.68
  334.1 0.1 slice.60
  334.2 0.6 pad_maximum_fusion
  334.8 0.6 fusion.2
  335.5 0.6 reduce_sum.9
  336.1 4.6 %bitcast_convert_fusion = f32[1,768,1536]{2,1,0:T(8,128)} fusion(bf16[768,1536]{1,0:T(8,128)(2,1)} %get-tuple-element.70), kind=kLoop, calls=%fused_computation.1 | loop fusion | flops 1179648 | bytes 7077888 | tf_op jit(solution)/shard_map/convert_element_type | solution.py:1599
  340.8 4.5 %convert_bitcast_fusion = f32[1,384,6448]{1,2,0:T(8,128)} fusion(bf16[6448,384]{1,0:T(8,128)(2,1)S(1)} %copy-done), kind=kLoop, calls=%fused_computation | loop fusion | flops 2476032 | bytes 14856192 | tf_op jit(solution)/shard_map/broadcast_in_dim | solution.py:1592
  345.3 0.7 copy.32
  346.1 0.7 copy.33
  (14 shorter events, 0.3 us)
Async XLA Ops:
  336.1 4.7 %copy-start = (bf16[6448,384]{1,0:T(8,128)(2,1)S(1)}, bf16[6448,384]{1,0:T(8,128)(2,1)}, u32[]{:S(2)}) copy-start(bf16[6448,384]{1,0:T(8,128)(2,1)} %get-tuple-element.69) | copy-start | bytes 14856196
  340.8 4.5 %copy-start.2 = (bf16[2,64,1536]{2,1,0:T(8,128)(2,1)S(1)}, bf16[2,64,1536]{2,1,0:T(8,128)(2,1)}, u32[]{:S(2)}) copy-start(bf16[2,64,1536]{2,1,0:T(8,128)(2,1)} %get-tuple-element.66) | copy-start | bytes 1179652
  340.8 5.3 %copy-start.1 = (bf16[2,64,1536]{2,1,0:T(8,128)(2,1)S(1)}, bf16[2,64,1536]{2,1,0:T(8,128)(2,1)}, u32[]{:S(2)}) copy-start(bf16[2,64,1536]{2,1,0:T(8,128)(2,1)} %get-tuple-element.67) | copy-start | bytes 1179652

commit v5 on v4

--- a/solution.py
+++ b/solution.py
@@ -408,14 +408,18 @@
     return by_channel, by_shared, by_head
 
 
-def add_small(sum_ref, ids, by_channel, by_shared, by_head):
+def add_small(small, by_channel, by_shared, by_head):
     for j in range(2):
         part = by_channel[:, j * THIRD : (j + 1) * THIRD]
-        part = jnp.concatenate([part, jnp.zeros((8, PIECE - THIRD), F32)], axis=1)
-        sum_ref[:, piece_lanes(ids, j)] += part
-    sum_ref[:, -SHARED:] += by_shared
-    sum_ref[7:8, DT_AT : DT_AT + HEADS] += by_head[0:1]
-    sum_ref[7:8, RATE_AT : RATE_AT + HEADS] += by_head[1:2]
+        small[:, j * PIECE : j * PIECE + THIRD] += part
+    small[:, 2 * PIECE : 3 * PIECE] += by_shared
+    small[7:8, 2 * PIECE : 2 * PIECE + HEADS] += by_head[0:1]
+    small[7:8, 2 * PIECE + LANES : 2 * PIECE + LANES + HEADS] += by_head[1:2]
+
+
+def add_gain(small, row):
+    for r in range(8):
+        small[r : r + 1, 3 * PIECE : 3 * PIECE + THIRD] = row[:, r * THIRD : (r + 1) * THIRD]
 
 
 def whole_spec(array):
@@ -841,9 +845,9 @@
 
 def open_kernel(*refs):
     ins, outs, weight_s, spread_a, spread_b, (own_tokens, own_cot, own_pack, load, *pack_sems) = take(
-        refs, (5, 5, 5, 3, 3, 7)
+        refs, (11, 5, 5, 3, 3, 7)
     )
-    w_in, w_out, pack, tokens, cotangent = ins
+    w_in, w_out, tokens, cotangent, *raw = ins
     tile, tile_out, packs, all_tokens, all_cot = outs
     spot = Spot()
     weights = Weights(spot, 0, w_in, w_out, tile, tile_out, weight_s)
@@ -852,7 +856,7 @@
     loads = [
         pltpu.make_async_copy(src, dst, load.at[n])
         for n, (src, dst) in enumerate(
-            ((tokens.at[spot.s], own_tokens), (cotangent.at[spot.s], own_cot), (pack, own_pack))
+            ((tokens.at[spot.s], own_tokens), (cotangent.at[spot.s], own_cot))
         )
     ]
     pack_here = pltpu.make_async_copy(own_pack, packs.at[spot.s], pack_sems[0])
@@ -865,6 +869,7 @@
         copy.wait()
     rows.start()
     weights.start()
+    pack_params(own_pack, *raw)
     pack_here.start()
     pack_there.start()
     rows.forward()
@@ -882,6 +887,22 @@
     pack_there.wait()
 
 
+def pack_params(pack, conv_weight, conv_bias, gate_gain, skip_gain, norm_gain, dt_bias, a_log):
+    pack[...] = jnp.zeros_like(pack)
+    for p in range(INNER // THIRD):
+        source, target = slice(p * THIRD, (p + 1) * THIRD), slice(p * PIECE, p * PIECE + THIRD)
+        pack[0:CONV, target] = conv_weight[:, source]
+        pack[CONV : CONV + 1, target] = conv_bias[:, source]
+        skips = [jnp.broadcast_to(skip_gain[:, 3 * p + h : 3 * p + h + 1], (1, HEADDIM)) for h in range(3)]
+        pack[5:6, target] = jnp.concatenate(skips, axis=1)
+        pack[6:7, target] = gate_gain[:, source]
+    pack[0:CONV, -SHARED:] = conv_weight[:, INNER:]
+    pack[CONV : CONV + 1, -SHARED:] = conv_bias[:, INNER:]
+    pack[7:8, :GAIN_END] = norm_gain[...]
+    pack[7:8, DT_AT : DT_AT + HEADS] = dt_bias[...]
+    pack[7:8, RATE_AT : RATE_AT + HEADS] = a_log[...]
+
+
 def layer_rows(total, rows_in, branch, scales, rows_out):
     width = rows_in.shape[1]
     square = jnp.sum(total[:, width:], axis=1, keepdims=True)
@@ -913,33 +934,32 @@
         target[rows, :] = total.astype(target.dtype)
 
 
-class GradsAcross:
+class Grads:
     ORDER = (4, 0, 1, 2, 3, 5)
 
     @staticmethod
     def scratch(shard, columns, wide, width):
         return [
-            pltpu.VMEM((2, columns, width), BF16),
-            pltpu.VMEM((2, wide, width), BF16),
-            pltpu.VMEM((3, columns, shard), BF16),
+            pltpu.VMEM((3, columns, width), BF16),
+            pltpu.VMEM((3, wide, width), BF16),
+            pltpu.VMEM((2, columns, shard), BF16),
+            pltpu.VMEM((2, columns, shard), BF16),
             pltpu.VMEM((THIRD, width), BF16),
             DMA((22,)),
-            DMA((22,)),
+            DMA((27,)),
         ]
 
     @staticmethod
     def results(shard, width):
         return [((2, 4 * THIRD, shard), BF16), ((SHARED + HEADS, shard), BF16), ((THIRD, width), BF16)]
 
-    def __init__(self, spot, layer, results, scratch):
-        self.spot, self.layer = spot, layer
+    def __init__(self, spot, results, scratch):
+        self.spot = spot
         self.reduced, self.shared, self.out = results
-        self.cores, self.cores_out, self.planes, self.mate_out, self.send, self.recv = scratch
+        self.cores, self.cores_out, self.planes, self.relay, self.mate_out, self.send, self.recv = scratch
         self.shard = self.planes.shape[2]
         self.others = 2 * (1 - spot.half)
-
-    def here(self, step):
-        pl.when(self.spot.s == self.layer)(step)
+        self.is_gateway = (spot.z == 1) | (spot.z == 2)
 
     def rows(self, n):
         _, first, size = tile_parts(self.spot, 0)[n]
@@ -951,98 +971,110 @@
     def core_copy(self, n):
         buffer, rows = (self.cores_out, pl.ds(0, self.cores_out.shape[1])) if n == 5 else (self.cores, self.rows(n))
         return remote(
-            buffer.at[0, rows], buffer.at[1, rows], self.send.at[n], self.recv.at[n], self.spot.sibling
+            buffer.at[2, rows], buffer.at[1, rows], self.send.at[n], self.recv.at[n], self.spot.sibling
         )
 
-    def product(self, n, proj_grad, normed, normed_out, h_rows):
+    def product(self, layer, n, proj_grad, normed, normed_out, h_rows):
         def flat(value):
             return value.reshape(-1, value.shape[-1])
 
         width = self.cores.shape[2]
+        slot = 2 * (self.spot.s - layer) * (self.spot.s - layer)
         if n == 5:
             total = dot_tn(flat(normed_out[...]), flat(h_rows[:, :, :width]))
-            self.cores_out[0] = total.astype(BF16)
+            self.cores_out[slot] = total.astype(BF16)
         else:
             _, first, size = tile_parts(self.spot, 0)[n]
             total = dot_tn(flat(proj_grad[:, :, first : first + size]), flat(normed[...]))
-            self.cores[0, first : first + size, :] = total.astype(BF16)
-        pl.when(self.spot.s != self.layer)(lambda: self.core_copy(n).start())
-
-    def plane_copy(self, c, n):
-        spot, rows = self.spot, self.rows(n)
-        z = spot.mate if c == 2 else self.others + c
-        slot = 2 if c == 2 else spot.lo
-        place = spot.at_mate if c == 2 else spot.column(z)
+            self.cores[slot, first : first + size, :] = total.astype(BF16)
+        pl.when(self.spot.s != layer)(lambda: self.core_copy(n).start())
+
+    def far_part(self, c, n):
+        return self.cores.at[0, self.rows(n), self.columns(self.others + c)]
+
+    def to_mate(self, n):
+        source = self.cores.at[0, self.rows(n), self.columns(self.spot.mate)]
+        target = self.planes.at[1, self.rows(n)]
+        return remote(source, target, self.send.at[6 + n], self.recv.at[11 + n], self.spot.at_mate)
+
+    def to_relay(self, c, n):
+        j = 2 * n + c
+        target = self.relay.at[c, self.rows(n)]
         return remote(
-            self.cores.at[0, rows, self.columns(z)], self.planes.at[slot, rows],
-            self.send.at[6 + 3 * n + c], self.recv.at[6 + 3 * n + slot], place,
+            self.far_part(c, n), target, self.send.at[11 + j], self.recv.at[16 + j], self.spot.at_mate
         )
 
-    def came(self, c, n):
-        part = self.planes.at[c, self.rows(n)]
-        j = 6 + 3 * n + c
-        return remote(part, part, self.send.at[j], self.recv.at[j], self.spot.at_mate)
+    def to_far(self, c, n):
+        target = self.planes.at[0, self.rows(n)]
+        place = self.spot.column(self.others + c)
+        return remote(
+            self.far_part(c, n), target, self.send.at[11 + 2 * n + c], self.recv.at[6 + n], place
+        )
 
     def out_rows(self, lo):
         return pl.ds(pl.multiple_of(lo * THIRD, 64), THIRD)
 
     def mate_copy(self):
         source = self.cores_out.at[0, self.out_rows(1 - self.spot.lo)]
-        return remote(source, self.mate_out, self.send.at[21], self.recv.at[21], self.spot.at_mate)
+        return remote(source, self.mate_out, self.send.at[21], self.recv.at[26], self.spot.at_mate)
 
     def sent(self, n):
-        @self.here
+        self.to_mate(n).wait_send()
+        for c in range(2):
+            self.to_relay(c, n).wait_send()
+
+    def to_planes(self, n):
+        self.core_copy(n).wait_recv()
+        if n == 5:
+            add_rows(self.cores_out.at[0], [self.cores_out.at[0], self.cores_out.at[1]])
+            self.mate_copy().start()
+            return
+        own, sibling = self.cores.at[0, self.rows(n)], self.cores.at[1, self.rows(n)]
+        add_rows(own, [own, sibling], 48 if n < 4 else 16)
+
+        @pl.when(jnp.logical_not(self.is_gateway))
         def _():
-            for c in range(3):
-                self.plane_copy(c, n).wait_send()
-
-    def to_planes(self, n):
-        @self.here
+            for c in range(2):
+                self.to_relay(c, n).start()
+
+        self.to_mate(n).start()
+
+    def pass_on(self, n):
+        @pl.when(self.is_gateway)
         def _():
-            self.core_copy(n).wait_recv()
-            if n == 5:
-                add_rows(self.cores_out.at[0], [self.cores_out.at[0], self.cores_out.at[1]])
-                self.mate_copy().start()
-                return
-            own, sibling = self.cores.at[0, self.rows(n)], self.cores.at[1, self.rows(n)]
-            add_rows(own, [own, sibling], 48 if n < 4 else 16)
-            for c in range(3):
-                self.plane_copy(c, n).start()
+            for c in range(2):
+                self.to_relay(c, n).wait_recv()
+                target, relay = self.far_part(c, n), self.relay.at[c, self.rows(n)]
+                add_rows(target, [target, relay], 48 if n < 4 else 16)
+                self.to_far(c, n).start()
 
     def gather(self, n):
-        @self.here
-        def _():
-            if n == 5:
-                self.mate_copy().wait_recv()
-                add_rows(self.out, [self.cores_out.at[0, self.out_rows(self.spot.lo)], self.mate_out], 48)
-                return
-            for c in range(3):
-                self.came(c, n).wait_recv()
-            _, first, size = tile_parts(self.spot, 0)[n]
-            mine = self.columns(self.spot.z)
-            chunk = 48 if n < 4 else 16
-
-            @pl.loop(0, size // chunk)
-            def _(r):
-                rows = pl.ds(pl.multiple_of(first + r * chunk, 16), chunk)
-                own = self.cores[0, rows, mine].astype(F32) + self.planes[2, rows, :].astype(F32)
-                other = self.planes[0, rows, :].astype(F32) + self.planes[1, rows, :].astype(F32)
-                if n < 4:
-                    self.reduced[0, rows, :] = own.astype(BF16)
-                    self.reduced[1, rows, :] = other.astype(BF16)
-                else:
-                    rows = pl.ds(pl.multiple_of(r * chunk, 16), chunk)
-                    self.shared[rows, :] = (own + other).astype(BF16)
+        if n == 5:
+            self.mate_copy().wait_recv()
+            add_rows(self.out, [self.cores_out.at[0, self.out_rows(self.spot.lo)], self.mate_out], 48)
+            return
+        self.to_mate(n).wait_recv()
+        self.to_far(0, n).wait_recv()
+        _, first, size = tile_parts(self.spot, 0)[n]
+        mine = self.columns(self.spot.z)
+        chunk = 48 if n < 4 else 16
+
+        @pl.loop(0, size // chunk)
+        def _(r):
+            rows = pl.ds(pl.multiple_of(first + r * chunk, 16), chunk)
+            own = self.cores[0, rows, mine].astype(F32) + self.planes[1, rows, :].astype(F32)
+            other = self.planes[0, rows, :]
+            if n < 4:
+                self.reduced[0, rows, :] = own.astype(BF16)
+                self.reduced[1, rows, :] = other
+            else:
+                rows = pl.ds(pl.multiple_of(r * chunk, 16), chunk)
+                self.shared[rows, :] = (own + other.astype(F32)).astype(BF16)
 
     def finish(self):
-        @self.here
-        def _():
-            self.mate_copy().wait_send()
-
-        @pl.when(self.spot.s != self.layer)
-        def _():
-            for n in self.ORDER:
-                self.core_copy(n).wait_send()
+        self.mate_copy().wait_send()
+        for n in self.ORDER:
+            self.core_copy(n).wait_send()
 
 
 class GradsAround:
@@ -1150,26 +1182,73 @@
 
 
 class SmallSum:
+    SHAPE = (8, 4 * PIECE)
+
     @staticmethod
-    def scratch(pack):
-        return [pltpu.VMEM((6, 8, pack), F32), DMA((5,)), DMA((5,))]
+    def scratch():
+        return [
+            pltpu.VMEM((4,) + SmallSum.SHAPE, F32),
+            pltpu.VMEM((8,) + SmallSum.SHAPE, F32),
+            DMA((9,)),
+            DMA((9,)),
+        ]
 
     def __init__(self, spot, scratch):
         self.spot = spot
-        self.small, self.send, self.recv = scratch
-
-    def copy(self, n):
+        self.small, self.group, self.send, self.recv = scratch
+
+    def to_sibling(self):
+        return remote(
+            self.small.at[0], self.small.at[1], self.send.at[0], self.recv.at[0], self.spot.sibling
+        )
+
+    def to_mate(self):
+        return remote(
+            self.small.at[2], self.small.at[3], self.send.at[1], self.recv.at[1], self.spot.at_mate
+        )
+
+    def to_group(self, j):
         spot = self.spot
-        place = [spot.sibling, spot.at_mate, spot.at_twin, spot.plane(1), spot.plane(2)][n]
-        return remote(self.small.at[0], self.small.at[1 + n], self.send.at[n], self.recv.at[n], place)
-
-    def start(self, n, value):
+        part = self.group.at[4 * spot.half + spot.q]
+        places = [spot.plane(k) for k in (1, 2, 3)] + [spot.at_twin]
+        places += [(spot.s, spot.around[k], spot.twin) for k in (1, 2, 3)]
+        return remote(part, part, self.send.at[2 + j], self.recv.at[2 + j], places[j])
+
+    def begin(self, value):
         self.small[0] = value
-        self.copy(n).start()
-
-    def end(self, n):
-        self.copy(n).wait()
-        return self.small[1 + n]
+        self.to_sibling().start()
+
+    def step(self, n, value=None):
+        if n == 0:
+            self.to_sibling().wait_recv()
+            self.small[2] = value + self.small[1]
+            self.to_mate().start()
+        else:
+            self.to_mate().wait_recv()
+            self.group[4 * self.spot.half + self.spot.q] = self.small[2] + self.small[3]
+            for j in range(7):
+                self.to_group(j).start()
+
+    def finish(self, out):
+        for j in range(7):
+            self.to_group(j).wait_recv()
+        total = self.group[0, :, 2 * PIECE :]
+        for n in range(1, 8):
+            total += self.group[n, :, 2 * PIECE :]
+        for half in range(2):
+            for j in range(2):
+                for q in range(4):
+                    at = (8 * half + 4 * j + q) * PIECE
+                    out[:, at : at + PIECE] = self.group[4 * half + q, :, j * PIECE : (j + 1) * PIECE]
+        out[:, -SHARED:] = total[:, :SHARED]
+        out[7:8, DT_AT : DT_AT + HEADS] = total[7:8, :HEADS]
+        out[7:8, RATE_AT : RATE_AT + HEADS] = total[7:8, LANES : LANES + HEADS]
+        for r in range(8):
+            out[7:8, r * THIRD : (r + 1) * THIRD] = total[r : r + 1, PIECE : PIECE + THIRD]
+        self.to_sibling().wait_send()
+        self.to_mate().wait_send()
+        for j in range(7):
+            self.to_group(j).wait_send()
 
 
 def loading(sources, targets, sems):
@@ -1187,6 +1266,7 @@
     tile, tile_out, all_rows, branch, scales, rows_out = outs
     u, w, wo, pack, *saved, load = layer_s
     spot = Spot()
+    rows_in = rows_in.at[spot.s]
     weights = Weights(spot, 1, w_in, w_out, tile, tile_out, weight_s)
     total = Sum(spot, rows_in.shape[1], sum_s)
     spread = Spread(spot, rows_out, all_rows, spread_s)
@@ -1258,23 +1338,30 @@
         self.mine[seq] = total
 
 
-def turn_kernel(heads, *refs):
-    ins, outs, sum_s, last_s, spread_s, across_s, row_s, back_s, layer_s, (h_rows, payload, *saved) = take(
-        refs, (9, 8, 5, 5, 3, 6, 4, 6, 5, 8)
+def back_kernel(heads, *refs):
+    ins, outs, first_s, last_s, second_s, spread_s, row_s, back_s, layer_s, grads_s, results, around_s, own_s, rest = take(
+        refs, (18, 5, 5, 5, 5, 3, 4, 6, 11, 7, 3, 4, 4, 10)
     )
-    layer_ins, (rows_in, grad_out, branch, scales) = take(ins, (5, 4))
-    all_rows, grad_rows, grad_gain, last_rows, *results, small = outs
-    u, w, wo, pack, load = layer_s
+    (all_rows, all_cot, packs), tiles, kept, own_ins = take(ins, (3, 4, 6, 5))
+    first_rows, tokens, grad_out, branch, scales = own_ins
+    home_rows, home_grads, final, final_out, small_out = outs
+    u, w, wo, pack, *saved, load = layer_s
+    h_rows, h_next, payload, last_rows, last_grad, first_grad, small, send, recv, local = rest
+    proj_grad, normed_out, *scratch = back_s
     spot = Spot()
-    width = rows_in.shape[1]
-    total = Sum(spot, width, sum_s)
+    tokens, grad_out = tokens.at[spot.s], grad_out.at[spot.s]
+    width = first_rows.shape[1]
+    total = Sum(spot, width, first_s)
     last = Sum(spot, width, last_s)
-    spread = Spread(spot, payload, all_rows, spread_s)
-    across = GradsAcross(spot, 1, results, across_s)
+    second = Sum(spot, width, second_s)
+    spread = Spread(spot, payload, h_next, spread_s)
     sums = RowSums(spot, row_s)
-    loads = loading(
-        layer_ins[:3] + [layer_ins[3].at[1], layer_ins[4]], [u, w, wo, pack, h_rows], load
-    )
+    grads = Grads(spot, results, grads_s)
+    around = GradsAround(spot, results, final, final_out, around_s)
+    own = SmallSum(spot, own_s)
+    first_core, last_core = pl.when(spot.s == 0), pl.when(spot.s == 1)
+    loads = loading([all_rows, *tiles[2:], packs, all_cot], [u, w, wo, pack, h_rows], load)
+    reloads = loading([*tiles[:2], *kept], [w, wo, *saved], load)
     for copy in loads:
         copy.start()
     places = [spot.plane(k) for k in (1, 2, 3)] + [spot.column((spot.z + k) % 4) for k in (1, 2, 3)]
@@ -1283,8 +1370,7 @@
     for copy in loads:
         copy.wait()
     ids = [spot.piece(spot.half, j) for j in range(2)]
-    params = load_params((ids, pack))
-    small[...] = jnp.zeros_like(small)
+    params = load_params((ids, pack.at[1]))
 
     @pl.loop(0, 2)
     def _(i):
@@ -1293,133 +1379,122 @@
         sums.start(seq)
         last.start(i)
 
-    proj_grad, normed_out, *scratch = back_s
-
-    @pl.loop(0, 2)
-    def _(i):
-        seq = total.half(i)
+    def backward(layer, params, total, h_ref, aux_of):
+        small[layer] = jnp.zeros(small.shape[1:], F32)
+
+        @pl.loop(0, 2)
+        def _(i):
+            seq = total.half(i)
+            aux = aux_of(seq)
+            outs = (total.parts, proj_grad, normed_out)
+            parts = backward_rows(heads, params, seq, h_ref, aux, saved[1:], w, wo, outs, scratch)
+            add_small(small.at[layer], *parts)
+            total.start(i)
+
+    def row_aux(seq):
         sums.finish(seq)
-        aux = aux_of_rows(sums.mine[seq])
-        outs = (total.parts, proj_grad, normed_out)
-        parts = backward_rows(heads, params, seq, h_rows, aux, saved[1:], w, wo, outs, scratch)
-        add_small(small, ids, *parts)
-        total.start(i)
-
-    def product(n):
-        across.product(n, proj_grad, saved[0], normed_out, h_rows)
-
-    last.forward()
-    product(4)
-    product(0)
+        return aux_of_rows(sums.mine[seq])
+
+    backward(1, params, total, h_rows, row_aux)
+
+    def product(layer, n):
+        grads.product(layer, n, proj_grad, saved[0], normed_out, h_rows if layer else h_next)
+
+    product(1, 4)
+    product(1, 0)
     total.forward()
-    across.to_planes(4)
-    across.to_planes(0)
-    grad, gain_row = norm_back(total.finish(), rows_in, pack[7:8, :width], grad_out)
+    for n in (1, 2, 3, 5):
+        product(1, n)
+    for copy in reloads:
+        copy.start()
+    grad, last_gain = norm_back(total.finish(), first_rows, pack[1, 7:8, :width], grad_out)
     low = grad.astype(BF16)
-    grad_rows[...] = low
-    grad_gain[...] = stacked([gain_row], 8)
+    last_grad[...] = low
     cross = jnp.sum(low.astype(F32) * branch[...], axis=1, keepdims=True)
     payload[:, :width] = low
-    lanes = lax.broadcasted_iota(jnp.int32, (rows_in.shape[0], LANES), 1)
-    first = split_three(scales[:, 0:1]).astype(F32)
-    second = pltpu.roll(split_three(cross).astype(F32), 3, 1)
-    payload[:, width:] = jnp.where(lanes < 3, first, second).astype(BF16)
+    lanes = lax.broadcasted_iota(jnp.int32, (payload.shape[0], LANES), 1)
+    scale_part = split_three(scales[:, 0:1]).astype(F32)
+    cross_part = pltpu.roll(split_three(cross).astype(F32), 3, 1)
+    payload[:, width:] = jnp.where(lanes < 3, scale_part, cross_part).astype(BF16)
     spread.start()
-    for n in (1, 2, 3, 5):
-        product(n)
+    add_gain(small.at[1], last_gain)
+    first_core(lambda: own.begin(small[1]))
     spread.forward()
-    for n in (1, 2, 3, 5):
-        across.to_planes(n)
-    layer_rows(last.finish(), rows_in, None, None, last_rows)
-    spread.finish()
-    for n in GradsAcross.ORDER:
-        across.gather(n)
-    for n in range(5):
-        across.sent(n)
-    across.finish()
-    total.close()
-    last.close()
-
-
-def close_kernel(heads, *refs):
-    ins, outs, sum_s, across_s, results, around_s, small_s, back_s, layer_s, rest = take(
-        refs, (19, 5, 5, 6, 3, 4, 3, 6, 11, 6)
-    )
-    layer_ins, (rows_in, last_rows, last_grad, small_1, gain_1), last_results = take(ins, (11, 5, 3))
-    home_rows, home_grads, final, final_out, small_out = outs
-    grad_rows, small_in, send, recv, local, load = rest
-    first_rows, *layer_ins = layer_ins
-    h_rows, w, wo, pack, normed, *saved, layer_load = layer_s
-    spot = Spot()
-    width = rows_in.shape[1]
-    total = Sum(spot, width, sum_s)
-    across = GradsAcross(spot, 0, results, across_s)
-    layer_loads = loading(
-        layer_ins[:3] + [layer_ins[3].at[0]] + layer_ins[4:], layer_s[:-1], layer_load
-    )
-    around = GradsAround(spot, results, final, final_out, around_s)
-    small = SmallSum(spot, small_s)
-    first_core, last_core = pl.when(spot.s == 0), pl.when(spot.s == 1)
-    loads = [
-        pltpu.make_async_copy(src, dst, load.at[n]) for n, (src, dst) in enumerate(zip(last_results, results))
-    ]
 
     @last_core
     def _():
-        for copy in loads:
-            copy.start()
-
-    for copy in layer_loads:
-        copy.start()
-    greet(all_places(spot))
+        for n in (4, 0):
+            grads.to_planes(n)
+        own.step(0, small[1])
+        for n in (1, 2):
+            grads.to_planes(n)
+        grads.pass_on(4)
+
+    spread.finish()
 
     @last_core
     def _():
-        for copy in loads:
-            copy.wait()
+        own.step(1)
+        for n in (3, 5):
+            grads.to_planes(n)
+        for n in (0, 1):
+            grads.pass_on(n)
+
+    last.forward()
+    for copy in reloads:
+        copy.wait()
+    params = load_params((ids, pack.at[0]))
+
+    backward(0, params, second, h_next, lambda seq: aux_of_columns(h_next, seq, width))
+    for n in Grads.ORDER:
+        product(0, n)
+
+    @first_core
+    def _():
+        for n in (4, 0, 1):
+            grads.to_planes(n)
+
+    @last_core
+    def _():
+        for n in (2, 3):
+            grads.pass_on(n)
+        grads.gather(4)
         around.shared_step(0)
-        for n in range(4):
+        for n in (0, 1):
+            grads.gather(n)
             around.send_part(n)
+
+    second.forward()
+
+    @first_core
+    def _():
+        grads.pass_on(4)
+        grads.to_planes(2)
+        grads.pass_on(0)
+        grads.to_planes(3)
+        grads.gather(4)
+        around.shared_step(0)
+        grads.pass_on(1)
+        grads.gather(0)
+        around.send_part(0)
+        grads.to_planes(5)
+        grads.pass_on(2)
+
+    @last_core
+    def _():
+        grads.gather(2)
+        around.send_part(2)
+        around.shared_step(1)
+        around.pass_part(0)
+        grads.gather(3)
+        around.send_part(3)
+        grads.gather(5)
         around.send_out()
-
-    for copy in layer_loads:
-        copy.wait()
-    proj_grad, normed_out, *scratch = back_s
-    ids = [spot.piece(spot.half, j) for j in range(2)]
-    params = load_params((ids, pack))
-    small_in[...] = jnp.zeros_like(small_in)
-
-    @pl.loop(0, 2)
-    def _(i):
-        seq = total.half(i)
-        aux = aux_of_columns(h_rows, seq, width)
-        outs = (total.parts, proj_grad, normed_out)
-        sums = backward_rows(heads, params, seq, h_rows, aux, saved, w, wo, outs, scratch)
-        add_small(small_in.at[0], ids, *sums)
-        total.start(i)
-
-    order = GradsAcross.ORDER
-
-    def product(n):
-        across.product(n, proj_grad, normed, normed_out, h_rows)
-
-    for n in order[:3]:
-        product(n)
-    for n in order[:3]:
-        across.to_planes(n)
-    total.forward()
-    for n in order[3:]:
-        product(n)
-    for at in range(3, 6):
-        across.sent(order[at - 3])
-        across.to_planes(order[at])
-    across.gather(4)
-    first_core(lambda: around.shared_step(0))
-    across.gather(0)
-    first_core(lambda: around.send_part(0))
-    grad, gain_row = norm_back(total.finish(), rows_in, pack[7:8, :width], last_grad)
-    grad_rows[...] = grad.astype(BF16)
-    layers = ((first_rows, grad_rows), (last_rows, last_grad))
+        around.pass_part(1)
+
+    grad, first_gain = norm_back(second.finish(), tokens, pack[0, 7:8, :width], last_grad)
+    first_grad[...] = grad.astype(BF16)
+    layers = ((first_rows, first_grad), (last_rows, last_grad))
 
     def home_copies(s):
         copies = []
@@ -1428,10 +1503,9 @@
             copies.append(pltpu.make_async_copy(layers[s][n], target.at[s], local.at[n]))
         return copies
 
-    small_in[1] = small_1[...]
-    small_in[0, 7:8, :width] = gain_row
-    small_in[1, 7:8, :width] = gain_1[0:1]
-    small.start(0, small_in[1 - spot.s])
+    add_gain(small.at[0], first_gain)
+    last_core(lambda: own.begin(small[0]))
+    layer_rows(last.finish(), first_rows, None, None, last_rows)
     for s in range(2):
 
         @pl.when(spot.s == s)
@@ -1439,34 +1513,39 @@
             for copy in home_copies(s):
                 copy.start()
 
-    across.gather(1)
-    first_core(lambda: around.send_part(1))
-    running = small_in[spot.s] + small.end(0)
-    small.start(1, running)
-    around.shared_step(1)
-    around.pass_part(0)
-    across.gather(2)
-    first_core(lambda: around.send_part(2))
-    running = running + small.end(1)
-    small.start(2, running)
-    around.pass_part(1)
-    across.gather(3)
-    first_core(lambda: around.send_part(3))
-    running = running + small.end(2)
-    small.start(3, running)
-    around.shared_step(2)
-    across.gather(5)
-    first_core(around.send_out)
-    around.pass_part(2)
-    running = running + small.end(3)
-    small.start(4, running)
-    around.pass_part(3)
-    around.pass_out()
-    small_out[...] = running + small.end(4)
+    @first_core
+    def _():
+        grads.pass_on(3)
+        grads.gather(1)
+        around.send_part(1)
+        around.shared_step(1)
+        around.pass_part(0)
+        own.step(0, small[0])
+        grads.gather(2)
+        around.send_part(2)
+        around.pass_part(1)
+        around.shared_step(2)
+        own.step(1)
+        grads.gather(3)
+        around.send_part(3)
+        grads.gather(5)
+        around.send_out()
+        for n in (2, 3):
+            around.pass_part(n)
+        around.pass_out()
+
+    @last_core
+    def _():
+        around.shared_step(2)
+        for n in (2, 3):
+            around.pass_part(n)
+        around.pass_out()
+
+    own.finish(small_out)
     around.finish()
-    for n in order[3:5]:
-        across.sent(n)
-    across.finish()
+    for n in range(5):
+        grads.sent(n)
+    grads.finish()
     for s in range(2):
 
         @pl.when(spot.s == s)
@@ -1475,6 +1554,8 @@
                 copy.wait()
 
     total.close()
+    last.close()
+    second.close()
 
 
 def comm_call(kernel, collective, ins, in_specs, outs, out_specs, scratch, name):
@@ -1494,110 +1575,138 @@
 def fast_shards(
     tokens, cotangent, norm_gain, w_in, conv_weight, conv_bias, dt_bias, a_log, skip_gain, gate_gain, w_out
 ):
-    section = lax.axis_index("section")
     span, width = tokens.shape[2:]
     heads = HEADS // 8
     wide = heads * HEADDIM
     columns = 2 * wide + SHARED + HEADS
     shard = w_in.shape[1]
     rows_in = w_in[0].T
-    channels = jnp.concatenate(
-        [
-            conv_weight[0, :, :INNER], conv_bias[:, :INNER],
-            jnp.repeat(skip_gain[0], HEADDIM)[None], gate_gain,
-        ]
-    )
-    channels = widened(channels.reshape(7, -1, THIRD), 2, PIECE).reshape(7, -1)
-    shared = jnp.concatenate([conv_weight[0, :, INNER:], conv_bias[:, INNER:], jnp.zeros((2, SHARED))])
-    last_row = jnp.concatenate(
-        [norm_gain, widened(dt_bias, 1, LANES), widened(a_log, 1, LANES)], axis=1
-    )
-    pack = jnp.concatenate([channels, shared], axis=1)
-    pack = jnp.concatenate([pack, widened(last_row, 1, pack.shape[1])])
+    pack_shape = (8, INNER // THIRD * PIECE + SHARED)
     group = (2, 4 * span, width)
     weight_outs = [((columns, width), BF16), ((wide, width), BF16)]
     weight_s = Weights.scratch(columns, shard, width)
     payload = width + LANES
     tile, tile_out, packs, all_rows, all_cot = comm_call(
         open_kernel, 1,
-        [rows_in, w_out[0], pack, tokens[:, 0], cotangent[:, 0]], [ANY] * 5,
-        weight_outs + [((2,) + pack.shape, F32), (group, BF16), (group, BF16)], [ANY] * 5,
+        [
+            rows_in, w_out[0], tokens[:, 0], cotangent[:, 0], conv_weight[0], conv_bias, gate_gain, skip_gain,
+            norm_gain, dt_bias, a_log,
+        ],
+        [ANY] * 4 + [VMEM] * 7,
+        weight_outs + [((2,) + pack_shape, F32), (group, BF16), (group, BF16)], [ANY] * 5,
         weight_s + Spread.SEMS + Spread.SEMS
-        + [pltpu.VMEM((span, width), BF16)] * 2 + [pltpu.VMEM(pack.shape, F32), DMA((3,)), DMA, DMA, DMA],
+        + [pltpu.VMEM((span, width), BF16)] * 2 + [pltpu.VMEM(pack_shape, F32), DMA((2,)), DMA, DMA, DMA],
         "open",
     )
-    own_tokens = lax.dynamic_index_in_dim(tokens[:, 0], section, 0, False)
-    own_cot = lax.dynamic_index_in_dim(cotangent[:, 0], section, 0, False)
     length = 4 * span
     rows_spec = ((span, width), BF16)
     layer_s = [
         pltpu.VMEM((2, length, width), BF16), pltpu.VMEM((columns, width), BF16),
-        pltpu.VMEM((wide, width), BF16), pltpu.VMEM(pack.shape, F32),
+        pltpu.VMEM((wide, width), BF16), pltpu.VMEM(pack_shape, F32),
     ]
     kept_shapes = saved_shapes(length, width, wide)
     kept_s = [pltpu.VMEM(*k) for k in kept_shapes]
     back_s = [pltpu.VMEM((2, length, columns), BF16), pltpu.VMEM((2, length, wide), BF16)]
     back_s += backward_scratch(length, wide)
-    results = GradsAcross.results(shard, width)
-    across_s = GradsAcross.scratch(shard, columns, wide, width)
+    results = Grads.results(shard, width)
     sum_s = Sum.scratch(span, width)
     first_tiles = [tile, tile_out]
     tile, tile_out, all_rows, branch, scales, rows, *kept = comm_call(
         partial(middle_kernel, heads), 2,
-        [rows_in, w_out[0], all_rows, tile, tile_out, packs, own_tokens], [ANY] * 6 + [VMEM],
+        [rows_in, w_out[0], all_rows, tile, tile_out, packs, tokens[:, 0]], [ANY] * 6 + [VMEM],
         weight_outs + [(group, BF16), ((span, width), F32), ((span, LANES), F32), rows_spec] + kept_shapes,
         [ANY] * 3 + [VMEM] * 3 + [ANY] * 6,
         weight_s + Sum.scratch(span, payload) + Spread.SEMS + layer_s + kept_s + [DMA((4,)), DMA((6,))],
         "middle",
     )
-    all_grads, last_grad, gain_1, last_rows, *last_results, small_1 = comm_call(
-        partial(turn_kernel, heads), 3,
-        [all_rows, tile, tile_out, packs, all_cot, rows, own_cot, branch, scales],
-        [ANY] * 5 + [VMEM] * 4,
-        [((2, length, payload), BF16), rows_spec, ((8, width), F32), rows_spec]
-        + results + [(pack.shape, F32)],
-        [ANY] + [VMEM] * 7,
-        sum_s + Sum.scratch(span, payload) + Spread.SEMS + across_s + RowSums.scratch(length) + back_s
-        + layer_s + [DMA((5,)), pltpu.VMEM((2, length, width), BF16), pltpu.VMEM((span, payload), BF16)]
-        + kept_s,
-        "turn",
-    )
     home_rows, home_grads, final, final_out, small = comm_call(
-        partial(close_kernel, heads), 4,
+        partial(back_kernel, heads), 3,
         [
-            rows, all_grads, *first_tiles, packs, *kept,
-            own_tokens, last_rows, last_grad, small_1, gain_1, *last_results,
+            all_rows, all_cot, packs, *first_tiles, tile, tile_out, *kept,
+            rows, tokens[:, 0], cotangent[:, 0], branch, scales,
         ],
-        [VMEM] + [ANY] * 10 + [VMEM] * 5 + [ANY] * 3,
+        [ANY] * 13 + [VMEM] * 5,
         [
             ((2, span, width), BF16), ((2, span, width), BF16),
-            ((2 * INNER + SHARED + HEADS, shard), BF16), (w_out.shape[1:], BF16), (pack.shape, F32),
+            ((2 * INNER + SHARED + HEADS, shard), BF16), (w_out.shape[1:], BF16), (pack_shape, F32),
         ],
         [ANY] * 4 + [VMEM],
-        sum_s + across_s + [pltpu.VMEM(*r) for r in results]
-        + GradsAround.scratch(shard) + SmallSum.scratch(pack.shape[1]) + back_s
-        + [pltpu.VMEM((2, length, payload), BF16)] + layer_s[1:] + kept_s + [DMA((10,))]
+        sum_s + Sum.scratch(span, payload) + sum_s + Spread.SEMS + RowSums.scratch(length) + back_s
+        + layer_s[:3] + [pltpu.VMEM((2,) + pack_shape, F32)] + kept_s + [DMA((8,))]
+        + Grads.scratch(shard, columns, wide, width) + [pltpu.VMEM(*r) for r in results]
+        + GradsAround.scratch(shard) + SmallSum.scratch()
         + [
-            pltpu.VMEM((span, width), BF16), pltpu.VMEM((2,) + pack.shape, F32),
-            DMA((2,)), DMA((2,)), DMA((2,)), DMA((3,)),
+            pltpu.VMEM((2, length, width), BF16), pltpu.VMEM((2, length, payload), BF16),
+            pltpu.VMEM((span, payload), BF16), *[pltpu.VMEM((span, width), BF16)] * 3,
+            pltpu.VMEM((2,) + SmallSum.SHAPE, F32), DMA((2,)), DMA((2,)), DMA((2,)),
         ],
-        "close",
+        "back",
     )
-    by_channel = small[:7, :-SHARED].reshape(7, -1, PIECE)[:, :, :THIRD].reshape(7, INNER)
-    conv_rows = jnp.concatenate([by_channel[: CONV + 1], small[: CONV + 1, -SHARED:]], axis=1)
+    grad_in, grad_out, gain, conv, bias, shift, rate, skip, gate = finish_call(final, final_out, small)
     return (
-        home_rows[None, :, None],
-        home_grads[None, :, None],
-        small[7:8, :width],
-        final.astype(F32).T[None],
-        conv_rows[None, :CONV],
-        conv_rows[CONV:],
-        small[7:8, DT_AT : DT_AT + HEADS],
-        small[7:8, RATE_AT : RATE_AT + HEADS],
-        by_channel[5].reshape(HEADS, HEADDIM).sum(-1)[None],
-        by_channel[6:7],
-        final_out[None].astype(F32),
+        home_rows[None, :, None], home_grads[None, :, None], gain, grad_in.T[None], conv[None],
+        bias, shift, rate, skip, gate, grad_out[None],
     )
+
+
+def finish_kernel(final, final_out, small, grad_in, grad_out, gain, conv, bias, shift, rate, skip, gate):
+    grad_in[...] = final[...].astype(F32)
+    step = pl.program_id(0)
+    grad_out[...] = final_out[...].astype(F32)
+
+    @pl.when(step == 0)
+    def _():
+        gain[...] = small[7:8, :GAIN_END]
+        shift[...] = small[7:8, DT_AT : DT_AT + HEADS]
+        rate[...] = small[7:8, RATE_AT : RATE_AT + HEADS]
+        heads = []
+        for p in range(INNER // THIRD):
+            source, target = slice(p * PIECE, p * PIECE + THIRD), slice(p * THIRD, (p + 1) * THIRD)
+            conv[:, target] = small[0:CONV, source]
+            bias[:, target] = small[CONV : CONV + 1, source]
+            gate[:, target] = small[6:7, source]
+            for h in range(3):
+                part = small[5:6, p * PIECE + h * HEADDIM : p * PIECE + (h + 1) * HEADDIM]
+                heads.append(jnp.sum(part, axis=1, keepdims=True))
+        skip[...] = jnp.concatenate(heads, axis=1)
+        conv[:, INNER:] = small[0:CONV, -SHARED:]
+        bias[:, INNER:] = small[CONV : CONV + 1, -SHARED:]
+
+
+def finish_call(final, final_out, small):
+    rows, shard = final.shape
+    out_rows, width = final_out.shape
+    steps = 13
+    out_steps = 12
+    assert rows % (16 * steps) == 0 and out_rows % (16 * out_steps) == 0
+    smalls = [(1, GAIN_END), (CONV, XBC), (1, XBC), (1, HEADS), (1, HEADS), (1, HEADS), (1, INNER)]
+
+    def in_block(i):
+        return (i, 0)
+
+    def out_block(i):
+        return (jnp.minimum(i, out_steps - 1), 0)
+
+    def same(i):
+        return (0, 0)
+
+    return pl.pallas_call(
+        finish_kernel,
+        grid=(steps,),
+        out_shape=[jax.ShapeDtypeStruct(s, F32) for s in [final.shape, final_out.shape] + smalls],
+        in_specs=[
+            pl.BlockSpec((rows // steps, shard), in_block),
+            pl.BlockSpec((out_rows // out_steps, width), out_block),
+            pl.BlockSpec(small.shape, same),
+        ],
+        out_specs=[
+            pl.BlockSpec((rows // steps, shard), in_block),
+            pl.BlockSpec((out_rows // out_steps, width), out_block),
+        ]
+        + [pl.BlockSpec(s, same) for s in smalls],
+        compiler_params=pltpu.CompilerParams(**PARAMS),
+        name="finish",
+    )(final, final_out, small)
 
 
 def shards(

time: 347 us -> 290 us (0.84)
  Pallas kernels: 318 us -> 285 us
  other arithmetic: 15.2 us -> 0 us
  local copies, waits for them, and re-layouts: 12.4 us -> 1.5 us
    pallas_call x4 -> x3, Pallas kernels: 318 us -> 273 us  [comm_call(): pl.pallas_call(kernel, out_shape=[jax.ShapeDtypeStruct(s, t) for s, t in...]
    pallas_call x0 -> x1, Pallas kernels: none -> 12.6 us  [finish_call(): pl.pallas_call(finish_kernel, grid=(steps,), out_shape=[jax.ShapeDtypeStr...]
    slice x11 -> x0, local copies, waits for them, and re-layouts: 7.21 us -> none  [the longest x1 1.4 us: fast_shards(): small[7:8, :width]]
    broadcast_in_dim x2 -> x0, other arithmetic: 5.17 us -> none  [the longest x1 4.53 us: fast_shards(): final.astype(F32).T[None]]
    convert_element_type x1 -> x0, other arithmetic: 4.65 us -> none  [fast_shards(): final_out[None].astype(F32)]
where the time goes in v5:
time: 290 us; the launch traced here: 288 us
  Pallas kernels  285 us (98%)
    pallas_call x3, Pallas kernels, comm_call(): pl.pallas_call(kernel, out_shape=[jax.ShapeDtypeStruct(s, t) for s, t in...  273 us
    pallas_call x1, Pallas kernels, finish_call(): pl.pallas_call(finish_kernel, grid=(steps,), out_shape=[jax.ShapeDtypeStr...  12.6 us

profile of v5, /device:TPU:0, one launch (start us, length us, event | category | flops | bytes accessed | tf_op | source)
XLA Modules:
  0.0 287.7 jit_solution(3784726604045620268)
XLA Ops:
  0.6 56.9 %open.1 = (bf16[1072,1536]{1,0:T(8,128)(2,1)}, bf16[384,1536]{1,0:T(8,128)(2,1)}, f32[2,8,4352]{2,1,0:T(8,128)}, bf16[2,256,1536]{2,1,0:T(8,128)(2,1)}, bf16[2,256,1536]{2,1,0:T(8,128)(2,1)}) custom-call(bf16[6448,384]{1,0:T(8,128)(2,1)} %bitcast.18, bf16[768,1536]{1,0:T(8,128)(2,1)} %bitcast.20, bf16[2,64,1536]{2,1,0:T(8,128)(2,1)} %bitcast.22, ...), custom_call_target="tpu_custom_call" | custom-call | tf_op jit(solution)/shard_map/open/pallas_call | solution.py:1562
  57.6 56.7 %middle.1 = (bf16[1072,1536]{1,0:T(8,128)(2,1)}, bf16[384,1536]{1,0:T(8,128)(2,1)}, bf16[2,256,1536]{2,1,0:T(8,128)(2,1)}, f32[64,1536]{1,0:T(8,128)}, f32[64,12...) custom-call(bf16[6448,384]{1,0:T(8,128)(2,1)} %bitcast.19, ...), custom_call_target="tpu_custom_call" | custom-call | tf_op jit(solution)/shard_map/middle/pallas_call | solution.py:1562
  114.3 159.3 %back.1 = (bf16[2,64,1536]{2,1,0:T(8,128)(2,1)}, bf16[2,64,1536]{2,1,0:T(8,128)(2,1)}, bf16[6448,384]{1,0:T(8,128)(2,1)}, bf16[768,1536]{1,0:T(8,128)(2,1)}, f32[8,4352]{1,0:T(8,128)}) custom-call(bf16[2,256,1536]{2,1,0:T(8,128)(2,1)} %get-tuple-element.46.refs_0_, bf16[2,256,1536]{2,1,0:T(8,128)(2,1)} %get-tuple-element.47.refs_1_, ...), custom_call_target="tpu_custom_call" | custom-call | tf_op jit(solution)/shard_map/back/pallas_call | solution.py:1562
  273.5 0.0 copy-start.1
  273.5 0.0 copy-start
  273.5 12.6 %finish.1 = (f32[6448,384]{1,0:T(8,128)}, f32[768,1536]{1,0:T(8,128)}, f32[1,1536]{1,0:T(1,128)}, f32[4,3328]{1,0:T(4,128)}, f32[1,3328]{1,0:T(1,128)}, /*index=...) custom-call(bf16[6448,384]{1,0:T(8,128)(2,1)} %get-tuple-element.61.final, ...), custom_call_target="tpu_custom_call" | custom-call | tf_op jit(solution)/shard_map/finish/pallas_call | solution.py:1693
  286.2 0.0 copy-done.1
  286.2 0.7 copy.26
  286.9 0.0 copy-done
  286.9 0.7 copy.27
Async XLA Ops:
  273.5 12.6 %copy-start.1 = (bf16[2,64,1536]{2,1,0:T(8,128)(2,1)S(1)}, bf16[2,64,1536]{2,1,0:T(8,128)(2,1)}, u32[]{:S(2)}) copy-start(bf16[2,64,1536]{2,1,0:T(8,128)(2,1)} %get-tuple-element.59) | copy-start | bytes 1179652
  273.5 13.4 %copy-start = (bf16[2,64,1536]{2,1,0:T(8,128)(2,1)S(1)}, bf16[2,64,1536]{2,1,0:T(8,128)(2,1)}, u32[]{:S(2)}) copy-start(bf16[2,64,1536]{2,1,0:T(8,128)(2,1)} %get-tuple-element.60) | copy-start | bytes 1179652

commit v6 on v5

--- a/solution.py
+++ b/solution.py
@@ -612,12 +612,23 @@
         for j in (4, 5, 6):
             self.copy(j).start()
 
-    def finish(self):
-        for j in (0, 1, 2, 4, 5, 6):
+    def own_half(self):
+        for j in (0, 1, 2):
             self.copy(j).wait_recv()
+        self.here().wait()
+
+    def other_half(self):
+        for j in (4, 5, 6):
+            self.copy(j).wait_recv()
+
+    def close(self):
         for j in range(7):
             self.copy(j).wait_send()
-        self.here().wait()
+
+    def finish(self):
+        self.own_half()
+        self.other_half()
+        self.close()
 
 
 class Sum:
@@ -1377,25 +1388,41 @@
         seq = last.half(i)
         forward_rows(heads, params, seq, u, w, wo, h_rows, [last.parts, sums.mine, *saved])
         sums.start(seq)
-        last.start(i)
-
-    def backward(layer, params, total, h_ref, aux_of):
+        pl.when(i == 0)(lambda: last.start(0))
+
+    def backward(layer, params, total, h_ref, aux_of, order):
         small[layer] = jnp.zeros(small.shape[1:], F32)
 
         @pl.loop(0, 2)
-        def _(i):
+        def _(n):
+            i = order(n)
             seq = total.half(i)
-            aux = aux_of(seq)
+            aux = aux_of(n, seq)
             outs = (total.parts, proj_grad, normed_out)
             parts = backward_rows(heads, params, seq, h_ref, aux, saved[1:], w, wo, outs, scratch)
             add_small(small.at[layer], *parts)
             total.start(i)
 
-    def row_aux(seq):
+    def row_aux(n, seq):
+        pl.when(n == 1)(last.forward)
         sums.finish(seq)
         return aux_of_rows(sums.mine[seq])
 
-    backward(1, params, total, h_rows, row_aux)
+    def column_aux(n, seq):
+        pl.when(n == 0)(spread.own_half)
+
+        @pl.when((n == 1) & (spot.s == 1))
+        def _():
+            own.step(1)
+            grads.to_planes(5)
+            grads.pass_on(1)
+            grads.gather(4)
+            around.shared_step(0)
+
+        pl.when(n == 1)(spread.other_half)
+        return aux_of_columns(h_next, seq, width)
+
+    backward(1, params, total, h_rows, row_aux, lambda n: n)
 
     def product(layer, n):
         grads.product(layer, n, proj_grad, saved[0], normed_out, h_rows if layer else h_next)
@@ -1403,8 +1430,10 @@
     product(1, 4)
     product(1, 0)
     total.forward()
+    last_core(lambda: grads.to_planes(4))
     for n in (1, 2, 3, 5):
         product(1, n)
+    last_core(lambda: grads.to_planes(0))
     for copy in reloads:
         copy.start()
     grad, last_gain = norm_back(total.finish(), first_rows, pack[1, 7:8, :width], grad_out)
@@ -1419,33 +1448,33 @@
     spread.start()
     add_gain(small.at[1], last_gain)
     first_core(lambda: own.begin(small[1]))
-    spread.forward()
 
     @last_core
     def _():
-        for n in (4, 0):
-            grads.to_planes(n)
-        own.step(0, small[1])
-        for n in (1, 2):
-            grads.to_planes(n)
         grads.pass_on(4)
-
-    spread.finish()
+        grads.to_planes(1)
+
+    spread.forward()
 
     @last_core
     def _():
-        own.step(1)
-        for n in (3, 5):
+        own.step(0, small[1])
+        grads.pass_on(0)
+        for n in (2, 3):
             grads.to_planes(n)
-        for n in (0, 1):
-            grads.pass_on(n)
-
-    last.forward()
+
+    last.start(1)
     for copy in reloads:
         copy.wait()
     params = load_params((ids, pack.at[0]))
-
-    backward(0, params, second, h_next, lambda seq: aux_of_columns(h_next, seq, width))
+    backward(0, params, second, h_next, column_aux, lambda n: 1 - n)
+
+    @last_core
+    def _():
+        grads.gather(0)
+        around.send_part(0)
+        grads.pass_on(2)
+
     for n in Grads.ORDER:
         product(0, n)
 
@@ -1453,43 +1482,46 @@
     def _():
         for n in (4, 0, 1):
             grads.to_planes(n)
-
-    @last_core
-    def _():
-        for n in (2, 3):
-            grads.pass_on(n)
+        grads.pass_on(4)
+        for n in (5, 2):
+            grads.to_planes(n)
+        grads.pass_on(0)
         grads.gather(4)
         around.shared_step(0)
-        for n in (0, 1):
-            grads.gather(n)
-            around.send_part(n)
-
-    second.forward()
-
-    @first_core
-    def _():
-        grads.pass_on(4)
-        grads.to_planes(2)
-        grads.pass_on(0)
         grads.to_planes(3)
-        grads.gather(4)
-        around.shared_step(0)
         grads.pass_on(1)
         grads.gather(0)
         around.send_part(0)
-        grads.to_planes(5)
-        grads.pass_on(2)
 
     @last_core
     def _():
+        grads.gather(1)
+        around.send_part(1)
+        grads.pass_on(3)
+        around.shared_step(1)
+
+    second.forward()
+
+    @first_core
+    def _():
+        grads.pass_on(2)
+        grads.gather(5)
+        around.send_out()
+        grads.gather(1)
+        around.send_part(1)
+        around.shared_step(1)
+        around.pass_part(0)
+        grads.pass_on(3)
+
+    @last_core
+    def _():
+        grads.gather(5)
+        around.send_out()
         grads.gather(2)
         around.send_part(2)
-        around.shared_step(1)
         around.pass_part(0)
         grads.gather(3)
         around.send_part(3)
-        grads.gather(5)
-        around.send_out()
         around.pass_part(1)
 
     grad, first_gain = norm_back(second.finish(), tokens, pack[0, 7:8, :width], last_grad)
@@ -1505,6 +1537,19 @@
 
     add_gain(small.at[0], first_gain)
     last_core(lambda: own.begin(small[0]))
+
+    @first_core
+    def _():
+        grads.gather(2)
+        around.send_part(2)
+        around.pass_out()
+        around.pass_part(1)
+        own.step(0, small[0])
+        grads.gather(3)
+        around.send_part(3)
+        around.shared_step(2)
+        own.step(1)
+
     layer_rows(last.finish(), first_rows, None, None, last_rows)
     for s in range(2):
 
@@ -1515,31 +1560,15 @@
 
     @first_core
     def _():
-        grads.pass_on(3)
-        grads.gather(1)
-        around.send_part(1)
-        around.shared_step(1)
-        around.pass_part(0)
-        own.step(0, small[0])
-        grads.gather(2)
-        around.send_part(2)
-        around.pass_part(1)
-        around.shared_step(2)
-        own.step(1)
-        grads.gather(3)
-        around.send_part(3)
-        grads.gather(5)
-        around.send_out()
         for n in (2, 3):
             around.pass_part(n)
-        around.pass_out()
 
     @last_core
     def _():
         around.shared_step(2)
+        around.pass_out()
         for n in (2, 3):
             around.pass_part(n)
-        around.pass_out()
 
     own.finish(small_out)
     around.finish()
@@ -1556,6 +1585,7 @@
     total.close()
     last.close()
     second.close()
+    spread.close()
 
 
 def comm_call(kernel, collective, ins, in_specs, outs, out_specs, scratch, name):
@@ -1676,16 +1706,12 @@
 def finish_call(final, final_out, small):
     rows, shard = final.shape
     out_rows, width = final_out.shape
-    steps = 13
-    out_steps = 12
-    assert rows % (16 * steps) == 0 and out_rows % (16 * out_steps) == 0
+    steps = 3
+    block, out_block = -(-rows // (16 * steps)) * 16, out_rows // steps
     smalls = [(1, GAIN_END), (CONV, XBC), (1, XBC), (1, HEADS), (1, HEADS), (1, HEADS), (1, INNER)]
 
     def in_block(i):
         return (i, 0)
-
-    def out_block(i):
-        return (jnp.minimum(i, out_steps - 1), 0)
 
     def same(i):
         return (0, 0)
@@ -1695,13 +1721,13 @@
         grid=(steps,),
         out_shape=[jax.ShapeDtypeStruct(s, F32) for s in [final.shape, final_out.shape] + smalls],
         in_specs=[
-            pl.BlockSpec((rows // steps, shard), in_block),
-            pl.BlockSpec((out_rows // out_steps, width), out_block),
+            pl.BlockSpec((block, shard), in_block),
+            pl.BlockSpec((out_block, width), in_block),
             pl.BlockSpec(small.shape, same),
         ],
         out_specs=[
-            pl.BlockSpec((rows // steps, shard), in_block),
-            pl.BlockSpec((out_rows // out_steps, width), out_block),
+            pl.BlockSpec((block, shard), in_block),
+            pl.BlockSpec((out_block, width), in_block),
         ]
         + [pl.BlockSpec(s, same) for s in smalls],
         compiler_params=pltpu.CompilerParams(**PARAMS),

time: 290 us -> 279 us (0.962)
  Pallas kernels: 285 us -> 276 us
    pallas_call x3, Pallas kernels: 273 us -> 267 us  [comm_call(): pl.pallas_call(kernel, out_shape=[jax.ShapeDtypeStruct(s, t) for s, t in...]
    pallas_call x1, Pallas kernels: 12.6 us -> 8.57 us  [finish_call(): pl.pallas_call(finish_kernel, grid=(steps,), out_shape=[jax.ShapeDtypeStr...]
where the time goes in v6:
time: 279 us; the launch traced here: 278 us
  Pallas kernels  276 us (99%)
    pallas_call x3, Pallas kernels, comm_call(): pl.pallas_call(kernel, out_shape=[jax.ShapeDtypeStruct(s, t) for s, t in...  267 us
    pallas_call x1, Pallas kernels, finish_call(): pl.pallas_call(finish_kernel, grid=(steps,), out_shape=[jax.ShapeDtypeStr...  8.57 us

profile of v6, /device:TPU:0, one launch (start us, length us, event | category | flops | bytes accessed | tf_op | source)
XLA Modules:
  0.0 278.2 jit_solution(7663218147875812043)
XLA Ops:
  0.6 56.9 %open.1 = (bf16[1072,1536]{1,0:T(8,128)(2,1)}, bf16[384,1536]{1,0:T(8,128)(2,1)}, f32[2,8,4352]{2,1,0:T(8,128)}, bf16[2,256,1536]{2,1,0:T(8,128)(2,1)}, bf16[2,256,1536]{2,1,0:T(8,128)(2,1)}) custom-call(bf16[6448,384]{1,0:T(8,128)(2,1)} %bitcast.18, bf16[768,1536]{1,0:T(8,128)(2,1)} %bitcast.20, bf16[2,64,1536]{2,1,0:T(8,128)(2,1)} %bitcast.22, ...), custom_call_target="tpu_custom_call" | custom-call | tf_op jit(solution)/shard_map/open/pallas_call | solution.py:1592
  57.6 56.7 %middle.1 = (bf16[1072,1536]{1,0:T(8,128)(2,1)}, bf16[384,1536]{1,0:T(8,128)(2,1)}, bf16[2,256,1536]{2,1,0:T(8,128)(2,1)}, f32[64,1536]{1,0:T(8,128)}, f32[64,12...) custom-call(bf16[6448,384]{1,0:T(8,128)(2,1)} %bitcast.19, ...), custom_call_target="tpu_custom_call" | custom-call | tf_op jit(solution)/shard_map/middle/pallas_call | solution.py:1592
  114.3 153.9 %back.1 = (bf16[2,64,1536]{2,1,0:T(8,128)(2,1)}, bf16[2,64,1536]{2,1,0:T(8,128)(2,1)}, bf16[6448,384]{1,0:T(8,128)(2,1)}, bf16[768,1536]{1,0:T(8,128)(2,1)}, f32[8,4352]{1,0:T(8,128)}) custom-call(bf16[2,256,1536]{2,1,0:T(8,128)(2,1)} %get-tuple-element.46.refs_0_, bf16[2,256,1536]{2,1,0:T(8,128)(2,1)} %get-tuple-element.47.refs_1_, ...), custom_call_target="tpu_custom_call" | custom-call | tf_op jit(solution)/shard_map/back/pallas_call | solution.py:1592
  268.1 0.0 copy-start.1
  268.1 0.0 copy-start
  268.2 8.6 %finish.1 = (f32[6448,384]{1,0:T(8,128)}, f32[768,1536]{1,0:T(8,128)}, f32[1,1536]{1,0:T(1,128)}, f32[4,3328]{1,0:T(4,128)}, f32[1,3328]{1,0:T(1,128)}, /*index=...) custom-call(bf16[6448,384]{1,0:T(8,128)(2,1)} %get-tuple-element.61.final, ...), custom_call_target="tpu_custom_call" | custom-call | tf_op jit(solution)/shard_map/finish/pallas_call | solution.py:1719
  276.7 0.0 copy-done.1
  276.7 0.7 copy.26
  277.5 0.0 copy-done
  277.5 0.7 copy.27
Async XLA Ops:
  268.1 8.6 %copy-start.1 = (bf16[2,64,1536]{2,1,0:T(8,128)(2,1)S(1)}, bf16[2,64,1536]{2,1,0:T(8,128)(2,1)}, u32[]{:S(2)}) copy-start(bf16[2,64,1536]{2,1,0:T(8,128)(2,1)} %get-tuple-element.59) | copy-start | bytes 1179652
  268.1 9.3 %copy-start = (bf16[2,64,1536]{2,1,0:T(8,128)(2,1)S(1)}, bf16[2,64,1536]{2,1,0:T(8,128)(2,1)}, u32[]{:S(2)}) copy-start(bf16[2,64,1536]{2,1,0:T(8,128)(2,1)} %get-tuple-element.60) | copy-start | bytes 1179652

commit v7 on v6

--- a/solution.py
+++ b/solution.py
@@ -699,6 +699,77 @@
         self.across().wait_send()
 
 
+class RelaySum(Sum):
+    @staticmethod
+    def scratch(rows, columns):
+        return [
+            pltpu.VMEM((2, 4 * rows, columns), BF16),
+            pltpu.VMEM((2, 2, rows, columns), BF16),
+            pltpu.VMEM((2, rows, columns), BF16),
+            DMA((9,)),
+            DMA((9,)),
+            pltpu.VMEM((2, rows, columns), BF16),
+        ]
+
+    def __init__(self, spot, width, scratch):
+        super().__init__(spot, width, scratch[:5])
+        self.relays = scratch[5]
+        columns = self.relays.shape[2]
+        cut = columns // 2 // LANES * LANES
+        self.cuts = [(0, cut), (cut, columns - cut)]
+
+    def relay(self, k, i):
+        spot = self.spot
+        columns = pl.ds(*self.cuts[k - 1])
+        return remote(
+            self.parts.at[self.half(i), self.block(spot.around[3]), columns], self.relays.at[i, :, columns],
+            self.send.at[5 + 2 * i + k - 1], self.recv.at[5 + 2 * i + k - 1], spot.plane(k),
+        )
+
+    def copy(self, k, i):
+        spot = self.spot
+        j = 2 * i + k - 1
+        return remote(
+            self.parts.at[self.half(i), self.block(spot.around[k])], self.recv_rows.at[k - 1, i],
+            self.send.at[j], self.recv.at[j], spot.plane(k),
+        )
+
+    def across(self):
+        return remote(
+            self.twin_rows.at[0], self.twin_rows.at[1], self.send.at[4], self.recv.at[4], self.spot.at_twin
+        )
+
+    def start(self, i):
+        for k in (1, 2):
+            self.relay(k, i).start()
+
+    def go_on(self, i):
+        for k in (1, 2):
+            self.relay(k, i).wait_recv()
+            at, size = self.cuts[k - 1]
+            rows = self.block(self.spot.around[3 - k])
+            half = self.half(i)
+            own = self.parts[half, rows, at : at + size].astype(F32)
+            total = own + self.relays[i, :, at : at + size].astype(F32)
+            self.parts[half, rows, at : at + size] = total.astype(BF16)
+        for k in (1, 2):
+            self.copy(k, i).start()
+
+    def plane_total(self, i):
+        total = self.parts[self.half(i), self.block(self.spot.q), :].astype(F32)
+        for k in (1, 2):
+            self.copy(k, i).wait_recv()
+            total += self.recv_rows[k - 1, i].astype(F32)
+        return total
+
+    def close(self):
+        for i in range(2):
+            for k in (1, 2):
+                self.copy(k, i).wait_send()
+                self.relay(k, i).wait_send()
+        self.across().wait_send()
+
+
 def tile_parts(spot, half):
     parts = []
     for part in range(2):
@@ -709,12 +780,14 @@
 
 
 class Weights:
-    PARTS = 5
+    PARTS = 6
+    ORDER = (4, 5, 0, 1, 2, 3)
+    QUARTER = SHARED // 4
 
     @staticmethod
     def scratch(columns, shard, width):
         buffers = [pltpu.VMEM((columns, shard), BF16), pltpu.VMEM((THIRD, width), BF16)]
-        return buffers + [DMA((4,)), DMA((43,)), DMA((43,))]
+        return buffers + [DMA((9,)), DMA((57,)), DMA((57,))]
 
     def __init__(self, spot, layer, w_in, w_out, tile, tile_out, scratch):
         self.spot, self.layer = spot, layer
@@ -728,22 +801,37 @@
     def at_source(self, step):
         pl.when(self.spot.s == self.layer)(step)
 
+    def at_relay(self, step):
+        pl.when(self.spot.s != self.layer)(step)
+
+    def parts(self, half, n):
+        if n < 4:
+            return tile_parts(self.spot, half)[n]
+        if n == 5:
+            return 2 * INNER + SHARED, 4 * THIRD + SHARED, HEADS
+        at = self.QUARTER * self.spot.q
+        return (
+            pl.multiple_of(2 * INNER + at, 64), pl.multiple_of(4 * THIRD + at, 64), self.QUARTER
+        )
+
     def source(self, half, n):
-        first, _, size = tile_parts(self.spot, half)[n]
+        first, _, size = self.parts(half, n)
         return self.w_in.at[pl.ds(first, size)]
 
     def target(self, z, n):
-        _, first, size = tile_parts(self.spot, 0)[n]
+        _, first, size = self.parts(0, n)
         columns = pl.ds(pl.multiple_of(z * self.shard, LANES), self.shard)
         return self.tile.at[pl.ds(first, size), columns]
 
+    def buffered(self, n):
+        _, first, size = self.parts(0, n)
+        return self.buffer.at[pl.ds(first, size)]
+
     def load(self, n):
-        part = self.buffer.at[pl.ds(*tile_parts(self.spot, 0)[n][1:])]
-        return pltpu.make_async_copy(self.source(self.spot.half, n), part, self.send.at[n])
-
-    def store(self):
-        columns = pl.ds(pl.multiple_of(self.spot.z * self.shard, LANES), self.shard)
-        return pltpu.make_async_copy(self.buffer, self.tile.at[:, columns], self.local.at[0])
+        return pltpu.make_async_copy(self.source(self.spot.half, n), self.buffered(n), self.send.at[n])
+
+    def store(self, n):
+        return pltpu.make_async_copy(self.buffered(n), self.target(self.spot.z, n), self.local.at[3 + n])
 
     def out_home(self):
         return Home(
@@ -757,16 +845,17 @@
 
     def to_gateway(self, n):
         source, target = self.source(1 - self.spot.half, n), self.target(self.spot.z, n)
-        j = 5 + 5 * self.spot.lo + n
-        return remote(source, target, self.send.at[5 + n], self.recv.at[j], self.spot.column(self.gateway))
+        j = 6 + 6 * self.spot.lo + n
+        place = (1 - self.spot.s, self.spot.q, self.gateway)
+        return remote(source, target, self.send.at[6 + n], self.recv.at[j], place)
 
     def passed(self, c, n):
         part = self.target(self.others + c, n)
-        j = 5 * c + n
-        return remote(part, part, self.send.at[10 + j], self.recv.at[5 + j], self.spot.at_mate)
+        j = 6 * c + n
+        return remote(part, part, self.send.at[12 + j], self.recv.at[6 + j], self.spot.at_mate)
 
     def to_sibling(self, b, n):
-        j = 20 + 5 * b + n
+        j = 24 + 6 * b + n
         part = self.target([self.spot.z, self.spot.mate, self.others, self.others + 1][b], n)
         source = self.source(self.spot.half, n) if b == 0 else part
         return remote(source, part, self.send.at[j], self.recv.at[j], self.spot.sibling)
@@ -781,7 +870,7 @@
         part = self.out_part(self.spot.lo if n < 2 else 1 - self.spot.lo)
         place = self.spot.sibling if n else self.spot.at_mate
         source = self.out_source() if n < 2 else part
-        return remote(source, part, self.send.at[40 + n], self.recv.at[40 + n], place)
+        return remote(source, part, self.send.at[48 + n], self.recv.at[48 + n], place)
 
     def send_part(self, n):
         if n < self.PARTS:
@@ -797,60 +886,118 @@
                 self.load(n).start()
             self.out_home().begin()
 
-    def start(self):
+    def quarter(self, q):
+        at = 4 * THIRD + self.QUARTER * q
+        return self.tile.at[pl.ds(pl.multiple_of(at, 64), self.QUARTER)]
+
+    def to_plane(self, k):
+        part = self.quarter(self.spot.q)
+        return remote(part, part, self.send.at[50 + k], self.recv.at[50 + k], self.spot.plane(k))
+
+    def quarter_to_sibling(self, k):
+        part = self.quarter(self.spot.around[k])
+        return remote(part, part, self.send.at[53 + k], self.recv.at[53 + k], self.spot.sibling)
+
+    def mates(self):
+        for n in self.ORDER:
+            self.to_mate(n).start()
+        self.out_to(0).start()
+
+    def start(self, window):
         @self.at_source
         def _():
-            for n in range(self.PARTS):
+            for n in self.ORDER:
                 self.load(n).wait()
-            for n in range(self.PARTS):
+            for n in self.ORDER[:window]:
                 self.to_gateway(n).start()
-                self.to_mate(n).start()
-            self.out_to(0).start()
-            for n in range(self.PARTS):
+            pl.when(self.is_gateway)(self.mates)
+            for n in self.ORDER:
                 self.to_sibling(0, n).start()
+                self.store(n).start()
             self.out_to(1).start()
-            self.store().start()
             self.out_home().go_on()
 
-    def step(self, n):
+    def more(self, at, window):
         @self.at_source
         def _():
-            for b in range(2):
-                self.passed(b, n).wait_recv()
-                pl.when(self.is_gateway)(lambda b=b: self.passed(b, n).start())
-                self.to_sibling(2 + b, n).start()
-            self.to_mate(n).wait_recv()
-            self.to_sibling(1, n).start()
-
-    def finish(self):
+            self.to_gateway(self.ORDER[at - window]).wait_send()
+            self.to_gateway(self.ORDER[at]).start()
+            if at == self.PARTS - 1:
+                pl.when(jnp.logical_not(self.is_gateway))(self.mates)
+
+    def relay(self, at):
+        n = self.ORDER[at]
+
+        @self.at_relay
+        def _():
+            for c in range(2):
+                self.passed(c, n).wait_recv()
+                pl.when(self.is_gateway)(lambda c=c: self.passed(c, n).start())
+                self.to_sibling(2 + c, n).start()
+
+    def share(self):
         @self.at_source
         def _():
+            self.store(4).wait()
+            self.to_mate(4).wait_recv()
+            self.to_sibling(1, 4).start()
+            for c in range(2):
+                self.to_sibling(2 + c, 4).wait_recv()
+            for k in (1, 2, 3):
+                self.to_plane(k).start()
+
+    def shared(self):
+        @self.at_source
+        def _():
+            for k in (1, 2, 3):
+                self.to_plane(k).wait_recv()
+                self.quarter_to_sibling(k).start()
+
+    def relay_mate(self):
+        @self.at_source
+        def _():
+            for n in self.ORDER[1:]:
+                self.to_mate(n).wait_recv()
+                self.to_sibling(1, n).start()
             self.out_to(0).wait_recv()
             self.out_to(2).start()
-            for n in range(self.PARTS):
+
+    def finish(self, window):
+        @self.at_source
+        def _():
+            for n in self.ORDER[-window:]:
                 self.to_gateway(n).wait_send()
+            for n in self.ORDER:
                 self.to_mate(n).wait_send()
-                for c in range(2):
-                    pl.when(self.is_gateway)(lambda c=c, n=n: self.passed(c, n).wait_send())
-                for b in range(4):
+                for b in range(2):
+                    if n != 4:
+                        self.to_sibling(2 + b, n).wait_recv()
                     self.to_sibling(b, n).wait_send()
-            self.store().wait()
+                if n != 4:
+                    self.store(n).wait()
+            for k in (1, 2, 3):
+                self.to_plane(k).wait_send()
+                self.quarter_to_sibling(k).wait_send()
             self.out_home().end()
             for n in range(3):
                 self.out_to(n).wait_send()
 
-        @pl.when(self.spot.s != self.layer)
+        @self.at_relay
         def _():
-            for b in range(4):
-                for n in range(self.PARTS):
-                    self.to_sibling(b, n).wait_recv()
+            for n in self.ORDER:
+                for c in range(2):
+                    self.to_sibling(c, n).wait_recv()
+                    self.to_sibling(2 + c, n).wait_send()
+                    pl.when(self.is_gateway)(lambda c=c, n=n: self.passed(c, n).wait_send())
+            for k in (1, 2, 3):
+                self.quarter_to_sibling(k).wait_recv()
             for n in (1, 2):
                 self.out_to(n).wait_recv()
 
 
 def all_places(spot):
     places = [spot.plane(k) for k in (1, 2, 3)]
-    places += [spot.column((spot.z + k) % 4) for k in (1, 2, 3)]
+    places += [(s, spot.q, (spot.z + k) % 4) for k in (1, 2, 3) for s in range(2)]
     return places + [spot.sibling]
 
 
@@ -878,22 +1025,30 @@
     greet(all_places(spot))
     for copy in loads:
         copy.wait()
+    few = 2
     rows.start()
-    weights.start()
+    weights.start(few)
     pack_params(own_pack, *raw)
     pack_here.start()
     pack_there.start()
+    weights.more(2, few)
     rows.forward()
+    for at in (3, 4, 5):
+        weights.more(at, few)
+    weights.relay(0)
+    weights.relay(1)
+    weights.share()
     grads.start()
-    weights.step(0)
-    weights.step(1)
-    weights.step(2)
+    weights.relay(2)
+    weights.relay(3)
+    weights.shared()
     grads.forward()
-    weights.step(3)
-    weights.step(4)
+    weights.relay(4)
+    weights.relay(5)
+    weights.relay_mate()
     rows.finish()
     grads.finish()
-    weights.finish()
+    weights.finish(few)
     pack_here.wait()
     pack_there.wait()
 
@@ -1286,7 +1441,8 @@
         copy.start()
     weights.begin()
     greet(all_places(spot))
-    weights.start()
+    few = 3
+    weights.start(few)
     for copy in loads:
         copy.wait()
     params = load_params(([spot.piece(spot.half, j) for j in range(2)], pack))
@@ -1296,21 +1452,32 @@
         forward_rows(heads, params, total.half(i), u, w, wo, None, [total.parts, None, *saved])
         total.start(i)
 
+
+        @pl.when(i == 0)
+        def _():
+            weights.more(3, few)
+            weights.more(4, few)
+
     stores = loading(saved, kept, store)
     for copy in stores:
         copy.start()
-    weights.step(0)
+    weights.more(5, few)
     total.forward()
-    weights.step(1)
+    weights.relay(0)
+    weights.relay(1)
+    weights.relay(2)
+    weights.share()
     layer_rows(total.finish(), rows_in, branch, scales, rows_out)
     spread.start()
-    weights.step(2)
+    weights.shared()
+    weights.relay(3)
     spread.forward()
-    weights.step(3)
-    weights.step(4)
+    weights.relay(4)
+    weights.relay(5)
+    weights.relay_mate()
     spread.finish()
     total.close()
-    weights.finish()
+    weights.finish(few)
     for copy in stores:
         copy.wait()
 
@@ -1351,7 +1518,7 @@
 
 def back_kernel(heads, *refs):
     ins, outs, first_s, last_s, second_s, spread_s, row_s, back_s, layer_s, grads_s, results, around_s, own_s, rest = take(
-        refs, (18, 5, 5, 5, 5, 3, 4, 6, 11, 7, 3, 4, 4, 10)
+        refs, (18, 5, 5, 6, 6, 3, 4, 6, 11, 7, 3, 4, 4, 10)
     )
     (all_rows, all_cot, packs), tiles, kept, own_ins = take(ins, (3, 4, 6, 5))
     first_rows, tokens, grad_out, branch, scales = own_ins
@@ -1363,8 +1530,8 @@
     tokens, grad_out = tokens.at[spot.s], grad_out.at[spot.s]
     width = first_rows.shape[1]
     total = Sum(spot, width, first_s)
-    last = Sum(spot, width, last_s)
-    second = Sum(spot, width, second_s)
+    last = RelaySum(spot, width, last_s)
+    second = RelaySum(spot, width, second_s)
     spread = Spread(spot, payload, h_next, spread_s)
     sums = RowSums(spot, row_s)
     grads = Grads(spot, results, grads_s)
@@ -1389,6 +1556,8 @@
         forward_rows(heads, params, seq, u, w, wo, h_rows, [last.parts, sums.mine, *saved])
         sums.start(seq)
         pl.when(i == 0)(lambda: last.start(0))
+
+    last.go_on(0)
 
     def backward(layer, params, total, h_ref, aux_of, order):
         small[layer] = jnp.zeros(small.shape[1:], F32)
@@ -1477,6 +1646,9 @@
 
     for n in Grads.ORDER:
         product(0, n)
+    second.go_on(1)
+    second.go_on(0)
+    last.go_on(1)
 
     @first_core
     def _():
@@ -1498,7 +1670,6 @@
         grads.gather(1)
         around.send_part(1)
         grads.pass_on(3)
-        around.shared_step(1)
 
     second.forward()
 
@@ -1522,6 +1693,7 @@
         around.pass_part(0)
         grads.gather(3)
         around.send_part(3)
+        around.shared_step(1)
         around.pass_part(1)
 
     grad, first_gain = norm_back(second.finish(), tokens, pack[0, 7:8, :width], last_grad)
@@ -1542,13 +1714,14 @@
     def _():
         grads.gather(2)
         around.send_part(2)
-        around.pass_out()
-        around.pass_part(1)
         own.step(0, small[0])
         grads.gather(3)
         around.send_part(3)
+        around.pass_out()
+        around.pass_part(1)
+        own.step(1)
+        around.pass_part(2)
         around.shared_step(2)
-        own.step(1)
 
     layer_rows(last.finish(), first_rows, None, None, last_rows)
     for s in range(2):
@@ -1558,17 +1731,14 @@
             for copy in home_copies(s):
                 copy.start()
 
-    @first_core
-    def _():
-        for n in (2, 3):
-            around.pass_part(n)
+    first_core(lambda: around.pass_part(3))
 
     @last_core
     def _():
-        around.shared_step(2)
         around.pass_out()
         for n in (2, 3):
             around.pass_part(n)
+        around.shared_step(2)
 
     own.finish(small_out)
     around.finish()
@@ -1661,7 +1831,7 @@
             ((2 * INNER + SHARED + HEADS, shard), BF16), (w_out.shape[1:], BF16), (pack_shape, F32),
         ],
         [ANY] * 4 + [VMEM],
-        sum_s + Sum.scratch(span, payload) + sum_s + Spread.SEMS + RowSums.scratch(length) + back_s
+        sum_s + RelaySum.scratch(span, payload) + RelaySum.scratch(span, width) + Spread.SEMS + RowSums.scratch(length) + back_s
         + layer_s[:3] + [pltpu.VMEM((2,) + pack_shape, F32)] + kept_s + [DMA((8,))]
         + Grads.scratch(shard, columns, wide, width) + [pltpu.VMEM(*r) for r in results]
         + GradsAround.scratch(shard) + SmallSum.scratch()

time: 279 us -> 267 us (0.957)
  Pallas kernels: 276 us -> 263 us
    pallas_call x3, Pallas kernels: 267 us -> 255 us  [comm_call(): pl.pallas_call(kernel, out_shape=[jax.ShapeDtypeStruct(s, t) for s, t in...]
where the time goes in v7:
time: 267 us; the launch traced here: 265 us
  Pallas kernels  263 us (99%)
    pallas_call x3, Pallas kernels, comm_call(): pl.pallas_call(kernel, out_shape=[jax.ShapeDtypeStruct(s, t) for s, t in...  255 us
    pallas_call x1, Pallas kernels, finish_call(): pl.pallas_call(finish_kernel, grid=(steps,), out_shape=[jax.ShapeDtypeStr...  8.57 us

profile of v7, /device:TPU:0, one launch (start us, length us, event | category | flops | bytes accessed | tf_op | source)
XLA Modules:
  0.0 265.4 jit_solution(3067628025035726421)
XLA Ops:
  0.6 53.3 %open.1 = (bf16[1072,1536]{1,0:T(8,128)(2,1)}, bf16[384,1536]{1,0:T(8,128)(2,1)}, f32[2,8,4352]{2,1,0:T(8,128)}, bf16[2,256,1536]{2,1,0:T(8,128)(2,1)}, bf16[2,256,1536]{2,1,0:T(8,128)(2,1)}) custom-call(bf16[6448,384]{1,0:T(8,128)(2,1)} %bitcast.18, bf16[768,1536]{1,0:T(8,128)(2,1)} %bitcast.20, bf16[2,64,1536]{2,1,0:T(8,128)(2,1)} %bitcast.22, ...), custom_call_target="tpu_custom_call" | custom-call | tf_op jit(solution)/shard_map/open/pallas_call | solution.py:1762
  53.9 55.5 %middle.1 = (bf16[1072,1536]{1,0:T(8,128)(2,1)}, bf16[384,1536]{1,0:T(8,128)(2,1)}, bf16[2,256,1536]{2,1,0:T(8,128)(2,1)}, f32[64,1536]{1,0:T(8,128)}, f32[64,12...) custom-call(bf16[6448,384]{1,0:T(8,128)(2,1)} %bitcast.19, ...), custom_call_target="tpu_custom_call" | custom-call | tf_op jit(solution)/shard_map/middle/pallas_call | solution.py:1762
  109.5 145.9 %back.1 = (bf16[2,64,1536]{2,1,0:T(8,128)(2,1)}, bf16[2,64,1536]{2,1,0:T(8,128)(2,1)}, bf16[6448,384]{1,0:T(8,128)(2,1)}, bf16[768,1536]{1,0:T(8,128)(2,1)}, f32[8,4352]{1,0:T(8,128)}) custom-call(bf16[2,256,1536]{2,1,0:T(8,128)(2,1)} %get-tuple-element.46.refs_0_, bf16[2,256,1536]{2,1,0:T(8,128)(2,1)} %get-tuple-element.47.refs_1_, ...), custom_call_target="tpu_custom_call" | custom-call | tf_op jit(solution)/shard_map/back/pallas_call | solution.py:1762
  255.3 0.0 copy-start.1
  255.4 0.0 copy-start
  255.4 8.6 %finish.1 = (f32[6448,384]{1,0:T(8,128)}, f32[768,1536]{1,0:T(8,128)}, f32[1,1536]{1,0:T(1,128)}, f32[4,3328]{1,0:T(4,128)}, f32[1,3328]{1,0:T(1,128)}, /*index=...) custom-call(bf16[6448,384]{1,0:T(8,128)(2,1)} %get-tuple-element.61.final, ...), custom_call_target="tpu_custom_call" | custom-call | tf_op jit(solution)/shard_map/finish/pallas_call | solution.py:1889
  263.9 0.0 copy-done.1
  263.9 0.7 copy.26
  264.7 0.0 copy-done
  264.7 0.7 copy.27
Async XLA Ops:
  255.3 8.6 %copy-start.1 = (bf16[2,64,1536]{2,1,0:T(8,128)(2,1)S(1)}, bf16[2,64,1536]{2,1,0:T(8,128)(2,1)}, u32[]{:S(2)}) copy-start(bf16[2,64,1536]{2,1,0:T(8,128)(2,1)} %get-tuple-element.59) | copy-start | bytes 1179652
  255.4 9.3 %copy-start = (bf16[2,64,1536]{2,1,0:T(8,128)(2,1)S(1)}, bf16[2,64,1536]{2,1,0:T(8,128)(2,1)}, u32[]{:S(2)}) copy-start(bf16[2,64,1536]{2,1,0:T(8,128)(2,1)} %get-tuple-element.60) | copy-start | bytes 1179652

commit v8 on v7

--- a/solution.py
+++ b/solution.py
@@ -228,7 +228,10 @@
     h_ref, aux_ref, *refs = refs
     saved, (w_ref, wo_ref), params, outs, sum_refs, scratch = take(refs, (5, 2, 4, 3, 3, 4))
     params = load_params(params)
-    aux = aux_ref[0, :, 0:1], aux_ref[0, :, 1:2]
+
+    def aux():
+        return aux_ref[0, :, 0:1], aux_ref[0, :, 1:2]
+
     sums = backward_rows(heads, params, 0, h_ref, aux, saved, w_ref, wo_ref, outs, scratch)
     for ref, value in zip(sum_refs, sums):
 
@@ -260,22 +263,6 @@
     length, width = dn_ref.shape[1:]
     wide = ch.shape[1]
     blocks = length // SPAN
-    h_rows = h_ref[i, :, :width]
-    scale, rdot = aux
-    gate = gate_ref[i]
-    mixed = mixed_ref[i].astype(F32)
-    sig = sigmoid(gate)
-    silu = gate * sig
-    gated = mixed * silu
-    gain = ch[6:7]
-    grad_no = dot_nt(h_rows, wo_ref[...])
-    grad_g = scale * (gain * grad_no) - gated * (scale * scale * (1.0 / INNER) * rdot)
-    scaled = gated * scale
-    no_ref[i] = (scaled * gain).astype(BF16)
-    gain_row = jnp.sum(grad_no * scaled, axis=0, keepdims=True)
-    dmix_s[...] = (grad_g * silu).astype(BF16)
-    pg_ref[i, :, :wide] = (grad_g * mixed * (sig * (1.0 + gate * (1.0 - sig)))).astype(BF16)
-
     x_raw = xraw_ref[i].astype(F32)
     bc_raw = bcraw_ref[i].astype(F32)
     conv_x = conv_sum(x_raw, ch)
@@ -307,6 +294,23 @@
             if entering[b][h] is not None:
                 fresh += jnp.exp(last) * entering[b][h]
             entering[b + 1][h] = fresh
+
+    scale, rdot = aux()
+    h_rows = h_ref[i, :, :width]
+    gate = gate_ref[i]
+    mixed = mixed_ref[i].astype(F32)
+    sig = sigmoid(gate)
+    silu = gate * sig
+    gated = mixed * silu
+    gain = ch[6:7]
+    grad_no = dot_nt(h_rows, wo_ref[...])
+    grad_g = scale * (gain * grad_no) - gated * (scale * scale * (1.0 / INNER) * rdot)
+    scaled = gated * scale
+    no_ref[i] = (scaled * gain).astype(BF16)
+    gain_row = jnp.sum(grad_no * scaled, axis=0, keepdims=True)
+    dmix_s[...] = (grad_g * silu).astype(BF16)
+    pg_ref[i, :, :wide] = (grad_g * mixed * (sig * (1.0 + gate * (1.0 - sig)))).astype(BF16)
+
     leaving = [None] * heads
     rate_row = jnp.zeros((1, LANES), F32)
     for b in reversed(range(blocks)):
@@ -1033,16 +1037,16 @@
     pack_there.start()
     weights.more(2, few)
     rows.forward()
+    grads.start()
     for at in (3, 4, 5):
         weights.more(at, few)
     weights.relay(0)
     weights.relay(1)
     weights.share()
-    grads.start()
     weights.relay(2)
+    grads.forward()
     weights.relay(3)
     weights.shared()
-    grads.forward()
     weights.relay(4)
     weights.relay(5)
     weights.relay_mate()
@@ -1555,7 +1559,7 @@
         seq = last.half(i)
         forward_rows(heads, params, seq, u, w, wo, h_rows, [last.parts, sums.mine, *saved])
         sums.start(seq)
-        pl.when(i == 0)(lambda: last.start(0))
+        last.start(i)
 
     last.go_on(0)
 
@@ -1566,14 +1570,20 @@
         def _(n):
             i = order(n)
             seq = total.half(i)
-            aux = aux_of(n, seq)
             outs = (total.parts, proj_grad, normed_out)
-            parts = backward_rows(heads, params, seq, h_ref, aux, saved[1:], w, wo, outs, scratch)
+            parts = backward_rows(
+                heads, params, seq, h_ref, lambda: aux_of(n, seq), saved[1:], w, wo, outs, scratch
+            )
             add_small(small.at[layer], *parts)
             total.start(i)
 
     def row_aux(n, seq):
-        pl.when(n == 1)(last.forward)
+
+        @pl.when(n == 1)
+        def _():
+            last.go_on(1)
+            last.forward()
+
         sums.finish(seq)
         return aux_of_rows(sums.mine[seq])
 
@@ -1632,7 +1642,6 @@
         for n in (2, 3):
             grads.to_planes(n)
 
-    last.start(1)
     for copy in reloads:
         copy.wait()
     params = load_params((ids, pack.at[0]))
@@ -1648,7 +1657,6 @@
         product(0, n)
     second.go_on(1)
     second.go_on(0)
-    last.go_on(1)
 
     @first_core
     def _():

time: 267 us -> 264 us (0.989)
  no operation moved by 1% of the time
where the time goes in v8:
time: 264 us; the launch traced here: 263 us
  Pallas kernels  261 us (99%)
    pallas_call x3, Pallas kernels, comm_call(): pl.pallas_call(kernel, out_shape=[jax.ShapeDtypeStruct(s, t) for s, t in...  253 us
    pallas_call x1, Pallas kernels, finish_call(): pl.pallas_call(finish_kernel, grid=(steps,), out_shape=[jax.ShapeDtypeStr...  8.57 us

profile of v8, /device:TPU:0, one launch (start us, length us, event | category | flops | bytes accessed | tf_op | source)
XLA Modules:
  0.0 263.4 jit_solution(17569514331570313293)
XLA Ops:
  0.6 53.3 %open.1 = (bf16[1072,1536]{1,0:T(8,128)(2,1)}, bf16[384,1536]{1,0:T(8,128)(2,1)}, f32[2,8,4352]{2,1,0:T(8,128)}, bf16[2,256,1536]{2,1,0:T(8,128)(2,1)}, bf16[2,256,1536]{2,1,0:T(8,128)(2,1)}) custom-call(bf16[6448,384]{1,0:T(8,128)(2,1)} %bitcast.18, bf16[768,1536]{1,0:T(8,128)(2,1)} %bitcast.20, bf16[2,64,1536]{2,1,0:T(8,128)(2,1)} %bitcast.22, ...), custom_call_target="tpu_custom_call" | custom-call | tf_op jit(solution)/shard_map/open/pallas_call | solution.py:1770
  53.9 54.1 %middle.1 = (bf16[1072,1536]{1,0:T(8,128)(2,1)}, bf16[384,1536]{1,0:T(8,128)(2,1)}, bf16[2,256,1536]{2,1,0:T(8,128)(2,1)}, f32[64,1536]{1,0:T(8,128)}, f32[64,12...) custom-call(bf16[6448,384]{1,0:T(8,128)(2,1)} %bitcast.19, ...), custom_call_target="tpu_custom_call" | custom-call | tf_op jit(solution)/shard_map/middle/pallas_call | solution.py:1770
  108.0 145.4 %back.1 = (bf16[2,64,1536]{2,1,0:T(8,128)(2,1)}, bf16[2,64,1536]{2,1,0:T(8,128)(2,1)}, bf16[6448,384]{1,0:T(8,128)(2,1)}, bf16[768,1536]{1,0:T(8,128)(2,1)}, f32[8,4352]{1,0:T(8,128)}) custom-call(bf16[2,256,1536]{2,1,0:T(8,128)(2,1)} %get-tuple-element.46.refs_0_, bf16[2,256,1536]{2,1,0:T(8,128)(2,1)} %get-tuple-element.47.refs_1_, ...), custom_call_target="tpu_custom_call" | custom-call | tf_op jit(solution)/shard_map/back/pallas_call | solution.py:1770
  253.3 0.0 copy-start.1
  253.4 0.0 copy-start
  253.4 8.6 %finish.1 = (f32[6448,384]{1,0:T(8,128)}, f32[768,1536]{1,0:T(8,128)}, f32[1,1536]{1,0:T(1,128)}, f32[4,3328]{1,0:T(4,128)}, f32[1,3328]{1,0:T(1,128)}, /*index=...) custom-call(bf16[6448,384]{1,0:T(8,128)(2,1)} %get-tuple-element.61.final, ...), custom_call_target="tpu_custom_call" | custom-call | tf_op jit(solution)/shard_map/finish/pallas_call | solution.py:1897
  261.9 0.0 copy-done.1
  261.9 0.7 copy.26
  262.7 0.0 copy-done
  262.7 0.7 copy.27
Async XLA Ops:
  253.3 8.6 %copy-start.1 = (bf16[2,64,1536]{2,1,0:T(8,128)(2,1)S(1)}, bf16[2,64,1536]{2,1,0:T(8,128)(2,1)}, u32[]{:S(2)}) copy-start(bf16[2,64,1536]{2,1,0:T(8,128)(2,1)} %get-tuple-element.59) | copy-start | bytes 1179652
  253.4 9.3 %copy-start = (bf16[2,64,1536]{2,1,0:T(8,128)(2,1)S(1)}, bf16[2,64,1536]{2,1,0:T(8,128)(2,1)}, u32[]{:S(2)}) copy-start(bf16[2,64,1536]{2,1,0:T(8,128)(2,1)} %get-tuple-element.60) | copy-start | bytes 1179652

commit v9 on v8

--- a/solution.py
+++ b/solution.py
@@ -1850,20 +1850,26 @@
         ],
         "back",
     )
-    grad_in, grad_out, gain, conv, bias, shift, rate, skip, gate = finish_call(final, final_out, small)
+    home_rows, home_grads, grad_in, grad_out, gain, conv, bias, shift, rate, skip, gate = finish_call(
+        home_rows, home_grads, final, final_out, small
+    )
     return (
         home_rows[None, :, None], home_grads[None, :, None], gain, grad_in.T[None], conv[None],
         bias, shift, rate, skip, gate, grad_out[None],
     )
 
 
-def finish_kernel(final, final_out, small, grad_in, grad_out, gain, conv, bias, shift, rate, skip, gate):
+def finish_kernel(
+    rows_in, grads_in, final, final_out, small, rows_out, grads_out, grad_in, grad_out, gain, conv, bias, shift, rate, skip, gate
+):
     grad_in[...] = final[...].astype(F32)
     step = pl.program_id(0)
     grad_out[...] = final_out[...].astype(F32)
 
     @pl.when(step == 0)
     def _():
+        rows_out[...] = rows_in[...]
+        grads_out[...] = grads_in[...]
         gain[...] = small[7:8, :GAIN_END]
         shift[...] = small[7:8, DT_AT : DT_AT + HEADS]
         rate[...] = small[7:8, RATE_AT : RATE_AT + HEADS]
@@ -1881,7 +1887,7 @@
         bias[:, INNER:] = small[CONV : CONV + 1, -SHARED:]
 
 
-def finish_call(final, final_out, small):
+def finish_call(home_rows, home_grads, final, final_out, small):
     rows, shard = final.shape
     out_rows, width = final_out.shape
     steps = 3
@@ -1894,23 +1900,31 @@
     def same(i):
         return (0, 0)
 
+    def same3(i):
+        return (0, 0, 0)
+
     return pl.pallas_call(
         finish_kernel,
         grid=(steps,),
-        out_shape=[jax.ShapeDtypeStruct(s, F32) for s in [final.shape, final_out.shape] + smalls],
+        out_shape=[jax.ShapeDtypeStruct(home_rows.shape, BF16)] * 2
+        + [jax.ShapeDtypeStruct(s, F32) for s in [final.shape, final_out.shape] + smalls],
         in_specs=[
+            pl.BlockSpec(home_rows.shape, same3),
+            pl.BlockSpec(home_rows.shape, same3),
             pl.BlockSpec((block, shard), in_block),
             pl.BlockSpec((out_block, width), in_block),
             pl.BlockSpec(small.shape, same),
         ],
         out_specs=[
+            pl.BlockSpec(home_rows.shape, same3),
+            pl.BlockSpec(home_rows.shape, same3),
             pl.BlockSpec((block, shard), in_block),
             pl.BlockSpec((out_block, width), in_block),
         ]
         + [pl.BlockSpec(s, same) for s in smalls],
         compiler_params=pltpu.CompilerParams(**PARAMS),
         name="finish",
-    )(final, final_out, small)
+    )(home_rows, home_grads, final, final_out, small)
 
 
 def shards(

time: 264 us -> 263 us (level)
  no operation moved by 1% of the time
where the time goes in v9:
time: 263 us; the launch traced here: 262 us
  Pallas kernels  262 us (100%)
    pallas_call x3, Pallas kernels, comm_call(): pl.pallas_call(kernel, out_shape=[jax.ShapeDtypeStruct(s, t) for s, t in...  253 us
    pallas_call x1, Pallas kernels, finish_call(): pl.pallas_call(finish_kernel, grid=(steps,), out_shape=[jax.ShapeDtypeStr...  9.01 us

profile of v9, /device:TPU:0, one launch (start us, length us, event | category | flops | bytes accessed | tf_op | source)
XLA Modules:
  0.0 262.5 jit_solution(8790429445746683705)
XLA Ops:
  0.6 53.3 %open.1 = (bf16[1072,1536]{1,0:T(8,128)(2,1)}, bf16[384,1536]{1,0:T(8,128)(2,1)}, f32[2,8,4352]{2,1,0:T(8,128)}, bf16[2,256,1536]{2,1,0:T(8,128)(2,1)}, bf16[2,256,1536]{2,1,0:T(8,128)(2,1)}) custom-call(bf16[6448,384]{1,0:T(8,128)(2,1)} %bitcast.18, bf16[768,1536]{1,0:T(8,128)(2,1)} %bitcast.20, bf16[2,64,1536]{2,1,0:T(8,128)(2,1)} %bitcast.22, ...), custom_call_target="tpu_custom_call" | custom-call | tf_op jit(solution)/shard_map/open/pallas_call | solution.py:1770
  53.9 54.1 %middle.1 = (bf16[1072,1536]{1,0:T(8,128)(2,1)}, bf16[384,1536]{1,0:T(8,128)(2,1)}, bf16[2,256,1536]{2,1,0:T(8,128)(2,1)}, f32[64,1536]{1,0:T(8,128)}, f32[64,12...) custom-call(bf16[6448,384]{1,0:T(8,128)(2,1)} %bitcast.19, ...), custom_call_target="tpu_custom_call" | custom-call | tf_op jit(solution)/shard_map/middle/pallas_call | solution.py:1770
  108.0 145.3 %back.1 = (bf16[2,64,1536]{2,1,0:T(8,128)(2,1)}, bf16[2,64,1536]{2,1,0:T(8,128)(2,1)}, bf16[6448,384]{1,0:T(8,128)(2,1)}, bf16[768,1536]{1,0:T(8,128)(2,1)}, f32[8,4352]{1,0:T(8,128)}) custom-call(bf16[2,256,1536]{2,1,0:T(8,128)(2,1)} %get-tuple-element.48.refs_0_, bf16[2,256,1536]{2,1,0:T(8,128)(2,1)} %get-tuple-element.49.refs_1_, ...), custom_call_target="tpu_custom_call" | custom-call | tf_op jit(solution)/shard_map/back/pallas_call | solution.py:1770
  253.3 9.0 %finish.1 = (bf16[2,64,1536]{2,1,0:T(8,128)(2,1)}, bf16[2,64,1536]{2,1,0:T(8,128)(2,1)}, f32[6448,384]{1,0:T(8,128)}, f32[768,1536]{1,0:T(8,128)}, f32[1,1536]{1...) custom-call(bf16[2,64,1536]{2,1,0:T(8,128)(2,1)} %get-tuple-element., ...), custom_call_target="tpu_custom_call" | custom-call | tf_op jit(solution)/shard_map/finish/pallas_call | solution.py:1906
